TPU v7x, 32 devices: a whole 2x2x4 slice. The times are simulated.
32 devices in a mesh: ctx: 16 (over z, y, x), ch: 2 (over core).
Axes of the slice: x: 2, y: 2, z: 4, core: 2. Of those that a mesh axis runs over, the one named last changes fastest.
Arguments:
- features: bfloat16 [6144, 4096], P('ctx', 'ch'), may hold values from -6 to 6
- proj_weight: bfloat16 [4096, 4096], P('ctx', 'ch'), may hold values from -0.09375 to 0.09375
- gate_q: bfloat16 [6144, 4096], P('ctx', 'ch'), may hold values from -6 to 6
- gate_k: bfloat16 [6144, 4096], P('ctx', 'ch'), may hold values from -6 to 6
- filter_spec: float32 [2, 32, 384, 4096], P(None, 'ctx', None, 'ch'), may hold values from -6 to 6
Outputs:
- gated: bfloat16 [6144, 4096], P('ctx', 'ch')
All inputs are finite; a program needn't handle non-finite values.
Results may differ from a plain program's by a relative error of at most 0.0049.
Values may be sent and summed in bfloat16 or wider, within the bound.
No kernel may reach another device: no remote copies, remote signals or barrier semaphores. Data moves between devices by JAX's collectives and lax.ppermute only.
A program may use at most 128 MiB of HBM per device.

v0:
```python
import math

import jax
import jax.numpy as jnp
from jax import lax
from jax.sharding import PartitionSpec as P

TWO_PI = 2.0 * math.pi
HIGHEST = lax.Precision.HIGHEST


def phase_table(left_index, right_index, modulus):
    angles = (left_index * right_index % modulus).astype(jnp.float32) * (TWO_PI / modulus)
    return (jnp.cos(angles), jnp.sin(angles))


def forward_channels(signal, freq_index, slab_count):
    slab_index = jnp.arange(slab_count, dtype=jnp.int32)
    cosine, sine_part = phase_table(freq_index[:, None], slab_index[None, :], 2 * slab_count)
    real_part = jnp.einsum("ks,cst->ckt", cosine, signal, precision=HIGHEST)
    imag_part = -jnp.einsum("ks,cst->ckt", sine_part, signal, precision=HIGHEST)
    return (real_part, imag_part)


def inverse_channels(real_part, imag_part, freq_index, slab_count):
    slab_index = jnp.arange(slab_count, dtype=jnp.int32)
    cosine, sine_part = phase_table(freq_index[:, None], slab_index[None, :], 2 * slab_count)
    return jnp.einsum("ks,ckt->cst", cosine, real_part, precision=HIGHEST) - jnp.einsum(
        "ks,ckt->cst", sine_part, imag_part, precision=HIGHEST
    )


def rotate_channels(real_part, imag_part, freq_index, time_index, modulus, direction):
    cosine, sine_part = phase_table(freq_index[:, None], time_index[None, :], modulus)
    cosine = cosine[None]
    sine_part = direction * sine_part[None]
    return (real_part * cosine - imag_part * sine_part, imag_part * cosine + real_part * sine_part)


def rows_channels(real_part, imag_part, direction):
    row_count = real_part.shape[2]
    row_index = jnp.arange(row_count, dtype=jnp.int32)
    cosine, sine_part = phase_table(row_index[:, None], row_index[None, :], row_count)
    sine_part = direction * sine_part

    def contract(matrix, operand):
        return jnp.einsum("jt,ckt->ckj", matrix, operand, precision=HIGHEST)

    new_real = contract(cosine, real_part) - contract(sine_part, imag_part)
    new_imag = contract(cosine, imag_part) + contract(sine_part, real_part)
    return (new_real, new_imag)


def filter_product(real_part, imag_part, spectra):
    return (
        spectra[0] * real_part - spectra[1] * imag_part,
        spectra[0] * imag_part + spectra[1] * real_part,
    )


def per_device(features, proj_weight, gate_q, gate_k, filter_spec):
    gathered = lax.all_gather(features, "ch", axis=1, tiled=True)
    tok_rows = gathered.shape[0]
    projected = jnp.dot(
        gathered,
        lax.all_gather(proj_weight, "ctx", axis=0, tiled=True),
        preferred_element_type=jnp.float32,
    )
    signal = (gate_k.astype(jnp.float32) * projected).astype(jnp.bfloat16)
    slab_count = lax.axis_size("ctx")
    freq_count = 2 * slab_count
    fft_length = freq_count * tok_rows
    freq_all = jnp.arange(freq_count, dtype=jnp.int32)
    time_all = jnp.arange(tok_rows, dtype=jnp.int32)
    chan_signal = lax.all_to_all(
        jnp.transpose(signal), "ctx", split_axis=0, concat_axis=1, tiled=True
    )
    spec_local = jnp.transpose(filter_spec, (0, 3, 1, 2))
    spectra = lax.all_to_all(spec_local, "ctx", split_axis=1, concat_axis=2, tiled=True)
    local_count = chan_signal.shape[0]
    local_signal = chan_signal.astype(jnp.float32).reshape(local_count, slab_count, tok_rows)
    real_part, imag_part = forward_channels(local_signal, freq_all, slab_count)
    real_part, imag_part = rotate_channels(
        real_part, imag_part, freq_all, time_all, fft_length, -1.0
    )
    real_part, imag_part = rows_channels(real_part, imag_part, -1.0)
    real_part, imag_part = filter_product(real_part, imag_part, spectra)
    real_part, imag_part = rows_channels(real_part, imag_part, 1.0)
    real_part, imag_part = rotate_channels(
        real_part, imag_part, freq_all, time_all, fft_length, 1.0
    )
    slab_values = inverse_channels(real_part, imag_part, freq_all, slab_count) / fft_length
    slab_values = slab_values.reshape(local_count, slab_count * tok_rows)
    returned = lax.all_to_all(slab_values, "ctx", split_axis=1, concat_axis=0, tiled=True)
    convolved = jnp.transpose(returned)
    return (gate_q.astype(jnp.float32) * convolved).astype(jnp.bfloat16)


def solution(mesh):
    in_specs = (
        P("ctx", "ch"),
        P("ctx", "ch"),
        P("ctx", "ch"),
        P("ctx", "ch"),
        P(None, "ctx", None, "ch"),
    )
    out_specs = P("ctx", "ch")
    return jax.shard_map(
        per_device, mesh=mesh, in_specs=in_specs, out_specs=out_specs, check_vma=False
    )
```

profile of v0, /device:TPU:0, one launch (start us, length us, event | category | flops | bytes accessed | tf_op | source)
XLA Modules:
  0.0 800.2 jit_solution(11276691478766329542)
XLA Ops:
  6.5 0.7 all-gather.3.cloned.1.call-update
  7.3 0.0 all-gather.5.cloned.1.call-start
  7.3 0.7 all-gather.5.cloned.1.call-update
  8.0 19.7 %copy.30 = f32[2,2,384,2048]{2,1,0,3:T(2,128)} copy(f32[2,2,384,2048]{3,2,1,0:T(8,128)} %param.9) | data formatting | bytes 25165824 | tf_op args[4]
  27.7 8.5 %all-to-all-start = ((f32[2,2048,2,384]{3,2,0,1:T(2,128)}), f32[2,2048,2,384]{3,2,0,1:T(2,128)}, u32[]{:S(2)}, u32[]{:S(2)}) async-start(f32[2,2048,2,384]{3,2,0,1:T(2,128)} %bitcast.90), calls=%async_computation | async-start | bytes 25165824 | tf_op jit(solution)/shard_map/all_to_all | solution.py:79
  36.2 430.2 %all-gather.5.cloned.1.call-done = bf16[4096,2048]{1,0:T(8,128)(2,1)} async-done(((bf16[256,2048]{1,0:T(8,128)(2,1)}), bf16[4096,2048]{1,0:T(8,128)(2,1)}) %all-gather.5.cloned.1.call-update) | async-done | bytes 16777232 | tf_op jit(solution)/shard_map/all_gather | solution.py:66
  466.5 11.1 %fusion.37 = bf16[2048,384]{0,1:T(8,128)(2,1)S(1)} fusion(bf16[384,4096]{1,0:T(8,128)(2,1)} %all-gather.3.cloned.1.call-done, bf16[4096,2048]{1,0:T(8,128)(2,1)} %all-gather.5.cloned.1.call-done, bf16[384,2048]{1,0:T(8,128)(2,1)S(1)} %copy-done.2), kind=kOutput, calls=%fused_computation.49 | convolution fusion | flops 6444810240 | bytes 23068672 | tf_op jit(solution)/shard_map/dot_general | solution.py:64
  477.6 1.6 copy.50
  479.2 6.2 all-to-all-start.1
  485.4 0.2 fusion.100
  485.6 0.2 fusion.101
  485.8 11.2 %copy.80 = f32[2,16,128,2,384]{4,2,3,1,0:T(8,128)} copy(f32[2,16,128,2,384]{4,3,0,2,1:T(2,128)} %bitcast.1) | data formatting | bytes 25165824 | tf_op jit(solution)/shard_map/all_to_all | solution.py:79
  497.0 10.6 %fusion.161 = (f32[1,128,16,2,384]{4,1,3,2,0:T(8,128)}, f32[1,128,16,2,384]{4,1,3,2,0:T(8,128)}) fusion(f32[2,128,16,2,384]{4,1,3,2,0:T(8,128)} %bitcast.91), kind=kLoop, calls=%fused_computation.159 | loop fusion | bytes 25165824 | tf_op jit(solution)/shard_map/slice | solution.py:56
  507.6 11.7 %all-to-all-done.1 = bf16[16,128,384]{2,1,0:T(8,128)(2,1)S(1)} async-done(((bf16[16,128,384]{2,1,0:T(8,128)(2,1)}), bf16[16,128,384]{2,1,0:T(8,128)(2,1)S(1)}, u32[]{:S(2)}, u32[]{:S(2)}) %all-to-all-start.1) | async-done | bytes 1572896 | tf_op jit(solution)/shard_map/all_to_all | solution.py:75
  519.3 2.9 fusion.38
  522.3 4.2 fusion.2
  526.5 21.1 %fusion.24 = f32[128,32,384]{2,0,1:T(8,128)} fusion(f32[128,32,384]{2,1,0:T(8,128)S(1)} %get-tuple-element.7), kind=kOutput, calls=%fused_computation.33 | convolution fusion | flops 7249231872 | bytes 12582912 | tf_op jit(solution)/shard_map/jt,ckt->ckj/dot_general | solution.py:47
  547.5 20.8 %fusion.26 = f32[128,32,384]{2,0,1:T(8,128)} fusion(f32[128,32,384]{2,1,0:T(8,128)S(1)} %get-tuple-element.7), kind=kOutput, calls=%fused_computation.35 | convolution fusion | flops 7249084416 | bytes 12582912 | tf_op jit(solution)/shard_map/jt,ckt->ckj/dot_general | solution.py:47
  568.3 20.7 %fusion.22 = f32[128,32,384]{2,0,1:T(8,128)} fusion(f32[128,32,384]{2,1,0:T(8,128)S(1)} %get-tuple-element.8), kind=kOutput, calls=%fused_computation.31 | convolution fusion | flops 7249231872 | bytes 12582912 | tf_op jit(solution)/shard_map/jt,ckt->ckj/dot_general | solution.py:47
  589.0 30.0 %fusion = (f32[128,32,384]{2,0,1:T(8,128)}, f32[128,32,384]{2,0,1:T(8,128)}) fusion(f32[1,128,16,2,384]{4,1,3,2,0:T(8,128)} %get-tuple-element.10, f32[1,128,16,2,384]{4,1,3,2,0:T(8,128)} %get-tuple-element.9, f32[128,32,384]{2,0,1:T(8,128)} %fusion.24, f32[128,32,384]{2,0,1:T(8,128)} %fusion.26, f32[128,32,384]{2,0,1:T(8,128)} %fusion.22, ...), kind=kOutput, calls=%fused_computation.3 | convolution fusion | flops 7261667328 | bytes 50331648 | tf_op jit(solution)/shard_map/jt,ckt->ckj/dot_general | solution.py:47
  619.1 24.5 %fusion.16 = f32[128,32,384]{2,1,0:T(8,128)S(1)} fusion(f32[128,32,384]{2,0,1:T(8,128)} %get-tuple-element.5), kind=kOutput, calls=%fused_computation.25 | convolution fusion | flops 7249084416 | bytes 12582912 | tf_op jit(solution)/shard_map/jt,ckt->ckj/dot_general | solution.py:47
  643.6 18.9 %fusion.18 = f32[128,32,384]{2,1,0:T(8,128)S(1)} fusion(f32[128,32,384]{2,0,1:T(8,128)S(1)} %copy-done), kind=kOutput, calls=%fused_computation.27 | convolution fusion | flops 7249084416 | bytes 12582912 | tf_op jit(solution)/shard_map/jt,ckt->ckj/dot_general | solution.py:47
  662.5 18.6 %fusion.12 = f32[128,32,384]{2,1,0:T(8,128)S(1)} fusion(f32[128,32,384]{2,0,1:T(8,128)S(1)} %bitcast.89), kind=kOutput, calls=%fused_computation.21 | convolution fusion | flops 7249084416 | bytes 12582912 | tf_op jit(solution)/shard_map/jt,ckt->ckj/dot_general | solution.py:47
  681.1 19.9 %fusion.14 = f32[128,32,384]{2,1,0:T(8,128)} fusion(f32[128,32,384]{2,0,1:T(8,128)S(1)} %bitcast.89), kind=kOutput, calls=%fused_computation.23 | convolution fusion | flops 7249084416 | bytes 12582912 | tf_op jit(solution)/shard_map/jt,ckt->ckj/dot_general | solution.py:47
  701.0 7.9 fusion.4
  708.9 7.7 multiply_bitcast_fusion
  716.6 2.6 copy.42
  719.2 7.3 all-to-all-start.2
  726.6 2.6 copy.29
  729.2 58.1 %all-to-all-done.2 = f32[128,16,384]{2,0,1:T(8,128)S(1)} async-done(((f32[128,16,384]{2,0,1:T(8,128)}), f32[128,16,384]{2,0,1:T(8,128)S(1)}, u32[]{:S(2)}, u32[]{:S(2)}) %all-to-all-start.2) | async-done | bytes 3145760 | tf_op jit(solution)/shard_map/all_to_all | solution.py:94
  787.2 3.3 fusion.28
  790.5 2.6 copy.43
  (14 shorter events, 0.0 us)
Async XLA Ops:
  6.5 29.7 %all-gather.3.cloned.1.call-start = ((), (), s32[]{:S(2)}) async-start(), calls=%async_computation.3 | async-start | bytes 4718592 | tf_op jit(solution)/shard_map/all_gather | solution.py:62
  7.3 459.2 %all-gather.5.cloned.1.call-start = ((), (), s32[]{:S(2)}) async-start(), calls=%async_computation.4 | async-start | bytes 17825792 | tf_op jit(solution)/shard_map/all_gather | solution.py:66
  27.7 438.7 %copy-start.2 = (bf16[384,2048]{1,0:T(8,128)(2,1)S(1)}, bf16[384,2048]{1,0:T(8,128)(2,1)}, u32[]{:S(2)}) copy-start(bf16[384,2048]{1,0:T(8,128)(2,1)} %param.8) | copy-start | bytes 4718596
  27.7 451.5 %all-to-all-start = ((f32[2,2048,2,384]{3,2,0,1:T(2,128)}), f32[2,2048,2,384]{3,2,0,1:T(2,128)}, u32[]{:S(2)}, u32[]{:S(2)}) async-start(f32[2,2048,2,384]{3,2,0,1:T(2,128)} %bitcast.90), calls=%async_computation | async-start | bytes 25165824 | tf_op jit(solution)/shard_map/all_to_all | solution.py:79
  479.2 40.2 %all-to-all-start.1 = ((bf16[16,128,384]{2,1,0:T(8,128)(2,1)}), bf16[16,128,384]{2,1,0:T(8,128)(2,1)S(1)}, u32[]{:S(2)}, u32[]{:S(2)}) async-start(bf16[16,128,384]{2,1,0:T(8,128)(2,1)} %bitcast.5), calls=%async_computation.1 | async-start | bytes 3145728 | tf_op jit(solution)/shard_map/all_to_all | solution.py:75
  526.4 41.9 %copy-start.1 = (f32[128,32,384]{2,1,0:T(8,128)}, f32[128,32,384]{2,1,0:T(8,128)S(1)}, u32[]{:S(2)}) copy-start(f32[128,32,384]{2,1,0:T(8,128)S(1)} %get-tuple-element.8) | copy-start | bytes 18874372
  619.1 24.5 %copy-start = (f32[128,32,384]{2,0,1:T(8,128)S(1)}, f32[128,32,384]{2,0,1:T(8,128)}, u32[]{:S(2)}) copy-start(f32[128,32,384]{2,0,1:T(8,128)} %get-tuple-element.5) | copy-start | bytes 18874372
  619.1 43.4 %slice-start = ((s8[6291456]{0:T(1024)(128)(4,1)}), s8[4194304]{0:T(1024)(128)(4,1)S(1)}, s32[]{:S(2)}) async-start(s8[6291456]{0:T(1024)(128)(4,1)} %bitcast.88), calls=%async_computation.5 | async-start | bytes 8388608
  643.5 18.9 %slice-start.1 = ((s8[6291456]{0:T(1024)(128)(4,1)}), s8[2097152]{0:T(1024)(128)(4,1)S(1)}, s32[]{:S(2)}) async-start(s8[6291456]{0:T(1024)(128)(4,1)} %bitcast.88), calls=%async_computation.6 | async-start | bytes 4194304
  719.2 68.0 %all-to-all-start.2 = ((f32[128,16,384]{2,0,1:T(8,128)}), f32[128,16,384]{2,0,1:T(8,128)S(1)}, u32[]{:S(2)}, u32[]{:S(2)}) async-start(f32[128,16,384]{2,0,1:T(8,128)} %copy.42), calls=%async_computation.2 | async-start | bytes 6291456 | tf_op jit(solution)/shard_map/all_to_all | solution.py:94
Sparse Core Ops, SparseCore 0:
  8.9 14.8 all-gather.2
  26.5 439.8 all-gather.4
where the time goes:
time: 812 us; the launch traced here: 800 us
  waiting for transfers between devices  501 us (62%)
  matrix products  208 us (26%)
  local copies, waits for them, and re-layouts  50.8 us (6%)
  starting transfers between devices  22.1 us (3%)
  between operations  13.8 us (2%)
    all_gather x1, waiting for transfers between devices, per_device(): lax.all_gather(proj_weight, 'ctx', axis=0, tiled=True)  430 us
    dot_general x8, matrix products, contract(): return jnp.einsum('jt,ckt->ckj', matrix, operand, precision=HIGHEST)  174 us
    all_to_all x1, waiting for transfers between devices, per_device(): lax.all_to_all(slab_values, 'ctx', split_axis=1, concat_axis=0, tiled=True)  58.1 us
    unnamed x12, local copies, waits for them, and re-layouts  22.3 us
  transfers between devices with their start and end apart: 5, of which 3 were waited for; matrix products, arithmetic and copies ran while one was open for 7% of the time, Pallas kernels for 0%

commit v1 on v0

v1 whole, which is shorter than its diff:
```python
import functools
import math

import jax
import jax.numpy as jnp
import numpy as np
from jax import lax
from jax.experimental import pallas as pl
from jax.experimental.pallas import tpu as pltpu
from jax.sharding import PartitionSpec as P

BF16 = jnp.bfloat16
F32 = jnp.float32
VMEM_LIMIT = 56 * 1024 * 1024
TIME_TILE = 16
FREQ_CHUNK = 4


def plane_size(ctx_size):
    size = 1
    while ctx_size % (2 * size) == 0 and 4 * size * size <= ctx_size:
        size *= 2
    return size


def best_scale(values):
    distinct, counts = np.unique(np.round(np.abs(values), 12), return_counts=True)
    best, best_error = 1.0, None
    for factor in np.linspace(1.0, 2.0, 2000, endpoint=False):
        scaled = distinct * factor
        rounded = scaled.astype(jnp.bfloat16).astype(np.float64)
        error = float((counts * (rounded - scaled) ** 2).sum()) / factor**2
        if best_error is None or error < best_error:
            best, best_error = float(factor), error
    return best


def split_table(table):
    high = table.astype(jnp.bfloat16)
    low = (table - high.astype(np.float64)).astype(jnp.bfloat16)
    return high, low


def transform_tables(slab_count, tok_rows):
    freq_count = 2 * slab_count
    length = freq_count * tok_rows
    freq = np.arange(freq_count)
    slab = np.arange(slab_count)
    fine = np.arange(TIME_TILE)
    group = np.arange(tok_rows // TIME_TILE)
    turns = (freq[:, None, None] * slab[None, None, :] % freq_count) / freq_count + (
        freq[:, None, None] * fine[None, :, None]
    ) / length
    phase = np.exp(-2j * np.pi * turns)
    slab_table = np.zeros((freq_count, 2, TIME_TILE, slab_count, TIME_TILE))
    for u in range(TIME_TILE):
        slab_table[:, 0, u, :, u] = phase[:, u].real
        slab_table[:, 1, u, :, u] = phase[:, u].imag
    slab_table = slab_table.reshape(freq_count * 2 * TIME_TILE, slab_count * TIME_TILE)
    row = np.arange(tok_rows)
    turns = (row[:, None] * row[None, :] % tok_rows) / tok_rows
    cosine, sine = np.cos(2 * np.pi * turns), np.sin(2 * np.pi * turns)
    forward_rows = np.block([[cosine, sine], [-sine, cosine]])
    scale = best_scale(forward_rows)
    forward_rows = forward_rows * scale
    coarse = np.exp(-2j * np.pi * (freq[:, None] * TIME_TILE * group[None, :] % length) / length)
    coarse = np.stack([coarse.real, coarse.imag], axis=-1)
    inverse_scale = 1.0 / (length * scale * scale)
    return {
        "slab": split_table(slab_table),
        "slab_back": split_table(slab_table.T),
        "rows": forward_rows.astype(jnp.bfloat16),
        "rows_back": forward_rows.T.astype(jnp.bfloat16),
        "coarse": coarse.astype(np.float32).reshape(-1),
        "coarse_back": (coarse * inverse_scale).astype(np.float32).reshape(-1),
    }


def convolve_kernel(
    slab_count,
    tok_rows,
    channels,
    coarse_ref,
    coarse_back_ref,
    signal_ref,
    spectrum_ref,
    slab_high_ref,
    slab_low_ref,
    back_high_ref,
    back_low_ref,
    rows_ref,
    rows_back_ref,
    out_ref,
    work_ref,
    rest_ref,
):
    freq_count = 2 * slab_count
    groups = tok_rows // TIME_TILE
    step = pl.program_id(0)
    tile = TIME_TILE

    def scalars(ref, freq, group):
        at = 2 * (freq * groups + group)
        return ref[at], ref[at + 1]

    @pl.when(step == 0)
    def _():
        @pl.loop(0, groups // 2)
        def _(pair):
            parts = []
            for half in range(2):
                start = pl.multiple_of((2 * pair + half) * tile, tile)
                piece = signal_ref[:, pl.ds(start, tile), :]
                parts.append(piece.reshape(slab_count * tile, channels))
            block = jnp.concatenate(parts, axis=1)
            summed = jnp.dot(slab_high_ref[...], block, preferred_element_type=F32)
            summed += jnp.dot(slab_low_ref[...], block, preferred_element_type=F32)
            for freq in range(freq_count):
                base = freq * 2 * tile
                for half in range(2):
                    lanes = slice(half * channels, (half + 1) * channels)
                    real = summed[base : base + tile, lanes]
                    imag = summed[base + tile : base + 2 * tile, lanes]
                    cos, sin = scalars(coarse_ref, freq, 2 * pair + half)
                    start = pl.multiple_of((2 * pair + half) * tile, tile)
                    work_ref[freq, 0, pl.ds(start, tile), :] = (real * cos - imag * sin).astype(BF16)
                    work_ref[freq, 1, pl.ds(start, tile), :] = (real * sin + imag * cos).astype(BF16)

    first = step * FREQ_CHUNK
    wide = jnp.concatenate(
        [work_ref[first + at].reshape(2 * tok_rows, channels) for at in range(FREQ_CHUNK)], axis=1
    )
    forward = jnp.dot(rows_ref[...], wide, preferred_element_type=F32)
    products = []
    for at in range(FREQ_CHUNK):
        lanes = slice(at * channels, (at + 1) * channels)
        real, imag = forward[:tok_rows, lanes], forward[tok_rows:, lanes]
        spec_real = spectrum_ref[at, 0].astype(F32)
        spec_imag = spectrum_ref[at, 1].astype(F32)
        products.append(
            jnp.concatenate(
                [
                    (spec_real * real - spec_imag * imag).astype(BF16),
                    (spec_real * imag + spec_imag * real).astype(BF16),
                ],
                axis=0,
            )
        )
    inverse = jnp.dot(
        rows_back_ref[...], jnp.concatenate(products, axis=1), preferred_element_type=F32
    )
    for at in range(FREQ_CHUNK):
        lanes = slice(at * channels, (at + 1) * channels)
        for group in range(groups):
            rows = slice(group * tile, (group + 1) * tile)
            real = inverse[rows, lanes]
            imag = inverse[tok_rows + group * tile : tok_rows + (group + 1) * tile, lanes]
            cos, sin = scalars(coarse_back_ref, first + at, group)
            for part, value in enumerate((real * cos + imag * sin, imag * cos - real * sin)):
                high = value.astype(BF16)
                work_ref[first + at, part, rows, :] = high
                rest_ref[first + at, part, rows, :] = (value - high.astype(F32)).astype(BF16)

    @pl.when(step == pl.num_programs(0) - 1)
    def _():
        @pl.loop(0, groups // 2)
        def _(pair):
            highs, lows = [], []
            for half in range(2):
                start = pl.multiple_of((2 * pair + half) * tile, tile)
                depth = freq_count * 2 * tile
                highs.append(work_ref[:, :, pl.ds(start, tile), :].reshape(depth, channels))
                lows.append(rest_ref[:, :, pl.ds(start, tile), :].reshape(depth, channels))
            high = jnp.concatenate(highs, axis=1)
            low = jnp.concatenate(lows, axis=1)
            total = jnp.dot(back_high_ref[...], high, preferred_element_type=F32)
            total += jnp.dot(back_low_ref[...], high, preferred_element_type=F32)
            total += jnp.dot(back_high_ref[...], low, preferred_element_type=F32)
            for half in range(2):
                start = pl.multiple_of((2 * pair + half) * tile, tile)
                lanes = slice(half * channels, (half + 1) * channels)
                out_ref[:, pl.ds(start, tile), :] = (
                    total[:, lanes].reshape(slab_count, tile, channels).astype(BF16)
                )


def convolve_fused(signal, spectrum, tables):
    slab_count, tok_rows, channels = signal.shape
    freq_count = 2 * slab_count
    whole = lambda array: pl.BlockSpec(array.shape, lambda i: (0,) * array.ndim)
    scalar = pl.BlockSpec(memory_space=pltpu.SMEM)
    consts = [
        *tables["slab"],
        *tables["slab_back"],
        tables["rows"],
        tables["rows_back"],
    ]
    consts = [jnp.asarray(c) for c in consts]
    flops = 2 * freq_count * channels * (2 * (2 * tok_rows) ** 2 + 5 * 2 * tok_rows * slab_count * TIME_TILE)
    return pl.pallas_call(
        functools.partial(convolve_kernel, slab_count, tok_rows, channels),
        grid=(freq_count // FREQ_CHUNK,),
        in_specs=[
            scalar,
            scalar,
            whole(signal),
            pl.BlockSpec((FREQ_CHUNK, 2, tok_rows, channels), lambda i: (i, 0, 0, 0)),
            *[whole(c) for c in consts],
        ],
        out_specs=whole(signal),
        out_shape=jax.ShapeDtypeStruct(signal.shape, BF16),
        scratch_shapes=[
            pltpu.VMEM((freq_count, 2, tok_rows, channels), BF16),
            pltpu.VMEM((freq_count, 2, tok_rows, channels), BF16),
        ],
        compiler_params=pltpu.CompilerParams(
            dimension_semantics=("arbitrary",), vmem_limit_bytes=VMEM_LIMIT
        ),
        cost_estimate=pl.CostEstimate(
            flops=flops, bytes_accessed=2 * spectrum.size + 4 * signal.size, transcendentals=0
        ),
        name="convolve",
    )(
        jnp.asarray(tables["coarse"]),
        jnp.asarray(tables["coarse_back"]),
        signal,
        spectrum,
        *consts,
    )


def convolve_plain(signal, spectrum):
    slab_count, tok_rows, channels = signal.shape
    freq_count = 2 * slab_count
    length = freq_count * tok_rows

    def phase(left, right, modulus):
        turns = (left[:, None] * right[None, :] % modulus).astype(F32) * (2.0 * math.pi / modulus)
        return jnp.cos(turns), jnp.sin(turns)

    dot = functools.partial(jnp.einsum, precision=lax.Precision.HIGH, preferred_element_type=F32)
    freq = jnp.arange(freq_count, dtype=jnp.int32)
    slab = jnp.arange(slab_count, dtype=jnp.int32)
    row = jnp.arange(tok_rows, dtype=jnp.int32)
    slab_cos, slab_sin = phase(freq, slab, freq_count)
    turn_cos, turn_sin = (part[:, :, None] for part in phase(freq, row, length))
    row_cos, row_sin = phase(row, row, tok_rows)
    values = signal.astype(F32)
    real, imag = dot("ks,stc->ktc", slab_cos, values), -dot("ks,stc->ktc", slab_sin, values)
    real, imag = real * turn_cos + imag * turn_sin, imag * turn_cos - real * turn_sin
    real, imag = (
        dot("jt,ktc->kjc", row_cos, real) + dot("jt,ktc->kjc", row_sin, imag),
        dot("jt,ktc->kjc", row_cos, imag) - dot("jt,ktc->kjc", row_sin, real),
    )
    spec_real, spec_imag = spectrum[:, 0].astype(F32), spectrum[:, 1].astype(F32)
    real, imag = real * spec_real - imag * spec_imag, imag * spec_real + real * spec_imag
    real, imag = (
        dot("jt,ktc->kjc", row_cos, real) - dot("jt,ktc->kjc", row_sin, imag),
        dot("jt,ktc->kjc", row_cos, imag) + dot("jt,ktc->kjc", row_sin, real),
    )
    real, imag = real * turn_cos - imag * turn_sin, imag * turn_cos + real * turn_sin
    values = dot("ks,ktc->stc", slab_cos, real) - dot("ks,ktc->stc", slab_sin, imag)
    return (values / length).astype(BF16)


def per_device(tables, features, proj_weight, gate_q, gate_k, filter_spec):
    ctx_size = lax.axis_size("ctx")
    ch_size = lax.axis_size("ch")
    plane = plane_size(ctx_size)
    lines = ctx_size // plane
    me = lax.axis_index("ctx")
    ch_me = lax.axis_index("ch")
    line_at, plane_at = me // plane, me % plane
    tok_rows, feat_cols = features.shape
    weight_rows, group_channels = proj_weight.shape
    wide = group_channels // plane
    channels = wide // lines
    freq_local = filter_spec.shape[1]

    plane_groups = [[z * plane + p for p in range(plane)] for z in range(lines)]
    line_groups = [[z * plane + p for z in range(lines)] for p in range(plane)]
    plane_perm = lambda d: [(i, i // plane * plane + (i % plane ^ d)) for i in range(ctx_size)]
    up = [(i, i + plane) for i in range(ctx_size - plane)]
    down = [(i + plane, i) for i in range(ctx_size - plane)]

    weight = proj_weight.reshape(weight_rows, plane, wide).transpose(1, 0, 2)
    weight = lax.all_to_all(weight, "ctx", 0, 0, tiled=True, axis_index_groups=plane_groups)
    weight = weight.reshape(plane * weight_rows, wide)
    from_below, from_above = [weight], [weight]
    for _ in range(lines - 1):
        from_below.append(lax.ppermute(from_below[-1], "ctx", up))
        from_above.append(lax.ppermute(from_above[-1], "ctx", down))

    feature_pieces = [features] + [
        lax.ppermute(features, "ctx", plane_perm(d)) for d in range(1, plane)
    ]
    gate_blocks = gate_k.reshape(tok_rows, plane, wide)
    gate_pieces = []
    for d in range(plane):
        block = lax.dynamic_index_in_dim(gate_blocks, plane_at ^ d, 1, keepdims=False)
        gate_pieces.append(block if d == 0 else lax.ppermute(block, "ctx", plane_perm(d)))

    spec = filter_spec.reshape(2, freq_local, tok_rows, plane, lines, channels)
    spec = spec.transpose(4, 3, 1, 0, 2, 5).astype(BF16)
    spec = spec.reshape(ctx_size, freq_local, 2, tok_rows, channels)
    spec = lax.all_to_all(spec, "ctx", 0, 0, tiled=True)
    spec = spec.reshape(ctx_size * freq_local, 2, tok_rows, channels)

    ordered = [weight] + [
        jnp.where(line_at + m < lines, from_above[m], from_below[lines - m]) for m in range(1, lines)
    ]
    stacked = jnp.stack(ordered)
    take = jnp.mod(jnp.arange(lines) - line_at, lines)
    full_weight = stacked[take].reshape(ch_size, feat_cols, wide)

    signals = []
    for d in range(plane):
        total = None
        for e in range(ch_size):
            piece = feature_pieces[d]
            if e:
                piece = lax.ppermute(
                    piece, "ch", [(i, (i + e) % ch_size) for i in range(ch_size)]
                )
            half = lax.dynamic_index_in_dim(
                full_weight, (ch_me - e) % ch_size, 0, keepdims=False
            )
            term = jnp.dot(piece, half, preferred_element_type=F32)
            total = term if total is None else total + term
        signals.append((gate_pieces[d].astype(F32) * total).astype(BF16))
    signal = jnp.stack(signals)
    signal = signal[jnp.arange(plane) ^ plane_at]
    signal = signal.reshape(plane, tok_rows, lines, channels).transpose(2, 0, 1, 3)
    signal = lax.all_to_all(signal, "ctx", 0, 0, tiled=True, axis_index_groups=line_groups)
    signal = signal.reshape(ctx_size, tok_rows, channels)

    if channels % 128 == 0:
        convolved = convolve_fused(signal, spec, tables)
    else:
        convolved = convolve_plain(signal, spec)
    returned = lax.all_to_all(convolved, "ctx", 0, 0, tiled=True)
    returned = returned.reshape(lines, plane, tok_rows, channels).transpose(2, 1, 0, 3)
    returned = returned.reshape(tok_rows, group_channels)
    return (gate_q.astype(F32) * returned.astype(F32)).astype(BF16)


def solution(mesh):
    ctx_size = mesh.shape["ctx"]

    def whole(features, proj_weight, gate_q, gate_k, filter_spec):
        tables = transform_tables(ctx_size, features.shape[0] // ctx_size)
        return jax.shard_map(
            functools.partial(per_device, tables),
            mesh=mesh,
            in_specs=(
                P("ctx", "ch"),
                P("ctx", "ch"),
                P("ctx", "ch"),
                P("ctx", "ch"),
                P(None, "ctx", None, "ch"),
            ),
            out_specs=P("ctx", "ch"),
            check_vma=False,
        )(features, proj_weight, gate_q, gate_k, filter_spec)

    return whole
```

time: 812 us -> 455 us (0.56); the launches traced: 800 us -> 453 us
  waiting for transfers between devices: 501 us -> 112 us
  blocking collectives: 0 us -> 203 us
  matrix products: 208 us -> 21.1 us
  Pallas kernels: 0 us -> 32.9 us
  local copies, waits for them, and re-layouts: 50.8 us -> 35.2 us
  other arithmetic: 3.74 us -> 18 us
  between operations: 13.8 us -> 0.29 us
  starting transfers between devices: 22.1 us -> 31.2 us
    all_gather x2 -> x0, waiting for transfers between devices: 430 us -> none  [the longest x1 430 us: per_device(): lax.all_gather(proj_weight, 'ctx', axis=0, tiled=True)]
    all_to_all x0 -> x3, blocking collectives: none -> 203 us  [the longest x1 143 us: per_device(): spec = lax.all_to_all(spec, 'ctx', 0, 0, tiled=True)]
    dot_general x13 -> x8, matrix products: 208 us -> 21.1 us  [per_device(): term = jnp.dot(piece, half, preferred_element_type=F32)]
    ppermute x0 -> x16, waiting for transfers between devices: none -> 101 us  [the longest x3 48.5 us: per_device(): from_below.append(lax.ppermute(from_below[-1], 'ctx', up))]
    all_to_all x3 -> x1, waiting for transfers between devices: 69.8 us -> 11.3 us  [per_device(): lax.all_to_all(signal, 'ctx', 0, 0, tiled=True, axis_index_groups=line_gr...]
    pallas_call x0 -> x1, Pallas kernels: none -> 32.9 us  [convolve_fused(): pl.pallas_call(functools.partial(convolve_kernel, slab_count, tok_rows, c...]
    ppermute x0 -> x16, starting transfers between devices: none -> 27.4 us  [the longest x3 14.4 us: per_device(): from_below.append(lax.ppermute(from_below[-1], 'ctx', up))]
    convert_element_type x1 -> x4, local copies, waits for them, and re-layouts: 2.58 us -> 22.9 us  [the longest x2 18 us: per_device(): spec = spec.transpose(4, 3, 1, 0, 2, 5).astype(BF16)]
  transfers between devices with their start and end apart: 5 -> 17, of which waited for: 3 -> 7; matrix products, arithmetic and copies ran while one was open for 7% -> 13% of each run, Pallas kernels for 0% -> 0%
where the time goes in v1:
time: 455 us; the launch traced here: 453 us
  blocking collectives  203 us (45%)
  waiting for transfers between devices  112 us (25%)
  local copies, waits for them, and re-layouts  35.2 us (8%)
  Pallas kernels  32.9 us (7%)
  starting transfers between devices  31.2 us (7%)
  matrix products  21.1 us (5%)
  other arithmetic  18 us (4%)
    all_to_all x1, blocking collectives, per_device(): spec = lax.all_to_all(spec, 'ctx', 0, 0, tiled=True)  143 us
    ppermute x3, waiting for transfers between devices, per_device(): from_below.append(lax.ppermute(from_below[-1], 'ctx', up))  48.5 us
    ppermute x3, waiting for transfers between devices, per_device(): lax.ppermute(features, 'ctx', plane_perm(d))  47.5 us
    all_to_all x1, blocking collectives, per_device(): returned = lax.all_to_all(convolved, 'ctx', 0, 0, tiled=True)  40.6 us
    pallas_call x1, Pallas kernels, convolve_fused(): pl.pallas_call(functools.partial(convolve_kernel, slab_count, tok_rows, c...  32.9 us
    dot_general x8, matrix products, per_device(): term = jnp.dot(piece, half, preferred_element_type=F32)  21.1 us
    all_to_all x1, blocking collectives, per_device(): lax.all_to_all(weight, 'ctx', 0, 0, tiled=True, axis_index_groups=plane_g...  19.1 us
    convert_element_type x2, local copies, waits for them, and re-layouts, per_device(): spec = spec.transpose(4, 3, 1, 0, 2, 5).astype(BF16)  18 us
  transfers between devices with their start and end apart: 17, of which 7 were waited for; matrix products, arithmetic and copies ran while one was open for 13% of the time, Pallas kernels for 0%

profile of v1, /device:TPU:0, one launch (start us, length us, event | category | flops | bytes accessed | tf_op | source)
XLA Modules:
  0.0 453.5 jit_solution(16981102517584096302)
XLA Ops:
  1.5 19.1 %all_to_all.20 = bf16[4,256,512]{1,2,0:T(8,128)(2,1)S(1)} all-to-all(bf16[4,256,512]{1,2,0:T(8,128)(2,1)S(1)} %bitcast.159), channel_id=1, replica_groups={{0,2,4,6},{8,10,12,14},{16,18,20,22},{24,26,28,30},{1,3,5,7},{9,11,13,1..., dimensions={0} | all-to-all | bytes 2097152 | tf_op jit(solution)/shard_map/all_to_all | solution.py:287
  21.1 3.5 collective-permute-start.1
  26.0 19.5 %collective-permute-done.1 = bf16[1024,512]{1,0:T(8,128)(2,1)S(1)} collective-permute-done((bf16[1024,512]{1,0:T(8,128)(2,1)S(1)}, bf16[1024,512]{1,0:T(8,128)(2,1)S(1)}, u32[]{:S(2)}, u32[]{:S(2)}) %collective-permute-start.1) | collective-permute-done | bytes 1048608 | tf_op jit(solution)/shard_map/ppermute | solution.py:291
  45.5 5.4 %collective-permute-start.2 = (bf16[1024,512]{1,0:T(8,128)(2,1)S(1)}, bf16[1024,512]{1,0:T(8,128)(2,1)}, u32[]{:S(2)}, u32[]{:S(2)}) collective-permute-start(bf16[1024,512]{1,0:T(8,128)(2,1)S(1)} %collective-permute-done.1), channel_id=1, source_target_pairs={{0,8},{2,10},{4,12},{6,14},{8,16},{10,18},{12,20},{14,22},{16,24},... | collective-permute-start | bytes 3145736 | tf_op jit(solution)/shard_map/ppermute | solution.py:291
  52.1 17.8 %collective-permute-done.2 = bf16[1024,512]{1,0:T(8,128)(2,1)} collective-permute-done((bf16[1024,512]{1,0:T(8,128)(2,1)S(1)}, bf16[1024,512]{1,0:T(8,128)(2,1)}, u32[]{:S(2)}, u32[]{:S(2)}) %collective-permute-start.2) | collective-permute-done | bytes 1048608 | tf_op jit(solution)/shard_map/ppermute | solution.py:291
  69.9 5.5 %collective-permute-start.3 = (bf16[1024,512]{1,0:T(8,128)(2,1)}, bf16[1024,512]{1,0:T(8,128)(2,1)}, u32[]{:S(2)}, u32[]{:S(2)}) collective-permute-start(bf16[1024,512]{1,0:T(8,128)(2,1)} %collective-permute-done.2), channel_id=1, source_target_pairs={{0,8},{2,10},{4,12},{6,14},{8,16},{10,18},{12,20},{14,22},{16,24},... | collective-permute-start | bytes 3145736 | tf_op jit(solution)/shard_map/ppermute | solution.py:291
  78.5 1.9 copy.22
  82.6 11.2 %collective-permute-done.3 = bf16[1024,512]{1,0:T(8,128)(2,1)} collective-permute-done((bf16[1024,512]{1,0:T(8,128)(2,1)}, bf16[1024,512]{1,0:T(8,128)(2,1)}, u32[]{:S(2)}, u32[]{:S(2)}) %collective-permute-start.3) | collective-permute-done | bytes 1048608 | tf_op jit(solution)/shard_map/ppermute | solution.py:291
  93.8 2.0 collective-permute-start.11
  98.6 14.4 %collective-permute-done.8 = bf16[384,2048]{1,0:T(8,128)(2,1)} collective-permute-done((bf16[384,2048]{1,0:T(8,128)(2,1)}, bf16[384,2048]{1,0:T(8,128)(2,1)}, u32[]{:S(2)}, u32[]{:S(2)}) %collective-permute-start.8) | collective-permute-done | bytes 1572896 | tf_op jit(solution)/shard_map/ppermute | solution.py:295
  114.6 33.0 %collective-permute-done.14 = bf16[384,2048]{1,0:T(8,128)(2,1)} collective-permute-done((bf16[384,2048]{1,0:T(8,128)(2,1)}, bf16[384,2048]{1,0:T(8,128)(2,1)}, u32[]{:S(2)}, u32[]{:S(2)}) %collective-permute-start.14) | collective-permute-done | bytes 1572896 | tf_op jit(solution)/shard_map/ppermute | solution.py:295
  148.3 2.4 pad_maximum_fusion
  150.7 5.0 %gather_fusion = bf16[4,1024,512]{2,1,0:T(8,128)(2,1)} fusion(bf16[4,1024,512]{2,1,0:T(8,128)(2,1)} %pad_maximum_fusion, s32[1024]{0:T(1024)S(1)} %pad_clamp_fusion.1), kind=kCustom, calls=%fused_computation | custom fusion | bytes 8388624 | tf_op jit(solution)/shard_map/gather | solution.py:314
  155.7 3.5 fusion.14
  159.2 2.7 fusion.12
  163.4 2.7 fusion.72
  166.7 2.8 fusion.75
  169.5 2.7 fusion.8
  172.2 2.7 fusion.10
  174.9 2.7 fusion.81
  177.7 4.7 %collective-permute-done.10 = bf16[384,512]{0,1:T(8,128)(2,1)S(1)} collective-permute-done((bf16[384,512]{0,1:T(8,128)(2,1)S(1)}, bf16[384,512]{0,1:T(8,128)(2,1)S(1)}, u32[]{:S(2)}, u32[]{:S(2)}) %collective-permute-start.10) | collective-permute-done | bytes 393248 | tf_op jit(solution)/shard_map/ppermute | solution.py:301
  186.4 3.8 all-to-all-start.1
  190.2 8.2 %convert_element_type.64 = bf16[2,2,384,2048]{3,2,1,0:T(8,128)(2,1)} convert(f32[2,2,384,2048]{3,2,1,0:T(8,128)} %param.17) | non-fusion elementwise | flops 3145728 | bytes 18874368 | tf_op jit(solution)/shard_map/convert_element_type | solution.py:304
  198.4 11.0 %convert_element_type.65 = bf16[2,2,384,4,4,128]{5,4,3,2,1,0:T(4,128)(2,1)} reshape(bf16[2,2,384,2048]{3,2,1,0:T(8,128)(2,1)} %convert_element_type.64) | data formatting | bytes 12582912 | tf_op jit(solution)/shard_map/convert_element_type | solution.py:304
  209.4 7.0 %copy.27 = bf16[4,4,2,2,384,128]{5,4,3,2,1,0:T(8,128)(2,1)} copy(bf16[4,4,2,2,384,128]{5,0,1,4,2,3:T(4,128)(2,1)} %bitcast.145) | data formatting | bytes 12582912 | tf_op jit(solution)/shard_map/convert_element_type | solution.py:304
  216.4 11.3 %all-to-all-done.1 = bf16[4,4,384,128]{3,2,1,0:T(8,128)(2,1)S(1)} async-done(((bf16[4,4,384,128]{3,2,1,0:T(8,128)(2,1)}), bf16[4,4,384,128]{3,2,1,0:T(8,128)(2,1)S(1)}, u32[]{:S(2)}, u32[]{:S(2)}) %all-to-all-start.1) | async-done | bytes 1572896 | tf_op jit(solution)/shard_map/all_to_all | solution.py:334
  227.7 143.2 %all_to_all.21 = bf16[16,2,2,384,128]{4,3,2,1,0:T(8,128)(2,1)} all-to-all(bf16[16,2,2,384,128]{4,3,2,1,0:T(8,128)(2,1)} %bitcast.144), channel_id=1, replica_groups=mesh['ctx'=16,'ch'=2] {'ctx'}, dimensions={0} | all-to-all | bytes 12582912 | tf_op jit(solution)/shard_map/all_to_all | solution.py:306
  370.8 32.9 %convolve.1 = bf16[16,384,128]{2,1,0:T(8,128)(2,1)} custom-call(f32[1536]{0:T(1024)} %constant.121.clone.coarse_ref, f32[1536]{0:T(1024)} %constant.122.clone.coarse_back_ref, bf16[16,384,128]{2,1,0:T(8,128)(2,1)} %bitcast.163, bf16[32,2,384,128]{3,2,1,0:T(8,128)(2,1)} %bitcast.146, bf16[1024,256]{1,0:T(8,128)(2,1)} %constant.115.clone.slab_high_ref, ...), custom_call_target="tpu_custom_call" | custom-call | flops 17716740096 | bytes 9437184 | tf_op jit(solution)/shard_map/convolve/pallas_call | solution.py:200
  403.7 40.6 %all_to_all.22 = bf16[16,384,128]{2,1,0:T(8,128)(2,1)S(1)} all-to-all(bf16[16,384,128]{2,1,0:T(8,128)(2,1)} %convolve.1), channel_id=1, replica_groups=mesh['ctx'=16,'ch'=2] {'ctx'}, dimensions={0} | all-to-all | bytes 3145728 | tf_op jit(solution)/shard_map/all_to_all | solution.py:341
  444.6 2.0 copy.28
  446.6 2.8 reshape.108
  449.5 4.0 multiply_convert_fusion
  (45 shorter events, 21.3 us)
Async XLA Ops:
  21.1 24.3 %collective-permute-start.1 = (bf16[1024,512]{1,0:T(8,128)(2,1)S(1)}, bf16[1024,512]{1,0:T(8,128)(2,1)S(1)}, u32[]{:S(2)}, u32[]{:S(2)}) collective-permute-start(bf16[1024,512]{1,0:T(8,128)(2,1)S(1)} %bitcast.160), channel_id=1, source_target_pairs={{0,8},{2,10},{4,12},{6,14},{8,16},{10,18},{12,20},{14,22},{16,24},... | collective-permute-start | bytes 3145736 | tf_op jit(solution)/shard_map/ppermute | solution.py:291
  24.7 26.2 %collective-permute-start = (bf16[1024,512]{1,0:T(8,128)(2,1)S(1)}, bf16[1024,512]{1,0:T(8,128)(2,1)}, u32[]{:S(2)}, u32[]{:S(2)}) collective-permute-start(bf16[1024,512]{1,0:T(8,128)(2,1)S(1)} %bitcast.161), channel_id=1, source_target_pairs={{8,0},{10,2},{12,4},{14,6},{16,8},{18,10},{20,12},{22,14},{24,16},... | collective-permute-start | bytes 3145736 | tf_op jit(solution)/shard_map/ppermute | solution.py:292
  45.5 5.4 %copy-start.2 = (bf16[1024,512]{1,0:T(8,128)(2,1)}, bf16[1024,512]{1,0:T(8,128)(2,1)S(1)}, u32[]{:S(2)}) copy-start(bf16[1024,512]{1,0:T(8,128)(2,1)S(1)} %collective-permute-done.1) | copy-start | bytes 3145732
  45.5 24.4 %collective-permute-start.2 = (bf16[1024,512]{1,0:T(8,128)(2,1)S(1)}, bf16[1024,512]{1,0:T(8,128)(2,1)}, u32[]{:S(2)}, u32[]{:S(2)}) collective-permute-start(bf16[1024,512]{1,0:T(8,128)(2,1)S(1)} %collective-permute-done.1), channel_id=1, source_target_pairs={{0,8},{2,10},{4,12},{6,14},{8,16},{10,18},{12,20},{14,22},{16,24},... | collective-permute-start | bytes 3145736 | tf_op jit(solution)/shard_map/ppermute | solution.py:291
  50.8 29.5 %collective-permute-start.4 = (bf16[1024,512]{1,0:T(8,128)(2,1)}, bf16[1024,512]{1,0:T(8,128)(2,1)}, u32[]{:S(2)}, u32[]{:S(2)}) collective-permute-start(bf16[1024,512]{1,0:T(8,128)(2,1)} %collective-permute-done), channel_id=1, source_target_pairs={{8,0},{10,2},{12,4},{14,6},{16,8},{18,10},{20,12},{22,14},{24,16},... | collective-permute-start | bytes 3145736 | tf_op jit(solution)/shard_map/ppermute | solution.py:292
  69.9 23.9 %collective-permute-start.3 = (bf16[1024,512]{1,0:T(8,128)(2,1)}, bf16[1024,512]{1,0:T(8,128)(2,1)}, u32[]{:S(2)}, u32[]{:S(2)}) collective-permute-start(bf16[1024,512]{1,0:T(8,128)(2,1)} %collective-permute-done.2), channel_id=1, source_target_pairs={{0,8},{2,10},{4,12},{6,14},{8,16},{10,18},{12,20},{14,22},{16,24},... | collective-permute-start | bytes 3145736 | tf_op jit(solution)/shard_map/ppermute | solution.py:291
  75.4 37.6 %collective-permute-start.8 = (bf16[384,2048]{1,0:T(8,128)(2,1)}, bf16[384,2048]{1,0:T(8,128)(2,1)}, u32[]{:S(2)}, u32[]{:S(2)}) collective-permute-start(bf16[384,2048]{1,0:T(8,128)(2,1)} %param.13), channel_id=1, source_target_pairs={{0,2},{2,0},{4,6},{6,4},{8,10},{10,8},{12,14},{14,12},{16,18},{18,... | collective-permute-start | bytes 4718600 | tf_op jit(solution)/shard_map/ppermute | solution.py:295
  77.0 70.7 %collective-permute-start.14 = (bf16[384,2048]{1,0:T(8,128)(2,1)}, bf16[384,2048]{1,0:T(8,128)(2,1)}, u32[]{:S(2)}, u32[]{:S(2)}) collective-permute-start(bf16[384,2048]{1,0:T(8,128)(2,1)} %param.13), channel_id=1, source_target_pairs={{0,6},{2,4},{4,2},{6,0},{8,14},{10,12},{12,10},{14,8},{16,22},{18,... | collective-permute-start | bytes 4718600 | tf_op jit(solution)/shard_map/ppermute | solution.py:295
  78.5 83.4 %collective-permute-start.6 = (bf16[384,2048]{1,0:T(8,128)(2,1)}, bf16[384,2048]{1,0:T(8,128)(2,1)}, u32[]{:S(2)}, u32[]{:S(2)}) collective-permute-start(bf16[384,2048]{1,0:T(8,128)(2,1)} %param.13), channel_id=1, source_target_pairs={{0,1},{1,0},{2,3},{3,2},{4,5},{5,4},{6,7},{7,6},{8,9},{9,8},{10,11... | collective-permute-start | bytes 4718600 | tf_op jit(solution)/shard_map/ppermute | solution.py:322
  80.4 67.3 %collective-permute-start.5 = (bf16[1024,512]{1,0:T(8,128)(2,1)}, bf16[1024,512]{1,0:T(8,128)(2,1)S(1)}, u32[]{:S(2)}, u32[]{:S(2)}) collective-permute-start(bf16[1024,512]{1,0:T(8,128)(2,1)} %collective-permute-done.4), channel_id=1, source_target_pairs={{8,0},{10,2},{12,4},{14,6},{16,8},{18,10},{20,12},{22,14},{24,16},... | collective-permute-start | bytes 3145736 | tf_op jit(solution)/shard_map/ppermute | solution.py:292
  93.8 69.6 %collective-permute-start.11 = (bf16[384,2048]{1,0:T(8,128)(2,1)}, bf16[384,2048]{1,0:T(8,128)(2,1)}, u32[]{:S(2)}, u32[]{:S(2)}) collective-permute-start(bf16[384,2048]{1,0:T(8,128)(2,1)} %param.13), channel_id=1, source_target_pairs={{0,4},{2,6},{4,0},{6,2},{8,12},{10,14},{12,8},{14,10},{16,20},{18,... | collective-permute-start | bytes 4718600 | tf_op jit(solution)/shard_map/ppermute | solution.py:295
  97.1 51.0 %copy-start.3 = (bf16[1024,512]{1,0:T(8,128)(2,1)S(1)}, bf16[1024,512]{1,0:T(8,128)(2,1)}, u32[]{:S(2)}) copy-start(bf16[1024,512]{1,0:T(8,128)(2,1)} %copy-done.2) | copy-start | bytes 3145732
  113.0 53.1 %collective-permute-start.7 = (bf16[384,512]{0,1:T(8,128)(2,1)}, bf16[384,512]{0,1:T(8,128)(2,1)}, u32[]{:S(2)}, u32[]{:S(2)}) collective-permute-start(bf16[384,512]{0,1:T(8,128)(2,1)} %get-tuple-element.5), channel_id=1, source_target_pairs={{0,2},{2,0},{4,6},{6,4},{8,10},{10,8},{12,14},{14,12},{16,18},{18,... | collective-permute-start | bytes 1179656 | tf_op jit(solution)/shard_map/ppermute | solution.py:301
  147.7 19.0 %collective-permute-start.9 = (bf16[384,2048]{1,0:T(8,128)(2,1)}, bf16[384,2048]{1,0:T(8,128)(2,1)}, u32[]{:S(2)}, u32[]{:S(2)}) collective-permute-start(bf16[384,2048]{1,0:T(8,128)(2,1)} %collective-permute-done.8), channel_id=1, source_target_pairs={{0,1},{1,0},{2,3},{3,2},{4,5},{5,4},{6,7},{7,6},{8,9},{9,8},{10,11... | collective-permute-start | bytes 4718600 | tf_op jit(solution)/shard_map/ppermute | solution.py:322
  147.7 27.3 %collective-permute-start.15 = (bf16[384,2048]{1,0:T(8,128)(2,1)}, bf16[384,2048]{1,0:T(8,128)(2,1)}, u32[]{:S(2)}, u32[]{:S(2)}) collective-permute-start(bf16[384,2048]{1,0:T(8,128)(2,1)} %collective-permute-done.14), channel_id=1, source_target_pairs={{0,1},{1,0},{2,3},{3,2},{4,5},{5,4},{6,7},{7,6},{8,9},{9,8},{10,11... | collective-permute-start | bytes 4718600 | tf_op jit(solution)/shard_map/ppermute | solution.py:322
  155.7 3.5 copy-start
  161.9 13.0 %collective-permute-start.13 = (bf16[384,512]{0,1:T(8,128)(2,1)S(1)}, bf16[384,512]{0,1:T(8,128)(2,1)S(1)}, u32[]{:S(2)}, u32[]{:S(2)}) collective-permute-start(bf16[384,512]{0,1:T(8,128)(2,1)S(1)} %get-tuple-element.6), channel_id=1, source_target_pairs={{0,6},{2,4},{4,2},{6,0},{8,14},{10,12},{12,10},{14,8},{16,22},{18,... | collective-permute-start | bytes 1179656 | tf_op jit(solution)/shard_map/ppermute | solution.py:301
  163.4 18.9 %collective-permute-start.12 = (bf16[384,2048]{1,0:T(8,128)(2,1)}, bf16[384,2048]{1,0:T(8,128)(2,1)S(1)}, u32[]{:S(2)}, u32[]{:S(2)}) collective-permute-start(bf16[384,2048]{1,0:T(8,128)(2,1)} %collective-permute-done.11), channel_id=1, source_target_pairs={{0,1},{1,0},{2,3},{3,2},{4,5},{5,4},{6,7},{7,6},{8,9},{9,8},{10,11... | collective-permute-start | bytes 4718600 | tf_op jit(solution)/shard_map/ppermute | solution.py:322
  166.2 16.1 %collective-permute-start.10 = (bf16[384,512]{0,1:T(8,128)(2,1)S(1)}, bf16[384,512]{0,1:T(8,128)(2,1)S(1)}, u32[]{:S(2)}, u32[]{:S(2)}) collective-permute-start(bf16[384,512]{0,1:T(8,128)(2,1)S(1)} %get-tuple-element.7), channel_id=1, source_target_pairs={{0,4},{2,6},{4,0},{6,2},{8,12},{10,14},{12,8},{14,10},{16,20},{18,... | collective-permute-start | bytes 1179656 | tf_op jit(solution)/shard_map/ppermute | solution.py:301
  186.4 41.2 %all-to-all-start.1 = ((bf16[4,4,384,128]{3,2,1,0:T(8,128)(2,1)}), bf16[4,4,384,128]{3,2,1,0:T(8,128)(2,1)S(1)}, u32[]{:S(2)}, u32[]{:S(2)}) async-start(bf16[4,4,384,128]{3,2,1,0:T(8,128)(2,1)} %bitcast.26), calls=%async_computation.1 | async-start | bytes 3145728 | tf_op jit(solution)/shard_map/all_to_all | solution.py:334
  227.6 143.2 %copy-start.1 = (bf16[4,4,384,128]{3,2,1,0:T(8,128)(2,1)}, bf16[4,4,384,128]{3,2,1,0:T(8,128)(2,1)S(1)}, u32[]{:S(2)}) copy-start(bf16[4,4,384,128]{3,2,1,0:T(8,128)(2,1)S(1)} %all-to-all-done.1) | copy-start | bytes 4718596

commit v2 on v1

v2 whole, which is shorter than its diff:
```python
import functools
import math

import jax
import jax.numpy as jnp
import numpy as np
from jax import lax
from jax.experimental import pallas as pl
from jax.experimental.pallas import tpu as pltpu
from jax.sharding import PartitionSpec as P

BF16 = jnp.bfloat16
F32 = jnp.float32
VMEM_LIMIT = 56 * 1024 * 1024
TIME_TILE = 16
FREQ_CHUNK = 4


def plane_size(ctx_size):
    size = 1
    while ctx_size % (2 * size) == 0 and 4 * size * size <= ctx_size:
        size *= 2
    return size


def best_scale(values):
    distinct, counts = np.unique(np.round(np.abs(values), 12), return_counts=True)
    best, best_error = 1.0, None
    for factor in np.linspace(1.0, 2.0, 2000, endpoint=False):
        scaled = distinct * factor
        rounded = scaled.astype(jnp.bfloat16).astype(np.float64)
        error = float((counts * (rounded - scaled) ** 2).sum()) / factor**2
        if best_error is None or error < best_error:
            best, best_error = float(factor), error
    return best


def split_table(table):
    high = table.astype(jnp.bfloat16)
    low = (table - high.astype(np.float64)).astype(jnp.bfloat16)
    return high, low


def transform_tables(slab_count, tok_rows, first, stride):
    freq_count = 2 * slab_count
    length = freq_count * tok_rows
    freq = np.arange(first, freq_count, stride)
    slab = np.arange(slab_count)
    fine = np.arange(TIME_TILE)
    group = np.arange(tok_rows // TIME_TILE)
    turns = (freq[:, None, None] * slab[None, None, :] % freq_count) / freq_count + (
        freq[:, None, None] * fine[None, :, None]
    ) / length
    phase = np.exp(-2j * np.pi * turns)
    slab_table = np.zeros((len(freq), 2, TIME_TILE, slab_count, TIME_TILE))
    for u in range(TIME_TILE):
        slab_table[:, 0, u, :, u] = phase[:, u].real
        slab_table[:, 1, u, :, u] = phase[:, u].imag
    slab_table = slab_table.reshape(len(freq) * 2 * TIME_TILE, slab_count * TIME_TILE)
    row = np.arange(tok_rows)
    turns = (row[:, None] * row[None, :] % tok_rows) / tok_rows
    cosine, sine = np.cos(2 * np.pi * turns), np.sin(2 * np.pi * turns)
    forward_rows = np.block([[cosine, sine], [-sine, cosine]])
    scale = best_scale(forward_rows)
    forward_rows = forward_rows * scale
    coarse = np.exp(-2j * np.pi * (freq[:, None] * TIME_TILE * group[None, :] % length) / length)
    coarse = np.stack([coarse.real, coarse.imag], axis=-1)
    inverse_scale = 1.0 / (length * scale * scale)
    return {
        "slab": split_table(slab_table),
        "slab_back": split_table(slab_table.T),
        "rows": forward_rows.astype(jnp.bfloat16),
        "rows_back": forward_rows.T.astype(jnp.bfloat16),
        "coarse": coarse.astype(np.float32).reshape(-1),
        "coarse_back": (coarse * inverse_scale).astype(np.float32).reshape(-1),
    }


def coarse_turn(ref, groups, freq, group):
    at = 2 * (freq * groups + group)
    return ref[at], ref[at + 1]


def slab_stage(coarse_ref, signal_ref, high_ref, low_ref, work_ref):
    slab_count, tok_rows, channels = signal_ref.shape
    freq_count = work_ref.shape[0]
    groups = tok_rows // TIME_TILE
    tile = TIME_TILE

    @pl.loop(0, groups // 2)
    def _(pair):
        parts = []
        for half in range(2):
            start = pl.multiple_of((2 * pair + half) * tile, tile)
            piece = signal_ref[:, pl.ds(start, tile), :]
            parts.append(piece.reshape(slab_count * tile, channels))
        block = jnp.concatenate(parts, axis=1)
        summed = jnp.dot(high_ref[...], block, preferred_element_type=F32)
        summed += jnp.dot(low_ref[...], block, preferred_element_type=F32)
        for freq in range(freq_count):
            base = freq * 2 * tile
            for half in range(2):
                lanes = slice(half * channels, (half + 1) * channels)
                real = summed[base : base + tile, lanes]
                imag = summed[base + tile : base + 2 * tile, lanes]
                cos, sin = coarse_turn(coarse_ref, groups, freq, 2 * pair + half)
                start = pl.multiple_of((2 * pair + half) * tile, tile)
                work_ref[freq, 0, pl.ds(start, tile), :] = (real * cos - imag * sin).astype(BF16)
                work_ref[freq, 1, pl.ds(start, tile), :] = (real * sin + imag * cos).astype(BF16)


def rows_stage(work_ref, rows_ref, first):
    _, _, tok_rows, channels = work_ref.shape
    wide = [work_ref[first + at].reshape(2 * tok_rows, channels) for at in range(FREQ_CHUNK)]
    return jnp.dot(rows_ref[...], jnp.concatenate(wide, axis=1), preferred_element_type=F32)


def product_and_back(forward, spectrum_ref, rows_back_ref, coarse_back_ref, work_ref, rest_ref, first):
    _, _, tok_rows, channels = work_ref.shape
    groups = tok_rows // TIME_TILE
    products = []
    for at in range(FREQ_CHUNK):
        real, imag = forward(at)
        spec_real = spectrum_ref[at, 0].astype(F32)
        spec_imag = spectrum_ref[at, 1].astype(F32)
        products.append(
            jnp.concatenate(
                [
                    (spec_real * real - spec_imag * imag).astype(BF16),
                    (spec_real * imag + spec_imag * real).astype(BF16),
                ],
                axis=0,
            )
        )
    inverse = jnp.dot(
        rows_back_ref[...], jnp.concatenate(products, axis=1), preferred_element_type=F32
    )
    for at in range(FREQ_CHUNK):
        lanes = slice(at * channels, (at + 1) * channels)
        for group in range(groups):
            rows = slice(group * TIME_TILE, (group + 1) * TIME_TILE)
            real = inverse[rows, lanes]
            imag = inverse[tok_rows + rows.start : tok_rows + rows.stop, lanes]
            cos, sin = coarse_turn(coarse_back_ref, groups, first + at, group)
            for part, value in enumerate((real * cos + imag * sin, imag * cos - real * sin)):
                high = value.astype(BF16)
                work_ref[first + at, part, rows, :] = high
                rest_ref[first + at, part, rows, :] = (value - high.astype(F32)).astype(BF16)


def slab_back_stage(work_ref, rest_ref, high_ref, low_ref, others, out_ref):
    slab_count, tok_rows, channels = out_ref.shape
    freq_count = work_ref.shape[0]
    tile = TIME_TILE
    depth = freq_count * 2 * tile

    @pl.loop(0, tok_rows // tile // 2)
    def _(pair):
        highs, lows = [], []
        for half in range(2):
            start = pl.multiple_of((2 * pair + half) * tile, tile)
            highs.append(work_ref[:, :, pl.ds(start, tile), :].reshape(depth, channels))
            lows.append(rest_ref[:, :, pl.ds(start, tile), :].reshape(depth, channels))
        high = jnp.concatenate(highs, axis=1)
        low = jnp.concatenate(lows, axis=1)
        total = jnp.dot(high_ref[...], high, preferred_element_type=F32)
        total += jnp.dot(low_ref[...], high, preferred_element_type=F32)
        total += jnp.dot(high_ref[...], low, preferred_element_type=F32)
        for half in range(2):
            start = pl.multiple_of((2 * pair + half) * tile, tile)
            lanes = slice(half * channels, (half + 1) * channels)
            value = total[:, lanes].reshape(slab_count, tile, channels)
            for other in others:
                value += other[:, pl.ds(start, tile), :]
            out_ref[:, pl.ds(start, tile), :] = value.astype(out_ref.dtype)


def convolve_kernel(
    coarse_ref,
    coarse_back_ref,
    signal_ref,
    spectrum_ref,
    slab_high_ref,
    slab_low_ref,
    back_high_ref,
    back_low_ref,
    rows_ref,
    rows_back_ref,
    out_ref,
    work_ref,
    rest_ref,
):
    _, tok_rows, channels = signal_ref.shape
    step = pl.program_id(0)

    @pl.when(step == 0)
    def _():
        slab_stage(coarse_ref, signal_ref, slab_high_ref, slab_low_ref, work_ref)

    first = step * FREQ_CHUNK
    transformed = rows_stage(work_ref, rows_ref, first)

    def forward(at):
        lanes = slice(at * channels, (at + 1) * channels)
        return transformed[:tok_rows, lanes], transformed[tok_rows:, lanes]

    product_and_back(forward, spectrum_ref, rows_back_ref, coarse_back_ref, work_ref, rest_ref, first)

    @pl.when(step == pl.num_programs(0) - 1)
    def _():
        slab_back_stage(work_ref, rest_ref, back_high_ref, back_low_ref, [], out_ref)


def forward_kernel(coarse_ref, signal_ref, slab_high_ref, slab_low_ref, rows_ref, out_ref, work_ref):
    _, tok_rows, channels = signal_ref.shape
    step = pl.program_id(0)

    @pl.when(step == 0)
    def _():
        slab_stage(coarse_ref, signal_ref, slab_high_ref, slab_low_ref, work_ref)

    transformed = rows_stage(work_ref, rows_ref, step * FREQ_CHUNK)
    for at in range(FREQ_CHUNK):
        lanes = slice(at * channels, (at + 1) * channels)
        out_ref[at, 0] = transformed[:tok_rows, lanes]
        out_ref[at, 1] = transformed[tok_rows:, lanes]


def inverse_kernel(
    coarse_back_ref,
    forward_ref,
    spectrum_ref,
    back_high_ref,
    back_low_ref,
    rows_back_ref,
    other_ref,
    out_ref,
    work_ref,
    rest_ref,
):
    step = pl.program_id(0)

    def forward(at):
        return forward_ref[at, 0], forward_ref[at, 1]

    product_and_back(
        forward, spectrum_ref, rows_back_ref, coarse_back_ref, work_ref, rest_ref, step * FREQ_CHUNK
    )

    @pl.when(step == pl.num_programs(0) - 1)
    def _():
        slab_back_stage(work_ref, rest_ref, back_high_ref, back_low_ref, [other_ref], out_ref)


def whole_block(array):
    return pl.BlockSpec(array.shape, lambda i: (0,) * array.ndim)


def frequency_call(kernel, name, freq_count, operands, out_shape, out_blocked, scratch, flops):
    arrays, specs = [], []

    def blocked(shape):
        return pl.BlockSpec((FREQ_CHUNK,) + shape[1:], lambda i: (i,) + (0,) * (len(shape) - 1))

    for array, kind in operands:
        array = jnp.asarray(array)
        arrays.append(array)
        if kind == "scalar":
            specs.append(pl.BlockSpec(memory_space=pltpu.SMEM))
        else:
            specs.append(blocked(array.shape) if kind == "blocked" else whole_block(array))
    moved = sum(a.size * a.dtype.itemsize for a in arrays)
    return pl.pallas_call(
        kernel,
        grid=(freq_count // FREQ_CHUNK,),
        in_specs=specs,
        out_specs=blocked(out_shape.shape) if out_blocked else whole_block(out_shape),
        out_shape=out_shape,
        scratch_shapes=scratch,
        compiler_params=pltpu.CompilerParams(
            dimension_semantics=("arbitrary",), vmem_limit_bytes=VMEM_LIMIT
        ),
        cost_estimate=pl.CostEstimate(flops=flops, bytes_accessed=moved, transcendentals=0),
        name=name,
    )(*arrays)


def convolve_fused(signal, spectra, tables):
    slab_count, tok_rows, channels = signal.shape
    freq_count = spectra[0].shape[0]
    rows_flops = 2 * freq_count * channels * (2 * tok_rows) ** 2
    slab_flops = 4 * freq_count * channels * tok_rows * slab_count * TIME_TILE
    work = pltpu.VMEM((freq_count, 2, tok_rows, channels), BF16)
    total = None
    for spectrum, table in zip(spectra[:-1], tables[:-1]):
        part = frequency_call(
            convolve_kernel,
            "convolve",
            freq_count,
            [
                (table["coarse"], "scalar"),
                (table["coarse_back"], "scalar"),
                (signal, "whole"),
                (spectrum, "blocked"),
                *[(t, "whole") for t in table["slab"]],
                *[(t, "whole") for t in table["slab_back"]],
                (table["rows"], "whole"),
                (table["rows_back"], "whole"),
            ],
            jax.ShapeDtypeStruct(signal.shape, F32),
            False,
            [work, work],
            2 * rows_flops + 5 * slab_flops,
        )
        total = part if total is None else total + part
    if total is None:
        total = jnp.zeros(signal.shape, F32)
    table = tables[-1]
    forward = frequency_call(
        forward_kernel,
        "forward",
        freq_count,
        [
            (table["coarse"], "scalar"),
            (signal, "whole"),
            *[(t, "whole") for t in table["slab"]],
            (table["rows"], "whole"),
        ],
        jax.ShapeDtypeStruct((freq_count, 2, tok_rows, channels), F32),
        True,
        [work],
        rows_flops + 2 * slab_flops,
    )
    return frequency_call(
        inverse_kernel,
        "inverse",
        freq_count,
        [
            (table["coarse_back"], "scalar"),
            (forward, "blocked"),
            (spectra[-1], "blocked"),
            *[(t, "whole") for t in table["slab_back"]],
            (table["rows_back"], "whole"),
            (total, "whole"),
        ],
        jax.ShapeDtypeStruct(signal.shape, BF16),
        False,
        [work, work],
        rows_flops + 3 * slab_flops,
    )


def spread_kernel(lines, channels, values_ref, out_ref):
    for line in range(lines):
        out_ref[line, 0, 0] = values_ref[0, 0, :, line * channels : (line + 1) * channels].astype(BF16)


def spread_spectrum(filter_spec, at, plane, lines):
    parts, _, tok_rows, group_channels = filter_spec.shape
    channels = group_channels // (plane * lines)
    if channels % 128:
        spec = filter_spec[:, at].reshape(parts, tok_rows, plane, lines, channels)
        spec = spec.transpose(3, 2, 0, 1, 4).astype(BF16)
    else:
        spec = pl.pallas_call(
            functools.partial(spread_kernel, lines, channels),
            grid=(parts, plane),
            in_specs=[
                pl.BlockSpec((1, 1, tok_rows, lines * channels), lambda i, j: (i, at, 0, j))
            ],
            out_specs=pl.BlockSpec((lines, 1, 1, tok_rows, channels), lambda i, j: (0, j, i, 0, 0)),
            out_shape=jax.ShapeDtypeStruct((lines, plane, parts, tok_rows, channels), BF16),
            compiler_params=pltpu.CompilerParams(
                dimension_semantics=("arbitrary", "arbitrary"), vmem_limit_bytes=VMEM_LIMIT
            ),
            cost_estimate=pl.CostEstimate(
                flops=0, bytes_accessed=6 * parts * tok_rows * group_channels, transcendentals=0
            ),
            name="spread_spectrum",
        )(filter_spec)
    return spec.reshape(plane * lines, parts, tok_rows, channels)


def gate_kernel(lines, channels, values_ref, gate_ref, out_ref):
    for line in range(lines):
        lanes = slice(line * channels, (line + 1) * channels)
        value = gate_ref[:, lanes].astype(F32) * values_ref[line, 0].astype(F32)
        out_ref[:, lanes] = value.astype(BF16)


def gate_output(returned, gate_q, plane, lines):
    _, tok_rows, channels = returned.shape
    returned = returned.reshape(lines, plane, tok_rows, channels)
    if channels % 128:
        returned = returned.transpose(2, 1, 0, 3).reshape(gate_q.shape)
        return (gate_q.astype(F32) * returned.astype(F32)).astype(BF16)
    flat = pl.BlockSpec((tok_rows, lines * channels), lambda i: (0, i))
    return pl.pallas_call(
        functools.partial(gate_kernel, lines, channels),
        grid=(plane,),
        in_specs=[pl.BlockSpec((lines, 1, tok_rows, channels), lambda i: (0, i, 0, 0)), flat],
        out_specs=flat,
        out_shape=jax.ShapeDtypeStruct(gate_q.shape, BF16),
        compiler_params=pltpu.CompilerParams(
            dimension_semantics=("arbitrary",), vmem_limit_bytes=VMEM_LIMIT
        ),
        cost_estimate=pl.CostEstimate(
            flops=gate_q.size, bytes_accessed=6 * gate_q.size, transcendentals=0
        ),
        name="gate_output",
    )(returned, gate_q)


def convolve_plain(signal, spectrum):
    slab_count, tok_rows, channels = signal.shape
    freq_count = 2 * slab_count
    length = freq_count * tok_rows

    def phase(left, right, modulus):
        turns = (left[:, None] * right[None, :] % modulus).astype(F32) * (2.0 * math.pi / modulus)
        return jnp.cos(turns), jnp.sin(turns)

    dot = functools.partial(jnp.einsum, precision=lax.Precision.HIGH, preferred_element_type=F32)
    freq = jnp.arange(freq_count, dtype=jnp.int32)
    slab = jnp.arange(slab_count, dtype=jnp.int32)
    row = jnp.arange(tok_rows, dtype=jnp.int32)
    slab_cos, slab_sin = phase(freq, slab, freq_count)
    turn_cos, turn_sin = (part[:, :, None] for part in phase(freq, row, length))
    row_cos, row_sin = phase(row, row, tok_rows)
    values = signal.astype(F32)
    real, imag = dot("ks,stc->ktc", slab_cos, values), -dot("ks,stc->ktc", slab_sin, values)
    real, imag = real * turn_cos + imag * turn_sin, imag * turn_cos - real * turn_sin
    real, imag = (
        dot("jt,ktc->kjc", row_cos, real) + dot("jt,ktc->kjc", row_sin, imag),
        dot("jt,ktc->kjc", row_cos, imag) - dot("jt,ktc->kjc", row_sin, real),
    )
    spec_real, spec_imag = spectrum[:, 0].astype(F32), spectrum[:, 1].astype(F32)
    real, imag = real * spec_real - imag * spec_imag, imag * spec_real + real * spec_imag
    real, imag = (
        dot("jt,ktc->kjc", row_cos, real) - dot("jt,ktc->kjc", row_sin, imag),
        dot("jt,ktc->kjc", row_cos, imag) + dot("jt,ktc->kjc", row_sin, real),
    )
    real, imag = real * turn_cos - imag * turn_sin, imag * turn_cos + real * turn_sin
    values = dot("ks,ktc->stc", slab_cos, real) - dot("ks,ktc->stc", slab_sin, imag)
    return (values / length).astype(BF16)


def after(values, earlier):
    values, earlier = list(values), list(earlier)
    anywhere = pl.BlockSpec(memory_space=pl.ANY)
    return pl.pallas_call(
        lambda *refs: None,
        in_specs=[anywhere] * (len(values) + len(earlier)),
        out_specs=[anywhere] * len(values),
        out_shape=[jax.ShapeDtypeStruct(v.shape, v.dtype) for v in values],
        input_output_aliases={i: i for i in range(len(values))},
        cost_estimate=pl.CostEstimate(flops=0, bytes_accessed=0, transcendentals=0),
        name="after",
    )(*values, *earlier)


def per_device(tables, features, proj_weight, gate_q, gate_k, filter_spec):
    ctx_size = lax.axis_size("ctx")
    ch_size = lax.axis_size("ch")
    plane = plane_size(ctx_size)
    lines = ctx_size // plane
    me = lax.axis_index("ctx")
    ch_me = lax.axis_index("ch")
    line_at, plane_at = me // plane, me % plane
    tok_rows, feat_cols = features.shape
    weight_rows, group_channels = proj_weight.shape
    wide = group_channels // plane
    channels = wide // lines
    freq_local = filter_spec.shape[1]
    tie = after if channels % 128 == 0 else lambda values, earlier: values

    plane_groups = [[z * plane + p for p in range(plane)] for z in range(lines)]
    line_groups = [[z * plane + p for z in range(lines)] for p in range(plane)]
    onward = [(i, (i + plane) % ctx_size) for i in range(ctx_size)]

    def swap(value, d):
        perm = [(i, i // plane * plane + (i % plane ^ d)) for i in range(ctx_size)]
        return lax.ppermute(value, "ctx", perm)

    def other_core(value, e):
        return lax.ppermute(value, "ch", [(i, (i + e) % ch_size) for i in range(ch_size)])

    weight = proj_weight.reshape(weight_rows, plane, wide).transpose(1, 0, 2)
    weight = lax.all_to_all(weight, "ctx", 0, 0, tiled=True, axis_index_groups=plane_groups)
    along = [weight.reshape(plane * weight_rows, wide)]
    spread = [spread_spectrum(filter_spec, at, plane, lines) for at in range(freq_local)]
    for step in range(1, lines):
        if 0 < step - 1 < freq_local + 1:
            along[-1] = tie(along[-1:], [spread[step - 2]])[0]
        along.append(lax.ppermute(along[-1], "ctx", onward))
    take = jnp.mod(line_at - jnp.arange(lines), lines)
    full_weight = jnp.stack(along)[take].reshape(ch_size, feat_cols, wide)

    plane_features = lax.all_gather(
        features, "ctx", axis=0, tiled=True, axis_index_groups=plane_groups
    )

    gate_blocks = gate_k.reshape(tok_rows, plane, wide)
    gate_pieces = [
        lax.dynamic_index_in_dim(gate_blocks, plane_at ^ d, 1, keepdims=False) for d in range(plane)
    ]
    gate_pieces = tie(gate_pieces, along[-1:])
    gate_pieces = [swap(piece, d) if d else piece for d, piece in enumerate(gate_pieces)]

    first = tie(spread[:1], along[-1:])
    spectra = [lax.all_to_all(first[0], "ctx", 0, 0, tiled=True)]

    plane_features = tie([plane_features], along[-1:])[0]
    projected = None
    for e in range(ch_size):
        piece = other_core(plane_features, e) if e else plane_features
        weights = lax.dynamic_index_in_dim(full_weight, (ch_me - e) % ch_size, 0, keepdims=False)
        term = jnp.dot(piece, weights, preferred_element_type=F32)
        projected = term if projected is None else projected + term
    projected = projected.reshape(plane, tok_rows, wide)
    gate_pieces = tie(gate_pieces, [projected])
    plane_gate = jnp.stack(gate_pieces)[jnp.arange(plane) ^ plane_at]
    signal = (plane_gate.astype(F32) * projected).astype(BF16)
    signal = signal.reshape(plane, tok_rows, lines, channels).transpose(2, 0, 1, 3)
    signal = tie([signal], spectra)[0]
    signal = lax.all_to_all(signal, "ctx", 0, 0, tiled=True, axis_index_groups=line_groups)
    signal = signal.reshape(ctx_size, tok_rows, channels)

    for at in range(1, freq_local):
        later = tie(spread[at : at + 1], [signal])
        spectra.append(lax.all_to_all(later[0], "ctx", 0, 0, tiled=True))

    if channels % 128 == 0:
        convolved = convolve_fused(signal, spectra, tables)
    else:
        spectrum = jnp.stack(spectra, 1).reshape(ctx_size * freq_local, 2, tok_rows, channels)
        convolved = convolve_plain(signal, spectrum)
    returned = lax.all_to_all(convolved, "ctx", 0, 0, tiled=True)
    return gate_output(returned, gate_q, plane, lines)


def solution(mesh):
    ctx_size = mesh.shape["ctx"]

    def whole(features, proj_weight, gate_q, gate_k, filter_spec):
        freq_local = filter_spec.shape[1] // ctx_size
        tables = [
            transform_tables(ctx_size, features.shape[0] // ctx_size, at, freq_local)
            for at in range(freq_local)
        ]
        return jax.shard_map(
            functools.partial(per_device, tables),
            mesh=mesh,
            in_specs=(
                P("ctx", "ch"),
                P("ctx", "ch"),
                P("ctx", "ch"),
                P("ctx", "ch"),
                P(None, "ctx", None, "ch"),
            ),
            out_specs=P("ctx", "ch"),
            check_vma=False,
        )(features, proj_weight, gate_q, gate_k, filter_spec)

    return whole
```

time: 455 us -> 368 us (0.81)
  blocking collectives: 203 us -> 126 us
  Pallas kernels: 32.9 us -> 63.2 us
  starting transfers between devices: 31.2 us -> 17.7 us
  between operations: 0.29 us -> 13.7 us
  waiting for transfers between devices: 112 us -> 98.9 us
  matrix products: 21.1 us -> 11.8 us
  local copies, waits for them, and re-layouts: 35.2 us -> 26.4 us
  other arithmetic: 18 us -> 9.26 us
    all_to_all x1, blocking collectives: 143 us -> 50.6 us  [per_device(): lax.all_to_all(signal, 'ctx', 0, 0, tiled=True, axis_index_groups=line_gr...]
    ppermute x16 -> x7, waiting for transfers between devices: 101 us -> 66.1 us  [the longest x3 51.2 us: per_device(): along.append(lax.ppermute(along[-1], 'ctx', onward))]
    pallas_call x1 -> x14, Pallas kernels: 32.9 us -> 63.2 us  [the longest x3 45.4 us: frequency_call(): pl.pallas_call(kernel, grid=(freq_count // FREQ_CHUNK,), in_specs=specs,...]
    ppermute x16 -> x7, starting transfers between devices: 27.4 us -> 5.15 us  [the longest x3 3.49 us: swap(): return lax.ppermute(value, 'ctx', perm)]
    all_to_all x1 -> x2, waiting for transfers between devices: 11.3 us -> 32 us  [the longest x1 29.7 us: per_device(): spectra.append(lax.all_to_all(later[0], 'ctx', 0, 0, tiled=True))]
    convert_element_type x4 -> x2, local copies, waits for them, and re-layouts: 22.9 us -> 4.09 us  [per_device(): signal = (plane_gate.astype(F32) * projected).astype(BF16)]
    convert_element_type x3 -> x0, other arithmetic: 12.5 us -> none  [the longest x1 8.17 us: per_device(): spec = spec.transpose(4, 3, 1, 0, 2, 5).astype(BF16)]
    all_to_all x1, blocking collectives: 40.6 us -> 51.3 us  [per_device(): returned = lax.all_to_all(convolved, 'ctx', 0, 0, tiled=True)]
  transfers between devices with their start and end apart: 17 -> 10, of which waited for: 7 -> 7; matrix products, arithmetic and copies ran while one was open for 13% -> 12% of each run, Pallas kernels for 0% -> 12%
where the time goes in v2:
time: 368 us; the launch traced here: 367 us
  blocking collectives  126 us (34%)
  waiting for transfers between devices  98.9 us (27%)
  Pallas kernels  63.2 us (17%)
  local copies, waits for them, and re-layouts  26.4 us (7%)
  starting transfers between devices  17.7 us (5%)
  between operations  13.7 us (4%)
  matrix products  11.8 us (3%)
  other arithmetic  9.26 us (3%)
    all_to_all x1, blocking collectives, per_device(): returned = lax.all_to_all(convolved, 'ctx', 0, 0, tiled=True)  51.3 us
    ppermute x3, waiting for transfers between devices, per_device(): along.append(lax.ppermute(along[-1], 'ctx', onward))  51.2 us
    all_to_all x1, blocking collectives, per_device(): lax.all_to_all(signal, 'ctx', 0, 0, tiled=True, axis_index_groups=line_gr...  50.6 us
    pallas_call x3, Pallas kernels, frequency_call(): pl.pallas_call(kernel, grid=(freq_count // FREQ_CHUNK,), in_specs=specs,...  45.4 us
    all_to_all x1, waiting for transfers between devices, per_device(): spectra.append(lax.all_to_all(later[0], 'ctx', 0, 0, tiled=True))  29.7 us
    all_to_all x1, blocking collectives, per_device(): lax.all_to_all(weight, 'ctx', 0, 0, tiled=True, axis_index_groups=plane_g...  24 us
    ppermute x3, waiting for transfers between devices, swap(): return lax.ppermute(value, 'ctx', perm)  14.9 us
    pallas_call x2, Pallas kernels, spread_spectrum(): pl.pallas_call(functools.partial(spread_kernel, lines, channels), grid=(p...  13.8 us
  transfers between devices with their start and end apart: 10, of which 7 were waited for; matrix products, arithmetic and copies ran while one was open for 12% of the time, Pallas kernels for 12%

profile of v2, /device:TPU:0, one launch (start us, length us, event | category | flops | bytes accessed | tf_op | source)
XLA Modules:
  0.0 366.8 jit_solution(12637088857091194996)
XLA Ops:
  8.6 24.0 %all_to_all.25 = bf16[4,256,512]{2,1,0:T(8,128)(2,1)S(1)} all-to-all(bf16[4,256,512]{2,1,0:T(8,128)(2,1)S(1)} %bitcast.59), channel_id=1, replica_groups={{0,2,4,6},{8,10,12,14},{16,18,20,22},{24,26,28,30},{1,3,5,7},{9,11,13,1..., dimensions={0} | all-to-all | bytes 2097152 | tf_op jit(solution)/shard_map/all_to_all | solution.py:489
  32.6 1.7 collective-permute-start
  34.2 6.9 %spread_spectrum.2 = bf16[4,4,2,384,128]{4,3,2,1,0:T(8,128)(2,1)} custom-call(f32[2,2,384,2048]{3,2,1,0:T(8,128)} %values_ref.3), custom_call_target="tpu_custom_call" | custom-call | bytes 9437184 | tf_op jit(solution)/shard_map/spread_spectrum/pallas_call | solution.py:365
  41.2 14.4 %collective-permute-done.refs_0_ = bf16[1024,512]{1,0:T(8,128)(2,1)S(1)} collective-permute-done((bf16[1024,512]{1,0:T(8,128)(2,1)S(1)}, bf16[1024,512]{1,0:T(8,128)(2,1)S(1)}, u32[]{:S(2)}, u32[]{:S(2)}) %collective-permute-start) | collective-permute-done | bytes 1048608 | tf_op jit(solution)/shard_map/ppermute | solution.py:495
  56.5 6.9 %spread_spectrum.3 = bf16[4,4,2,384,128]{4,3,2,1,0:T(8,128)(2,1)} custom-call(f32[2,2,384,2048]{3,2,1,0:T(8,128)} %values_ref.3), custom_call_target="tpu_custom_call" | custom-call | bytes 9437184 | tf_op jit(solution)/shard_map/spread_spectrum/pallas_call | solution.py:365
  63.4 15.4 %collective-permute-done.1.refs_0_ = bf16[1024,512]{1,0:T(8,128)(2,1)S(1)} collective-permute-done((bf16[1024,512]{1,0:T(8,128)(2,1)}, bf16[1024,512]{1,0:T(8,128)(2,1)S(1)}, u32[]{:S(2)}, u32[]{:S(2)}) %collective-permute-start.1) | collective-permute-done | bytes 1048608 | tf_op jit(solution)/shard_map/ppermute | solution.py:495
  79.9 21.4 %collective-permute-done.2.refs_4_.refs_1_ = bf16[1024,512]{1,0:T(8,128)(2,1)S(1)} collective-permute-done((bf16[1024,512]{1,0:T(8,128)(2,1)}, bf16[1024,512]{1,0:T(8,128)(2,1)S(1)}, u32[]{:S(2)}, u32[]{:S(2)}) %collective-permute-start.2) | collective-permute-done | bytes 1048608 | tf_op jit(solution)/shard_map/ppermute | solution.py:495
  102.2 4.6 %all-to-all-start.1 = ((bf16[16,2,384,128]{3,2,1,0:T(8,128)(2,1)}), bf16[16,2,384,128]{3,2,1,0:T(8,128)(2,1)}, u32[]{:S(2)}, u32[]{:S(2)}) async-start(bf16[16,2,384,128]{3,2,1,0:T(8,128)(2,1)} %after.13), calls=%async_computation.1 | async-start | bytes 6291456 | tf_op jit(solution)/shard_map/all_to_all | solution.py:511
  108.2 3.3 constant_dynamic-slice_fusion
  113.8 1.7 collective-permute-start.3
  115.5 1.5 collective-permute-start.4
  117.3 3.3 pad_maximum_fusion
  120.5 5.0 %gather_fusion = bf16[4,1024,512]{2,1,0:T(8,128)(2,1)} fusion(bf16[4,1024,512]{2,1,0:T(8,128)(2,1)} %pad_maximum_fusion, s32[1024]{0:T(1024)S(1)} %pad_clamp_fusion.1), kind=kCustom, calls=%fused_computation | custom fusion | bytes 8388624 | tf_op jit(solution)/shard_map/gather | solution.py:497
  125.5 6.3 %fusion.1 = f32[1536,512]{1,0:T(8,128)S(1)} fusion(bf16[1536,2048]{1,0:T(8,128)(2,1)} %collective-permute-done.6, bf16[2,2048,512]{2,1,0:T(8,128)(2,1)} %bitcast.57, s32[]{:T(128)S(6)} %select_n.83), kind=kOutput, calls=%fused_computation.6 | convolution fusion | flops 3221225472 | bytes 11534340 | tf_op jit(solution)/shard_map/dot_general | solution.py:518
  131.8 5.5 %convolution_add_fusion = f32[1536,512]{1,0:T(8,128)S(1)} fusion(f32[1536,512]{1,0:T(8,128)S(1)} %fusion.1, bf16[1536,2048]{1,0:T(8,128)(2,1)} %after.11, bf16[2,2048,512]{2,1,0:T(8,128)(2,1)S(1)} %bitcast.58, s32[]{:T(128)S(6)} %select_n.81), kind=kOutput, calls=%fused_computation.3 | convolution fusion | flops 3222011904 | bytes 14680068 | tf_op jit(solution)/shard_map/dot_general | solution.py:518
  137.3 2.9 reshape.106
  140.3 14.1 %collective-permute-done.4.refs_2_ = bf16[384,512]{1,0:T(8,128)(2,1)} collective-permute-done((bf16[384,512]{1,0:T(8,128)(2,1)}, bf16[384,512]{1,0:T(8,128)(2,1)}, u32[]{:S(2)}, u32[]{:S(2)}) %collective-permute-start.4) | collective-permute-done | bytes 393248 | tf_op jit(solution)/shard_map/ppermute | solution.py:483
  155.2 1.5 pad_maximum_fusion.1
  156.7 1.8 gather_fusion.1
  158.5 1.7 copy.46
  160.2 2.4 copy.47
  162.6 4.4 %fusion.6.refs_0_ = bf16[4,4,384,128]{3,2,1,0:T(8,128)(2,1)} fusion(f32[4,384,4,128]{3,1,0,2:T(8,128)} %copy.47, f32[4,384,4,128]{3,2,1,0:T(4,128)} %reshape.106), kind=kLoop, calls=%fused_computation.11 | loop fusion | flops 1572864 | bytes 7864320 | tf_op jit(solution)/shard_map/transpose | solution.py:524
  167.0 2.3 all-to-all-done.1.refs_1_.spectrum_ref
  169.4 50.6 %all_to_all.26 = bf16[4,4,384,128]{3,2,1,0:T(8,128)(2,1)} all-to-all(bf16[4,4,384,128]{3,2,1,0:T(8,128)(2,1)} %after.14), channel_id=1, replica_groups={{0,8,16,24},{2,10,18,26},{4,12,20,28},{6,14,22,30},{1,9,17,25},{3,11,19..., dimensions={0} | all-to-all | bytes 3145728 | tf_op jit(solution)/shard_map/all_to_all | solution.py:526
  220.0 8.0 %all-to-all-start.3 = ((bf16[16,2,384,128]{3,2,1,0:T(8,128)(2,1)}), bf16[16,2,384,128]{3,2,1,0:T(8,128)(2,1)S(1)}, u32[]{:S(2)}, u32[]{:S(2)}) async-start(bf16[16,2,384,128]{3,2,1,0:T(8,128)(2,1)} %after.15), calls=%async_computation.3 | async-start | bytes 6291456 | tf_op jit(solution)/shard_map/all_to_all | solution.py:531
  227.9 10.4 %forward.1.forward_ref = f32[16,2,384,128]{3,2,1,0:T(8,128)} custom-call(f32[768]{0:T(1024)} %constant.111.clone.coarse_ref, bf16[16,384,128]{2,1,0:T(8,128)(2,1)} %bitcast.55, bf16[512,256]{1,0:T(8,128)(2,1)} %constant.112.clone.slab_high_ref, bf16[512,256]{1,0:T(8,128)(2,1)} %constant.113.clone.slab_low_ref, bf16[768,768]{1,0:T(8,128)(2,1)} %constant.109.clone.rows_ref), custom_call_target="tpu_custom_call" | custom-call | flops 4026531840 | bytes 3279872 | tf_op jit(solution)/shard_map/forward/pallas_call | solution.py:273
  238.4 20.6 %convolve.1.other_ref = f32[16,384,128]{2,1,0:T(8,128)} custom-call(f32[768]{0:T(1024)} %constant.103.clone.coarse_ref, f32[768]{0:T(1024)} %constant.104.clone.coarse_back_ref, bf16[16,384,128]{2,1,0:T(8,128)(2,1)} %bitcast.56, bf16[16,2,384,128]{3,2,1,0:T(8,128)(2,1)} %all-to-all-done.1.refs_1_.spectrum_ref, ...), custom_call_target="tpu_custom_call" | custom-call | flops 8858370048 | bytes 8132608 | tf_op jit(solution)/shard_map/convolve/pallas_call | solution.py:273
  259.0 29.7 %all-to-all-done.3.spectrum_ref = bf16[16,2,384,128]{3,2,1,0:T(8,128)(2,1)S(1)} async-done(((bf16[16,2,384,128]{3,2,1,0:T(8,128)(2,1)}), bf16[16,2,384,128]{3,2,1,0:T(8,128)(2,1)S(1)}, u32[]{:S(2)}, u32[]{:S(2)}) %all-to-all-start.3) | async-done | bytes 3145760 | tf_op jit(solution)/shard_map/all_to_all | solution.py:531
  288.7 1.7 copy-done.9
  290.4 14.3 %inverse.1 = bf16[16,384,128]{2,1,0:T(8,128)(2,1)} custom-call(f32[768]{0:T(1024)} %constant.114.clone.coarse_back_ref, f32[16,2,384,128]{3,2,1,0:T(8,128)} %forward.1.forward_ref, bf16[16,2,384,128]{3,2,1,0:T(8,128)(2,1)} %copy-done.9, bf16[256,512]{1,0:T(8,128)(2,1)} %constant.115.clone.back_high_ref, bf16[256,512]{1,0:T(8,128)(2,1)} %constant.116.clone.back_low_ref, ...), custom_call_target="tpu_custom_call" | custom-call | flops 4831838208 | bytes 14289920 | tf_op jit(solution)/shard_map/inverse/pallas_call | solution.py:273
  304.7 51.3 %all_to_all.27 = bf16[16,384,128]{2,1,0:T(8,128)(2,1)} all-to-all(bf16[16,384,128]{2,1,0:T(8,128)(2,1)} %inverse.1), channel_id=1, replica_groups=mesh['ctx'=16,'ch'=2] {'ctx'}, dimensions={0} | all-to-all | bytes 3145728 | tf_op jit(solution)/shard_map/all_to_all | solution.py:538
  356.0 4.0 %gate_output.1 = bf16[384,2048]{1,0:T(8,128)(2,1)} custom-call(bf16[4,4,384,128]{3,2,1,0:T(8,128)(2,1)} %bitcast.53, bf16[384,2048]{1,0:T(8,128)(2,1)} %gate_ref.1), custom_call_target="tpu_custom_call" | custom-call | flops 786432 | bytes 4718592 | tf_op jit(solution)/shard_map/gate_output/pallas_call | solution.py:398
  (49 shorter events, 9.5 us)
Async XLA Ops:
  6.5 94.7 %all-gather.2.cloned.1.call-start = ((), (), s32[]{:S(2)}) async-start(), calls=%async_computation.5 | async-start | bytes 7864320 | tf_op jit(solution)/shard_map/all_gather | solution.py:499
  32.6 8.6 %copy-start.8 = (bf16[4,256,512]{2,1,0:T(8,128)(2,1)}, bf16[4,256,512]{2,1,0:T(8,128)(2,1)S(1)}, u32[]{:S(2)}) copy-start(bf16[4,256,512]{2,1,0:T(8,128)(2,1)S(1)} %all_to_all.25) | copy-start | bytes 3145732
  32.6 23.0 %collective-permute-start = (bf16[1024,512]{1,0:T(8,128)(2,1)S(1)}, bf16[1024,512]{1,0:T(8,128)(2,1)S(1)}, u32[]{:S(2)}, u32[]{:S(2)}) collective-permute-start(bf16[1024,512]{1,0:T(8,128)(2,1)S(1)} %bitcast.62), channel_id=1, source_target_pairs={{0,8},{2,10},{4,12},{6,14},{8,16},{10,18},{12,20},{14,22},{16,24},... | collective-permute-start | bytes 3145736 | tf_op jit(solution)/shard_map/ppermute | solution.py:495
  55.6 1.0 copy-start.4
  56.5 22.3 %collective-permute-start.1 = (bf16[1024,512]{1,0:T(8,128)(2,1)}, bf16[1024,512]{1,0:T(8,128)(2,1)S(1)}, u32[]{:S(2)}, u32[]{:S(2)}) collective-permute-start(bf16[1024,512]{1,0:T(8,128)(2,1)} %after.8), channel_id=1, source_target_pairs={{0,8},{2,10},{4,12},{6,14},{8,16},{10,18},{12,20},{14,22},{16,24},... | collective-permute-start | bytes 3145736 | tf_op jit(solution)/shard_map/ppermute | solution.py:495
  78.9 1.0 copy-start.6
  79.9 21.4 %collective-permute-start.2 = (bf16[1024,512]{1,0:T(8,128)(2,1)}, bf16[1024,512]{1,0:T(8,128)(2,1)S(1)}, u32[]{:S(2)}, u32[]{:S(2)}) collective-permute-start(bf16[1024,512]{1,0:T(8,128)(2,1)} %after.9), channel_id=1, source_target_pairs={{0,8},{2,10},{4,12},{6,14},{8,16},{10,18},{12,20},{14,22},{16,24},... | collective-permute-start | bytes 3145736 | tf_op jit(solution)/shard_map/ppermute | solution.py:495
  101.3 1.0 copy-start
  102.2 23.3 %collective-permute-start.6 = (bf16[1536,2048]{1,0:T(8,128)(2,1)}, bf16[1536,2048]{1,0:T(8,128)(2,1)}, u32[]{:S(2)}, u32[]{:S(2)}) collective-permute-start(bf16[1536,2048]{1,0:T(8,128)(2,1)} %after.11), channel_id=1, source_target_pairs={{0,1},{1,0},{2,3},{3,2},{4,5},{5,4},{6,7},{7,6},{8,9},{9,8},{10,11... | collective-permute-start | bytes 18874376 | tf_op jit(solution)/shard_map/ppermute | solution.py:486
  102.2 4.7 %copy-start.11 = (bf16[384,2048]{1,0:T(8,128)(2,1)S(1)}, bf16[384,2048]{1,0:T(8,128)(2,1)}, u32[]{:S(2)}) copy-start(bf16[384,2048]{1,0:T(8,128)(2,1)} %param.24) | copy-start | bytes 4718596
  102.2 67.2 %all-to-all-start.1 = ((bf16[16,2,384,128]{3,2,1,0:T(8,128)(2,1)}), bf16[16,2,384,128]{3,2,1,0:T(8,128)(2,1)}, u32[]{:S(2)}, u32[]{:S(2)}) async-start(bf16[16,2,384,128]{3,2,1,0:T(8,128)(2,1)} %after.13), calls=%async_computation.1 | async-start | bytes 6291456 | tf_op jit(solution)/shard_map/all_to_all | solution.py:511
  111.5 5.8 %copy-start.1 = (bf16[1024,512]{1,0:T(8,128)(2,1)S(1)}, bf16[1024,512]{1,0:T(8,128)(2,1)}, u32[]{:S(2)}) copy-start(bf16[1024,512]{1,0:T(8,128)(2,1)} %copy-done) | copy-start | bytes 3145732
  111.5 5.7 %copy-start.5 = (bf16[1024,512]{1,0:T(8,128)(2,1)S(1)}, bf16[1024,512]{1,0:T(8,128)(2,1)}, u32[]{:S(2)}) copy-start(bf16[1024,512]{1,0:T(8,128)(2,1)} %after.8) | copy-start | bytes 3145732
  111.5 5.7 %copy-start.7 = (bf16[1024,512]{1,0:T(8,128)(2,1)S(1)}, bf16[1024,512]{1,0:T(8,128)(2,1)}, u32[]{:S(2)}) copy-start(bf16[1024,512]{1,0:T(8,128)(2,1)} %after.9) | copy-start | bytes 3145732
  113.8 26.5 %collective-permute-start.3 = (bf16[384,512]{1,0:T(8,128)(2,1)}, bf16[384,512]{1,0:T(8,128)(2,1)S(1)}, u32[]{:S(2)}, u32[]{:S(2)}) collective-permute-start(bf16[384,512]{1,0:T(8,128)(2,1)} %get-tuple-element.14), channel_id=1, source_target_pairs={{0,2},{2,0},{4,6},{6,4},{8,10},{10,8},{12,14},{14,12},{16,18},{18,... | collective-permute-start | bytes 1179656 | tf_op jit(solution)/shard_map/ppermute | solution.py:483
  115.5 38.9 %collective-permute-start.4 = (bf16[384,512]{1,0:T(8,128)(2,1)}, bf16[384,512]{1,0:T(8,128)(2,1)}, u32[]{:S(2)}, u32[]{:S(2)}) collective-permute-start(bf16[384,512]{1,0:T(8,128)(2,1)} %get-tuple-element.15), channel_id=1, source_target_pairs={{0,4},{2,6},{4,0},{6,2},{8,12},{10,14},{12,8},{14,10},{16,20},{18,... | collective-permute-start | bytes 1179656 | tf_op jit(solution)/shard_map/ppermute | solution.py:483
  116.9 38.2 %collective-permute-start.5 = (bf16[384,512]{1,0:T(8,128)(2,1)}, bf16[384,512]{1,0:T(8,128)(2,1)}, u32[]{:S(2)}, u32[]{:S(2)}) collective-permute-start(bf16[384,512]{1,0:T(8,128)(2,1)} %get-tuple-element.16), channel_id=1, source_target_pairs={{0,6},{2,4},{4,2},{6,0},{8,14},{10,12},{12,10},{14,8},{16,22},{18,... | collective-permute-start | bytes 1179656 | tf_op jit(solution)/shard_map/ppermute | solution.py:483
  125.5 6.3 %copy-start.3 = (bf16[4,1024,512]{2,1,0:T(8,128)(2,1)S(1)}, bf16[4,1024,512]{2,1,0:T(8,128)(2,1)}, u32[]{:S(2)}) copy-start(bf16[4,1024,512]{2,1,0:T(8,128)(2,1)} %gather_fusion) | copy-start | bytes 12582916
  137.3 3.0 copy-start.2
  140.3 14.9 %copy-start.10 = (bf16[384,512]{1,0:T(8,128)(2,1)}, bf16[384,512]{1,0:T(8,128)(2,1)S(1)}, u32[]{:S(2)}) copy-start(bf16[384,512]{1,0:T(8,128)(2,1)S(1)} %collective-permute-done.3.refs_1_) | copy-start | bytes 1179652
  220.0 68.7 %all-to-all-start.3 = ((bf16[16,2,384,128]{3,2,1,0:T(8,128)(2,1)}), bf16[16,2,384,128]{3,2,1,0:T(8,128)(2,1)S(1)}, u32[]{:S(2)}, u32[]{:S(2)}) async-start(bf16[16,2,384,128]{3,2,1,0:T(8,128)(2,1)} %after.15), calls=%async_computation.3 | async-start | bytes 6291456 | tf_op jit(solution)/shard_map/all_to_all | solution.py:531
  288.7 1.7 copy-start.9
Sparse Core Ops, SparseCore 0:
  9.2 76.7 all-gather.1

commit v3 on v2

--- a/solution.py
+++ b/solution.py
@@ -445,8 +445,77 @@
     return (values / length).astype(BF16)
 
 
+def project_kernel(lines, plane, place_ref, *refs):
+    along_refs, refs = refs[:lines], refs[lines:]
+    feature_refs, refs = refs[: 4 * plane], refs[4 * plane :]
+    gate_refs, (out_ref, weight_ref) = refs[:plane], refs[plane:]
+    line_at, plane_at, core = place_ref[0], place_ref[1], place_ref[2]
+    for k in range(lines):
+        line = lax.rem(line_at + lines - k, lines)
+        weight_ref[pl.ds(line * plane, plane)] = along_refs[k][...]
+    _, weight_rows, wide = weight_ref.shape
+    depth = feature_refs[0].shape[1]
+    channels = out_ref.shape[3]
+    blocks = depth // weight_rows
+    for d in range(plane):
+        total = None
+        for e in range(2):
+            for half in range(2):
+                first = (2 * lax.rem(core + e, 2) + half) * blocks
+                weights = weight_ref[pl.ds(first, blocks)].reshape(depth, wide)
+                features = feature_refs[(e * plane + d) * 2 + half][...]
+                term = jnp.dot(features, weights, preferred_element_type=F32)
+                total = term if total is None else total + term
+        value = (gate_refs[d][...].astype(F32) * total).astype(BF16)
+        for line in range(lines):
+            out_ref[line, plane_at ^ d] = value[:, line * channels : (line + 1) * channels]
+
+
+def project_fused(place, along, pieces, gates):
+    lines, plane = len(along), len(gates)
+    _, weight_rows, wide = along[0].shape
+    tok_rows = gates[0].shape[0]
+    flat = [half for core in pieces for d in core for half in d]
+    operands = [*along, *flat, *gates]
+    local = pl.BlockSpec(memory_space=pltpu.VMEM)
+    return pl.pallas_call(
+        functools.partial(project_kernel, lines, plane),
+        in_specs=[pl.BlockSpec(memory_space=pltpu.SMEM)] + [local] * len(operands),
+        out_specs=local,
+        out_shape=jax.ShapeDtypeStruct((lines, plane, tok_rows, wide // lines), BF16),
+        scratch_shapes=[pltpu.VMEM((lines * plane, weight_rows, wide), BF16)],
+        compiler_params=pltpu.CompilerParams(vmem_limit_bytes=VMEM_LIMIT),
+        cost_estimate=pl.CostEstimate(
+            flops=2 * wide * sum(f.size for f in flat),
+            bytes_accessed=2 * sum(o.size for o in operands),
+            transcendentals=0,
+        ),
+        name="project",
+    )(place, *operands)
+
+
+def project_plain(place, along, pieces, gates):
+    line_at, plane_at, core = place[0], place[1], place[2]
+    lines = len(along)
+    pieces = [jnp.stack([jnp.stack(d) for d in by_core]) for by_core in pieces]
+    gates = jnp.stack(gates)
+    plane, _, tok_rows, depth = pieces[0].shape
+    wide = along[0].shape[2]
+    take_line = jnp.mod(line_at - jnp.arange(lines), lines)
+    take_plane = jnp.arange(plane) ^ plane_at
+    weight = jnp.stack(along)[take_line].reshape(len(pieces), 2, depth, wide)
+    total = jnp.zeros((plane, tok_rows, wide), F32)
+    for e, piece in enumerate(pieces):
+        at = jnp.mod(core - e, len(pieces))
+        total += jnp.einsum("phtk,hkc->ptc", piece, weight[at], preferred_element_type=F32)
+    value = (gates.astype(F32) * total).astype(BF16)[take_plane]
+    return value.reshape(plane, tok_rows, lines, wide // lines).transpose(2, 0, 1, 3)
+
+
 def after(values, earlier):
     values, earlier = list(values), list(earlier)
+    if not earlier:
+        return values
     anywhere = pl.BlockSpec(memory_space=pl.ANY)
     return pl.pallas_call(
         lambda *refs: None,
@@ -487,41 +556,61 @@
 
     weight = proj_weight.reshape(weight_rows, plane, wide).transpose(1, 0, 2)
     weight = lax.all_to_all(weight, "ctx", 0, 0, tiled=True, axis_index_groups=plane_groups)
-    along = [weight.reshape(plane * weight_rows, wide)]
-    spread = [spread_spectrum(filter_spec, at, plane, lines) for at in range(freq_local)]
-    for step in range(1, lines):
-        if 0 < step - 1 < freq_local + 1:
-            along[-1] = tie(along[-1:], [spread[step - 2]])[0]
-        along.append(lax.ppermute(along[-1], "ctx", onward))
-    take = jnp.mod(line_at - jnp.arange(lines), lines)
-    full_weight = jnp.stack(along)[take].reshape(ch_size, feat_cols, wide)
-
-    plane_features = lax.all_gather(
-        features, "ctx", axis=0, tiled=True, axis_index_groups=plane_groups
-    )
+    along = [weight]
+
+    halves = jnp.split(features, 2, axis=1)
+    held = [{0: half} for half in halves]
+    arrival = [[0], [0]]
+    bits = [1 << b for b in range(plane.bit_length() - 1)]
+    rounds = [
+        (turn, k) for turn in range(len(bits)) for k in reversed(range(1 << turn))
+    ]
+
+    def feature_round(turn, k, beside):
+        ds = [bits[(turn + at) % len(bits)] for at in range(2)]
+        sources = [arrival[at][k] for at in range(2)]
+        values = [held[at][sources[at]] for at in range(2)]
+        if sources[0]:
+            values = tie(values, beside)
+        new = []
+        for at in range(2):
+            held[at][sources[at]] = values[at]
+            place = sources[at] ^ ds[at]
+            held[at][place] = swap(values[at], ds[at])
+            new.append(held[at][place])
+        if k == 0:
+            arrival[:] = [sorted(held[at], key=list(held[at]).index) for at in range(2)]
+        return new
 
     gate_blocks = gate_k.reshape(tok_rows, plane, wide)
-    gate_pieces = [
+    gates = [
         lax.dynamic_index_in_dim(gate_blocks, plane_at ^ d, 1, keepdims=False) for d in range(plane)
     ]
-    gate_pieces = tie(gate_pieces, along[-1:])
-    gate_pieces = [swap(piece, d) if d else piece for d, piece in enumerate(gate_pieces)]
-
-    first = tie(spread[:1], along[-1:])
+    spread = [spread_spectrum(filter_spec, at, plane, lines) for at in range(freq_local)]
+    beside = []
+    for step in range(max(lines - 1, len(rounds))):
+        if step < lines - 1:
+            along[-1] = tie(along[-1:], beside)[0]
+            along.append(lax.ppermute(along[-1], "ctx", onward))
+        if step < len(rounds):
+            beside = feature_round(*rounds[step], beside + along[step : step + 1])
+        beside = beside + spread[step : step + 1] + (gates if step == 1 else [])
+    gates = tie(gates, along[-1:])
+    gates = [swap(gate, d) if d else gate for d, gate in enumerate(gates)]
+
+    first = tie(spread[:1], along[-1:] + beside)
     spectra = [lax.all_to_all(first[0], "ctx", 0, 0, tiled=True)]
 
-    plane_features = tie([plane_features], along[-1:])[0]
-    projected = None
-    for e in range(ch_size):
-        piece = other_core(plane_features, e) if e else plane_features
-        weights = lax.dynamic_index_in_dim(full_weight, (ch_me - e) % ch_size, 0, keepdims=False)
-        term = jnp.dot(piece, weights, preferred_element_type=F32)
-        projected = term if projected is None else projected + term
-    projected = projected.reshape(plane, tok_rows, wide)
-    gate_pieces = tie(gate_pieces, [projected])
-    plane_gate = jnp.stack(gate_pieces)[jnp.arange(plane) ^ plane_at]
-    signal = (plane_gate.astype(F32) * projected).astype(BF16)
-    signal = signal.reshape(plane, tok_rows, lines, channels).transpose(2, 0, 1, 3)
+    place = jnp.stack([line_at, plane_at, ch_me]).astype(jnp.int32)
+    own = [[held[at][d] for at in range(2)] for d in range(plane)]
+    pieces = [own] + [
+        [[other_core(half, e) for half in d] for d in own] for e in range(1, ch_size)
+    ]
+    fits = channels % 128 == 0 and ch_size == 2 and feat_cols // 2 % weight_rows == 0
+    if fits and weight_rows % 16 == 0 and tok_rows % 16 == 0:
+        signal = project_fused(place, along, pieces, gates)
+    else:
+        signal = project_plain(place, along, pieces, gates)
     signal = tie([signal], spectra)[0]
     signal = lax.all_to_all(signal, "ctx", 0, 0, tiled=True, axis_index_groups=line_groups)
     signal = signal.reshape(ctx_size, tok_rows, channels)

time: 368 us -> 346 us (0.940)
  Pallas kernels: 63.2 us -> 77.5 us
  between operations: 13.7 us -> 0.18 us
  matrix products: 11.8 us -> 0 us
  waiting for transfers between devices: 98.9 us -> 108 us
  blocking collectives: 126 us -> 117 us
  other arithmetic: 9.26 us -> 0.64 us
  local copies, waits for them, and re-layouts: 26.4 us -> 18.5 us
  starting transfers between devices: 17.7 us -> 22.6 us
    ppermute x3 -> x9, waiting for transfers between devices: 14.9 us -> 61.4 us  [swap(): return lax.ppermute(value, 'ctx', perm)]
    ppermute x3, waiting for transfers between devices: 51.2 us -> 12.6 us  [per_device(): along.append(lax.ppermute(along[-1], 'ctx', onward))]
    pallas_call x0 -> x1, Pallas kernels: none -> 14.3 us  [project_fused(): pl.pallas_call(functools.partial(project_kernel, lines, plane), in_specs=...]
    dot_general x2 -> x0, matrix products: 11.8 us -> none  [per_device(): term = jnp.dot(piece, weights, preferred_element_type=F32)]
    ppermute x3 -> x9, starting transfers between devices: 3.49 us -> 10.3 us  [swap(): return lax.ppermute(value, 'ctx', perm)]
    gather x2 -> x0, local copies, waits for them, and re-layouts: 6.74 us -> none  [the longest x1 4.95 us: per_device(): full_weight = jnp.stack(along)[take].reshape(ch_size, feat_cols, wide)]
    unnamed x24 -> x35, local copies, waits for them, and re-layouts: 4.63 us -> 11.1 us
    all_to_all x1, blocking collectives: 24 us -> 19.2 us  [per_device(): lax.all_to_all(weight, 'ctx', 0, 0, tiled=True, axis_index_groups=plane_g...]
  transfers between devices with their start and end apart: 10 -> 22, of which waited for: 7 -> 16; matrix products, arithmetic and copies ran while one was open for 12% -> 3% of each run, Pallas kernels for 12% -> 17%
where the time goes in v3:
time: 346 us; the launch traced here: 345 us
  blocking collectives  117 us (34%)
  waiting for transfers between devices  108 us (31%)
  Pallas kernels  77.5 us (22%)
  starting transfers between devices  22.6 us (7%)
  local copies, waits for them, and re-layouts  18.5 us (5%)
    ppermute x9, waiting for transfers between devices, swap(): return lax.ppermute(value, 'ctx', perm)  61.4 us
    all_to_all x1, blocking collectives, per_device(): returned = lax.all_to_all(convolved, 'ctx', 0, 0, tiled=True)  51.2 us
    all_to_all x1, blocking collectives, per_device(): lax.all_to_all(signal, 'ctx', 0, 0, tiled=True, axis_index_groups=line_gr...  46.8 us
    pallas_call x3, Pallas kernels, frequency_call(): pl.pallas_call(kernel, grid=(freq_count // FREQ_CHUNK,), in_specs=specs,...  45.3 us
    all_to_all x1, waiting for transfers between devices, per_device(): spectra.append(lax.all_to_all(later[0], 'ctx', 0, 0, tiled=True))  29.7 us
    all_to_all x1, blocking collectives, per_device(): lax.all_to_all(weight, 'ctx', 0, 0, tiled=True, axis_index_groups=plane_g...  19.2 us
    pallas_call x1, Pallas kernels, project_fused(): pl.pallas_call(functools.partial(project_kernel, lines, plane), in_specs=...  14.3 us
    pallas_call x2, Pallas kernels, spread_spectrum(): pl.pallas_call(functools.partial(spread_kernel, lines, channels), grid=(p...  13.9 us
  transfers between devices with their start and end apart: 22, of which 16 were waited for; matrix products, arithmetic and copies ran while one was open for 3% of the time, Pallas kernels for 17%

profile of v3, /device:TPU:0, one launch (start us, length us, event | category | flops | bytes accessed | tf_op | source)
XLA Modules:
  0.0 344.9 jit_solution(16985126805613832160)
XLA Ops:
  0.0 1.5 copy.37
  2.0 19.2 %all_to_all.25.refs_0_ = bf16[4,256,512]{2,1,0:T(8,128)(2,1)S(1)} all-to-all(bf16[4,256,512]{2,1,0:T(8,128)(2,1)S(1)} %bitcast.26), channel_id=1, replica_groups={{0,2,4,6},{8,10,12,14},{16,18,20,22},{24,26,28,30},{1,3,5,7},{9,11,13,1..., dimensions={0} | all-to-all | bytes 2097152 | tf_op jit(solution)/shard_map/all_to_all | solution.py:558
  21.3 1.6 collective-permute-start
  24.6 6.9 %spread_spectrum.2 = bf16[4,4,2,384,128]{4,3,2,1,0:T(8,128)(2,1)} custom-call(f32[2,2,384,2048]{3,2,1,0:T(8,128)} %values_ref.3), custom_call_target="tpu_custom_call" | custom-call | bytes 9437184 | tf_op jit(solution)/shard_map/spread_spectrum/pallas_call | solution.py:365
  31.5 9.1 %collective-permute-done.1.refs_1_.refs_2_ = bf16[384,1024]{1,0:T(8,128)(2,1)S(1)} collective-permute-done((bf16[384,1024]{1,0:T(8,128)(2,1)S(1)}, bf16[384,1024]{1,0:T(8,128)(2,1)S(1)}, u32[]{:S(2)}, u32[]{:S(2)}) %collective-permute-start.1) | collective-permute-done | bytes 786464 | tf_op jit(solution)/shard_map/ppermute | solution.py:552
  41.5 5.0 %collective-permute-done.refs_0_ = bf16[4,256,512]{2,1,0:T(8,128)(2,1)S(1)} collective-permute-done((bf16[4,256,512]{2,1,0:T(8,128)(2,1)S(1)}, bf16[4,256,512]{2,1,0:T(8,128)(2,1)S(1)}, u32[]{:S(2)}, u32[]{:S(2)}) %collective-permute-start) | collective-permute-done | bytes 1048608 | tf_op jit(solution)/shard_map/ppermute | solution.py:594
  47.5 2.2 copy.52.refs_0_
  52.3 7.0 %spread_spectrum.3 = bf16[4,4,2,384,128]{4,3,2,1,0:T(8,128)(2,1)} custom-call(f32[2,2,384,2048]{3,2,1,0:T(8,128)} %values_ref.3), custom_call_target="tpu_custom_call" | custom-call | bytes 9437184 | tf_op jit(solution)/shard_map/spread_spectrum/pallas_call | solution.py:365
  60.5 3.3 constant_dynamic-slice_fusion
  66.1 1.6 collective-permute-done.4.refs_1_.refs_10_
  69.1 3.0 collective-permute-done.3.refs_0_
  73.2 1.6 collective-permute-start.7
  75.3 14.1 %collective-permute-done.7.refs_7_.refs_3_ = bf16[384,1024]{1,0:T(8,128)(2,1)S(1)} collective-permute-done((bf16[384,1024]{1,0:T(8,128)(2,1)S(1)}, bf16[384,1024]{1,0:T(8,128)(2,1)S(1)}, u32[]{:S(2)}, u32[]{:S(2)}) %collective-permute-start.7) | collective-permute-done | bytes 786464 | tf_op jit(solution)/shard_map/ppermute | solution.py:552
  89.4 1.7 collective-permute-done.8.refs_8_.refs_2_
  91.1 4.6 %collective-permute-done.6.refs_4_.refs_3_.refs_1_ = bf16[4,256,512]{2,1,0:T(8,128)(2,1)S(1)} collective-permute-done((bf16[4,256,512]{2,1,0:T(8,128)(2,1)}, bf16[4,256,512]{2,1,0:T(8,128)(2,1)S(1)}, u32[]{:S(2)}, u32[]{:S(2)}) %collective-permute-start.6) | collective-permute-done | bytes 1048608 | tf_op jit(solution)/shard_map/ppermute | solution.py:594
  96.7 3.7 %all-to-all-start.1 = ((bf16[16,2,384,128]{3,2,1,0:T(8,128)(2,1)}), bf16[16,2,384,128]{3,2,1,0:T(8,128)(2,1)S(1)}, u32[]{:S(2)}, u32[]{:S(2)}) async-start(bf16[16,2,384,128]{3,2,1,0:T(8,128)(2,1)} %after.11), calls=%async_computation.1 | async-start | bytes 6291456 | tf_op jit(solution)/shard_map/all_to_all | solution.py:602
  101.6 1.5 collective-permute-done.10.refs_13_
  106.5 1.9 collective-permute-start.17
  109.7 1.7 collective-permute-start.19
  112.0 6.6 %collective-permute-done.17.refs_21_ = bf16[384,512]{1,0:T(8,128)(2,1)S(1)} collective-permute-done((bf16[384,512]{1,0:T(8,128)(2,1)}, bf16[384,512]{1,0:T(8,128)(2,1)S(1)}, u32[]{:S(2)}, u32[]{:S(2)}) %collective-permute-start.17) | collective-permute-done | bytes 393248 | tf_op jit(solution)/shard_map/ppermute | solution.py:552
  118.7 26.1 %collective-permute-done.18.refs_22_ = bf16[384,512]{1,0:T(8,128)(2,1)} collective-permute-done((bf16[384,512]{1,0:T(8,128)(2,1)}, bf16[384,512]{1,0:T(8,128)(2,1)}, u32[]{:S(2)}, u32[]{:S(2)}) %collective-permute-start.18) | collective-permute-done | bytes 393248 | tf_op jit(solution)/shard_map/ppermute | solution.py:552
  144.7 14.3 %project.1.refs_0_ = bf16[4,4,384,128]{3,2,1,0:T(8,128)(2,1)} custom-call(s32[3]{0:T(128)} %pad_add_fusion.place_ref, bf16[4,256,512]{2,1,0:T(8,128)(2,1)} %copy-done.9, bf16[4,256,512]{2,1,0:T(8,128)(2,1)} %after.7.refs_5_.refs_1_, bf16[4,256,512]{2,1,0:T(8,128)(2,1)} %after.9.refs_2_, bf16[4,256,512]{2,1,0:T(8,128)(2,1)} %copy-done.4, ...), custom_call_target="tpu_custom_call" | custom-call | flops 6442450944 | bytes 18350080 | tf_op jit(solution)/shard_map/project/pallas_call | solution.py:481
  159.0 1.7 copy-done
  160.7 46.8 %all_to_all.26 = bf16[4,4,384,128]{3,2,1,0:T(8,128)(2,1)} all-to-all(bf16[4,4,384,128]{3,2,1,0:T(8,128)(2,1)} %after.12), channel_id=1, replica_groups={{0,8,16,24},{2,10,18,26},{4,12,20,28},{6,14,22,30},{1,9,17,25},{3,11,19..., dimensions={0} | all-to-all | bytes 3145728 | tf_op jit(solution)/shard_map/all_to_all | solution.py:615
  207.6 5.4 %all-to-all-start.3 = ((bf16[16,2,384,128]{3,2,1,0:T(8,128)(2,1)}), bf16[16,2,384,128]{3,2,1,0:T(8,128)(2,1)S(1)}, u32[]{:S(2)}, u32[]{:S(2)}) async-start(bf16[16,2,384,128]{3,2,1,0:T(8,128)(2,1)} %after.13), calls=%async_computation.3 | async-start | bytes 6291456 | tf_op jit(solution)/shard_map/all_to_all | solution.py:620
  213.0 10.4 %forward.1.forward_ref = f32[16,2,384,128]{3,2,1,0:T(8,128)} custom-call(f32[768]{0:T(1024)} %constant.83.clone.coarse_ref, bf16[16,384,128]{2,1,0:T(8,128)(2,1)} %bitcast.24, bf16[512,256]{1,0:T(8,128)(2,1)} %constant.84.clone.slab_high_ref, bf16[512,256]{1,0:T(8,128)(2,1)} %constant.85.clone.slab_low_ref, bf16[768,768]{1,0:T(8,128)(2,1)} %constant.81.clone.rows_ref), custom_call_target="tpu_custom_call" | custom-call | flops 4026531840 | bytes 3279872 | tf_op jit(solution)/shard_map/forward/pallas_call | solution.py:273
  223.3 20.6 %convolve.1.other_ref = f32[16,384,128]{2,1,0:T(8,128)} custom-call(f32[768]{0:T(1024)} %constant.75.clone.coarse_ref, f32[768]{0:T(1024)} %constant.76.clone.coarse_back_ref, bf16[16,384,128]{2,1,0:T(8,128)(2,1)} %bitcast.25, bf16[16,2,384,128]{3,2,1,0:T(8,128)(2,1)} %copy-done, bf16[512,256]{1,0:T(8,128)(2,1)} %constant.77.clone.slab_high_ref, ...), custom_call_target="tpu_custom_call" | custom-call | flops 8858370048 | bytes 8132608 | tf_op jit(solution)/shard_map/convolve/pallas_call | solution.py:273
  244.0 29.7 %all-to-all-done.3.spectrum_ref = bf16[16,2,384,128]{3,2,1,0:T(8,128)(2,1)S(1)} async-done(((bf16[16,2,384,128]{3,2,1,0:T(8,128)(2,1)}), bf16[16,2,384,128]{3,2,1,0:T(8,128)(2,1)S(1)}, u32[]{:S(2)}, u32[]{:S(2)}) %all-to-all-start.3) | async-done | bytes 3145760 | tf_op jit(solution)/shard_map/all_to_all | solution.py:620
  273.7 1.7 copy-done.6
  275.4 14.3 %inverse.1 = bf16[16,384,128]{2,1,0:T(8,128)(2,1)} custom-call(f32[768]{0:T(1024)} %constant.86.clone.coarse_back_ref, f32[16,2,384,128]{3,2,1,0:T(8,128)} %forward.1.forward_ref, bf16[16,2,384,128]{3,2,1,0:T(8,128)(2,1)} %copy-done.6, bf16[256,512]{1,0:T(8,128)(2,1)} %constant.87.clone.back_high_ref, bf16[256,512]{1,0:T(8,128)(2,1)} %constant.88.clone.back_low_ref, ...), custom_call_target="tpu_custom_call" | custom-call | flops 4831838208 | bytes 14289920 | tf_op jit(solution)/shard_map/inverse/pallas_call | solution.py:273
  289.7 51.2 %all_to_all.27 = bf16[16,384,128]{2,1,0:T(8,128)(2,1)} all-to-all(bf16[16,384,128]{2,1,0:T(8,128)(2,1)} %inverse.1), channel_id=1, replica_groups=mesh['ctx'=16,'ch'=2] {'ctx'}, dimensions={0} | all-to-all | bytes 3145728 | tf_op jit(solution)/shard_map/all_to_all | solution.py:627
  340.9 4.0 %gate_output.1 = bf16[384,2048]{1,0:T(8,128)(2,1)} custom-call(bf16[4,4,384,128]{3,2,1,0:T(8,128)(2,1)} %bitcast.22, bf16[384,2048]{1,0:T(8,128)(2,1)} %gate_ref.1), custom_call_target="tpu_custom_call" | custom-call | flops 786432 | bytes 4718592 | tf_op jit(solution)/shard_map/gate_output/pallas_call | solution.py:398
  (71 shorter events, 20.8 us)
Async XLA Ops:
  2.0 20.8 %copy-start.7 = (bf16[384,2048]{1,0:T(8,128)(2,1)S(1)}, bf16[384,2048]{1,0:T(8,128)(2,1)}, u32[]{:S(2)}) copy-start(bf16[384,2048]{1,0:T(8,128)(2,1)} %param.21) | copy-start | bytes 4718596
  21.3 25.2 %collective-permute-start = (bf16[4,256,512]{2,1,0:T(8,128)(2,1)S(1)}, bf16[4,256,512]{2,1,0:T(8,128)(2,1)S(1)}, u32[]{:S(2)}, u32[]{:S(2)}) collective-permute-start(bf16[4,256,512]{2,1,0:T(8,128)(2,1)S(1)} %all_to_all.25.refs_0_), channel_id=1, source_target_pairs={{0,8},{2,10},{4,12},{6,14},{8,16},{10,18},{12,20},{14,22},{16,24},... | collective-permute-start | bytes 3145736 | tf_op jit(solution)/shard_map/ppermute | solution.py:594
  23.0 8.5 %copy-start.12 = (bf16[384,1024]{1,0:T(8,128)(2,1)}, bf16[384,1024]{1,0:T(8,128)(2,1)S(1)}, u32[]{:S(2)}) copy-start(bf16[384,1024]{1,0:T(8,128)(2,1)S(1)} %get-tuple-element.21.refs_5_) | copy-start | bytes 2359300
  23.0 8.5 %copy-start.14 = (bf16[384,1024]{1,0:T(8,128)(2,1)}, bf16[384,1024]{1,0:T(8,128)(2,1)S(1)}, u32[]{:S(2)}) copy-start(bf16[384,1024]{1,0:T(8,128)(2,1)S(1)} %get-tuple-element.22.refs_4_) | copy-start | bytes 2359300
  23.0 17.5 %collective-permute-start.1 = (bf16[384,1024]{1,0:T(8,128)(2,1)S(1)}, bf16[384,1024]{1,0:T(8,128)(2,1)S(1)}, u32[]{:S(2)}, u32[]{:S(2)}) collective-permute-start(bf16[384,1024]{1,0:T(8,128)(2,1)S(1)} %get-tuple-element.22.refs_4_), channel_id=1, source_target_pairs={{0,2},{2,0},{4,6},{6,4},{8,10},{10,8},{12,14},{14,12},{16,18},{18,... | collective-permute-start | bytes 2359304 | tf_op jit(solution)/shard_map/ppermute | solution.py:552
  24.0 17.5 %collective-permute-start.2 = (bf16[384,1024]{1,0:T(8,128)(2,1)S(1)}, bf16[384,1024]{1,0:T(8,128)(2,1)S(1)}, u32[]{:S(2)}, u32[]{:S(2)}) collective-permute-start(bf16[384,1024]{1,0:T(8,128)(2,1)S(1)} %get-tuple-element.21.refs_5_), channel_id=1, source_target_pairs={{0,4},{2,6},{4,0},{6,2},{8,12},{10,14},{12,8},{14,10},{16,20},{18,... | collective-permute-start | bytes 2359304 | tf_op jit(solution)/shard_map/ppermute | solution.py:552
  40.6 5.9 %copy-start.1 = (bf16[384,1024]{1,0:T(8,128)(2,1)}, bf16[384,1024]{1,0:T(8,128)(2,1)S(1)}, u32[]{:S(2)}) copy-start(bf16[384,1024]{1,0:T(8,128)(2,1)S(1)} %collective-permute-done.1.refs_1_.refs_2_) | copy-start | bytes 2359300
  41.5 5.0 %copy-start.2 = (bf16[384,1024]{1,0:T(8,128)(2,1)}, bf16[384,1024]{1,0:T(8,128)(2,1)S(1)}, u32[]{:S(2)}) copy-start(bf16[384,1024]{1,0:T(8,128)(2,1)S(1)} %collective-permute-done.2.refs_2_.refs_3_) | copy-start | bytes 2359300
  47.5 2.2 copy-start.3
  47.5 24.6 %collective-permute-start.3 = (bf16[4,256,512]{2,1,0:T(8,128)(2,1)}, bf16[4,256,512]{2,1,0:T(8,128)(2,1)}, u32[]{:S(2)}, u32[]{:S(2)}) collective-permute-start(bf16[4,256,512]{2,1,0:T(8,128)(2,1)} %after.7.refs_5_.refs_1_), channel_id=1, source_target_pairs={{0,8},{2,10},{4,12},{6,14},{8,16},{10,18},{12,20},{14,22},{16,24},... | collective-permute-start | bytes 3145736 | tf_op jit(solution)/shard_map/ppermute | solution.py:594
  50.6 17.2 %collective-permute-start.4 = (bf16[384,1024]{1,0:T(8,128)(2,1)}, bf16[384,1024]{1,0:T(8,128)(2,1)}, u32[]{:S(2)}, u32[]{:S(2)}) collective-permute-start(bf16[384,1024]{1,0:T(8,128)(2,1)} %get-tuple-element.11.refs_6_), channel_id=1, source_target_pairs={{0,4},{2,6},{4,0},{6,2},{8,12},{10,14},{12,8},{14,10},{16,20},{18,... | collective-permute-start | bytes 2359304 | tf_op jit(solution)/shard_map/ppermute | solution.py:552
  51.8 17.3 %collective-permute-start.5 = (bf16[384,1024]{1,0:T(8,128)(2,1)}, bf16[384,1024]{1,0:T(8,128)(2,1)}, u32[]{:S(2)}, u32[]{:S(2)}) collective-permute-start(bf16[384,1024]{1,0:T(8,128)(2,1)} %get-tuple-element.12.refs_9_), channel_id=1, source_target_pairs={{0,2},{2,0},{4,6},{6,4},{8,10},{10,8},{12,14},{14,12},{16,18},{18,... | collective-permute-start | bytes 2359304 | tf_op jit(solution)/shard_map/ppermute | solution.py:552
  52.3 7.0 %copy-start.8 = (bf16[384,2048]{1,0:T(8,128)(2,1)S(1)}, bf16[384,2048]{1,0:T(8,128)(2,1)}, u32[]{:S(2)}) copy-start(bf16[384,2048]{1,0:T(8,128)(2,1)} %param.24) | copy-start | bytes 4718596
  72.1 23.6 %collective-permute-start.6 = (bf16[4,256,512]{2,1,0:T(8,128)(2,1)}, bf16[4,256,512]{2,1,0:T(8,128)(2,1)S(1)}, u32[]{:S(2)}, u32[]{:S(2)}) collective-permute-start(bf16[4,256,512]{2,1,0:T(8,128)(2,1)} %after.9.refs_2_), channel_id=1, source_target_pairs={{0,8},{2,10},{4,12},{6,14},{8,16},{10,18},{12,20},{14,22},{16,24},... | collective-permute-start | bytes 3145736 | tf_op jit(solution)/shard_map/ppermute | solution.py:594
  73.2 16.2 %collective-permute-start.7 = (bf16[384,1024]{1,0:T(8,128)(2,1)S(1)}, bf16[384,1024]{1,0:T(8,128)(2,1)S(1)}, u32[]{:S(2)}, u32[]{:S(2)}) collective-permute-start(bf16[384,1024]{1,0:T(8,128)(2,1)S(1)} %copy-done.13), channel_id=1, source_target_pairs={{0,2},{2,0},{4,6},{6,4},{8,10},{10,8},{12,14},{14,12},{16,18},{18,... | collective-permute-start | bytes 2359304 | tf_op jit(solution)/shard_map/ppermute | solution.py:552
  74.8 16.2 %collective-permute-start.8 = (bf16[384,1024]{1,0:T(8,128)(2,1)}, bf16[384,1024]{1,0:T(8,128)(2,1)S(1)}, u32[]{:S(2)}, u32[]{:S(2)}) collective-permute-start(bf16[384,1024]{1,0:T(8,128)(2,1)} %copy-done.14), channel_id=1, source_target_pairs={{0,4},{2,6},{4,0},{6,2},{8,12},{10,14},{12,8},{14,10},{16,20},{18,... | collective-permute-start | bytes 2359304 | tf_op jit(solution)/shard_map/ppermute | solution.py:552
  89.4 6.3 %copy-start.10 = (bf16[384,1024]{1,0:T(8,128)(2,1)}, bf16[384,1024]{1,0:T(8,128)(2,1)S(1)}, u32[]{:S(2)}) copy-start(bf16[384,1024]{1,0:T(8,128)(2,1)S(1)} %collective-permute-done.7.refs_7_.refs_3_) | copy-start | bytes 2359300
  91.1 4.6 %copy-start.11 = (bf16[384,1024]{1,0:T(8,128)(2,1)}, bf16[384,1024]{1,0:T(8,128)(2,1)S(1)}, u32[]{:S(2)}) copy-start(bf16[384,1024]{1,0:T(8,128)(2,1)S(1)} %collective-permute-done.8.refs_8_.refs_2_) | copy-start | bytes 2359300
  96.7 62.3 %all-to-all-start.1 = ((bf16[16,2,384,128]{3,2,1,0:T(8,128)(2,1)}), bf16[16,2,384,128]{3,2,1,0:T(8,128)(2,1)S(1)}, u32[]{:S(2)}, u32[]{:S(2)}) async-start(bf16[16,2,384,128]{3,2,1,0:T(8,128)(2,1)} %after.11), calls=%async_computation.1 | async-start | bytes 6291456 | tf_op jit(solution)/shard_map/all_to_all | solution.py:602
  100.4 2.7 collective-permute-start.10
  100.5 3.7 %collective-permute-start.9 = (bf16[384,1024]{1,0:T(8,128)(2,1)}, bf16[384,1024]{1,0:T(8,128)(2,1)}, u32[]{:S(2)}, u32[]{:S(2)}) collective-permute-start(bf16[384,1024]{1,0:T(8,128)(2,1)} %copy-done.14), channel_id=1, source_target_pairs={{0,1},{1,0},{2,3},{3,2},{4,5},{5,4},{6,7},{7,6},{8,9},{9,8},{10,11... | collective-permute-start | bytes 2359304 | tf_op jit(solution)/shard_map/ppermute | solution.py:555
  101.0 4.4 %collective-permute-start.12 = (bf16[384,1024]{1,0:T(8,128)(2,1)}, bf16[384,1024]{1,0:T(8,128)(2,1)}, u32[]{:S(2)}, u32[]{:S(2)}) collective-permute-start(bf16[384,1024]{1,0:T(8,128)(2,1)} %copy-done.10), channel_id=1, source_target_pairs={{0,1},{1,0},{2,3},{3,2},{4,5},{5,4},{6,7},{7,6},{8,9},{9,8},{10,11... | collective-permute-start | bytes 2359304 | tf_op jit(solution)/shard_map/ppermute | solution.py:555
  101.1 5.4 %collective-permute-start.13 = (bf16[384,1024]{1,0:T(8,128)(2,1)}, bf16[384,1024]{1,0:T(8,128)(2,1)}, u32[]{:S(2)}, u32[]{:S(2)}) collective-permute-start(bf16[384,1024]{1,0:T(8,128)(2,1)} %copy-done.11), channel_id=1, source_target_pairs={{0,1},{1,0},{2,3},{3,2},{4,5},{5,4},{6,7},{7,6},{8,9},{9,8},{10,11... | collective-permute-start | bytes 2359304 | tf_op jit(solution)/shard_map/ppermute | solution.py:555
  101.5 6.8 %collective-permute-start.11 = (bf16[384,1024]{1,0:T(8,128)(2,1)}, bf16[384,1024]{1,0:T(8,128)(2,1)}, u32[]{:S(2)}, u32[]{:S(2)}) collective-permute-start(bf16[384,1024]{1,0:T(8,128)(2,1)} %get-tuple-element.11.refs_6_), channel_id=1, source_target_pairs={{0,1},{1,0},{2,3},{3,2},{4,5},{5,4},{6,7},{7,6},{8,9},{9,8},{10,11... | collective-permute-start | bytes 2359304 | tf_op jit(solution)/shard_map/ppermute | solution.py:555
  103.1 6.6 %collective-permute-start.14 = (bf16[384,1024]{1,0:T(8,128)(2,1)}, bf16[384,1024]{1,0:T(8,128)(2,1)}, u32[]{:S(2)}, u32[]{:S(2)}) collective-permute-start(bf16[384,1024]{1,0:T(8,128)(2,1)} %get-tuple-element.12.refs_9_), channel_id=1, source_target_pairs={{0,1},{1,0},{2,3},{3,2},{4,5},{5,4},{6,7},{7,6},{8,9},{9,8},{10,11... | collective-permute-start | bytes 2359304 | tf_op jit(solution)/shard_map/ppermute | solution.py:555
  104.2 7.8 %collective-permute-start.15 = (bf16[384,1024]{1,0:T(8,128)(2,1)}, bf16[384,1024]{1,0:T(8,128)(2,1)}, u32[]{:S(2)}, u32[]{:S(2)}) collective-permute-start(bf16[384,1024]{1,0:T(8,128)(2,1)} %collective-permute-done.4.refs_1_.refs_10_), channel_id=1, source_target_pairs={{0,1},{1,0},{2,3},{3,2},{4,5},{5,4},{6,7},{7,6},{8,9},{9,8},{10,11... | collective-permute-start | bytes 2359304 | tf_op jit(solution)/shard_map/ppermute | solution.py:555
  105.4 6.7 %collective-permute-start.16 = (bf16[384,1024]{1,0:T(8,128)(2,1)}, bf16[384,1024]{1,0:T(8,128)(2,1)}, u32[]{:S(2)}, u32[]{:S(2)}) collective-permute-start(bf16[384,1024]{1,0:T(8,128)(2,1)} %collective-permute-done.5.refs_2_.refs_11_), channel_id=1, source_target_pairs={{0,1},{1,0},{2,3},{3,2},{4,5},{5,4},{6,7},{7,6},{8,9},{9,8},{10,11... | collective-permute-start | bytes 2359304 | tf_op jit(solution)/shard_map/ppermute | solution.py:555
  106.5 12.2 %collective-permute-start.17 = (bf16[384,512]{1,0:T(8,128)(2,1)}, bf16[384,512]{1,0:T(8,128)(2,1)S(1)}, u32[]{:S(2)}, u32[]{:S(2)}) collective-permute-start(bf16[384,512]{1,0:T(8,128)(2,1)} %get-tuple-element.14), channel_id=1, source_target_pairs={{0,2},{2,0},{4,6},{6,4},{8,10},{10,8},{12,14},{14,12},{16,18},{18,... | collective-permute-start | bytes 1179656 | tf_op jit(solution)/shard_map/ppermute | solution.py:552
  108.4 36.4 %collective-permute-start.18 = (bf16[384,512]{1,0:T(8,128)(2,1)}, bf16[384,512]{1,0:T(8,128)(2,1)}, u32[]{:S(2)}, u32[]{:S(2)}) collective-permute-start(bf16[384,512]{1,0:T(8,128)(2,1)} %get-tuple-element.15), channel_id=1, source_target_pairs={{0,4},{2,6},{4,0},{6,2},{8,12},{10,14},{12,8},{14,10},{16,20},{18,... | collective-permute-start | bytes 1179656 | tf_op jit(solution)/shard_map/ppermute | solution.py:552
  109.7 35.0 %collective-permute-start.19 = (bf16[384,512]{1,0:T(8,128)(2,1)}, bf16[384,512]{1,0:T(8,128)(2,1)}, u32[]{:S(2)}, u32[]{:S(2)}) collective-permute-start(bf16[384,512]{1,0:T(8,128)(2,1)} %get-tuple-element.16), channel_id=1, source_target_pairs={{0,6},{2,4},{4,2},{6,0},{8,14},{10,12},{12,10},{14,8},{16,22},{18,... | collective-permute-start | bytes 1179656 | tf_op jit(solution)/shard_map/ppermute | solution.py:552
  118.7 26.1 %copy-start.15 = (bf16[384,512]{1,0:T(8,128)(2,1)}, bf16[384,512]{1,0:T(8,128)(2,1)S(1)}, u32[]{:S(2)}) copy-start(bf16[384,512]{1,0:T(8,128)(2,1)S(1)} %collective-permute-done.17.refs_21_) | copy-start | bytes 1179652
  207.6 66.2 %all-to-all-start.3 = ((bf16[16,2,384,128]{3,2,1,0:T(8,128)(2,1)}), bf16[16,2,384,128]{3,2,1,0:T(8,128)(2,1)S(1)}, u32[]{:S(2)}, u32[]{:S(2)}) async-start(bf16[16,2,384,128]{3,2,1,0:T(8,128)(2,1)} %after.13), calls=%async_computation.3 | async-start | bytes 6291456 | tf_op jit(solution)/shard_map/all_to_all | solution.py:620
  (6 other events, 8.2 us)

commit v4 on v3

--- a/solution.py
+++ b/solution.py
@@ -14,6 +14,7 @@
 VMEM_LIMIT = 56 * 1024 * 1024
 TIME_TILE = 16
 FREQ_CHUNK = 4
+PRODUCT_CHUNK = 2
 
 
 def plane_size(ctx_size):
@@ -118,34 +119,35 @@
 def product_and_back(forward, spectrum_ref, rows_back_ref, coarse_back_ref, work_ref, rest_ref, first):
     _, _, tok_rows, channels = work_ref.shape
     groups = tok_rows // TIME_TILE
-    products = []
-    for at in range(FREQ_CHUNK):
-        real, imag = forward(at)
-        spec_real = spectrum_ref[at, 0].astype(F32)
-        spec_imag = spectrum_ref[at, 1].astype(F32)
-        products.append(
-            jnp.concatenate(
-                [
-                    (spec_real * real - spec_imag * imag).astype(BF16),
-                    (spec_real * imag + spec_imag * real).astype(BF16),
-                ],
-                axis=0,
+    for chunk in range(0, FREQ_CHUNK, PRODUCT_CHUNK):
+        products = []
+        for at in range(chunk, chunk + PRODUCT_CHUNK):
+            real, imag = forward(at)
+            spec_real = spectrum_ref[at, 0].astype(F32)
+            spec_imag = spectrum_ref[at, 1].astype(F32)
+            products.append(
+                jnp.concatenate(
+                    [
+                        (spec_real * real - spec_imag * imag).astype(BF16),
+                        (spec_real * imag + spec_imag * real).astype(BF16),
+                    ],
+                    axis=0,
+                )
             )
+        inverse = jnp.dot(
+            rows_back_ref[...], jnp.concatenate(products, axis=1), preferred_element_type=F32
         )
-    inverse = jnp.dot(
-        rows_back_ref[...], jnp.concatenate(products, axis=1), preferred_element_type=F32
-    )
-    for at in range(FREQ_CHUNK):
-        lanes = slice(at * channels, (at + 1) * channels)
-        for group in range(groups):
-            rows = slice(group * TIME_TILE, (group + 1) * TIME_TILE)
-            real = inverse[rows, lanes]
-            imag = inverse[tok_rows + rows.start : tok_rows + rows.stop, lanes]
-            cos, sin = coarse_turn(coarse_back_ref, groups, first + at, group)
-            for part, value in enumerate((real * cos + imag * sin, imag * cos - real * sin)):
-                high = value.astype(BF16)
-                work_ref[first + at, part, rows, :] = high
-                rest_ref[first + at, part, rows, :] = (value - high.astype(F32)).astype(BF16)
+        for at in range(chunk, chunk + PRODUCT_CHUNK):
+            lanes = slice((at - chunk) * channels, (at - chunk + 1) * channels)
+            for group in range(groups):
+                rows = slice(group * TIME_TILE, (group + 1) * TIME_TILE)
+                real = inverse[rows, lanes]
+                imag = inverse[tok_rows + rows.start : tok_rows + rows.stop, lanes]
+                cos, sin = coarse_turn(coarse_back_ref, groups, first + at, group)
+                for part, value in enumerate((real * cos + imag * sin, imag * cos - real * sin)):
+                    high = value.astype(BF16)
+                    work_ref[first + at, part, rows, :] = high
+                    rest_ref[first + at, part, rows, :] = (value - high.astype(F32)).astype(BF16)
 
 
 def slab_back_stage(work_ref, rest_ref, high_ref, low_ref, others, out_ref):
@@ -175,26 +177,23 @@
             out_ref[:, pl.ds(start, tile), :] = value.astype(out_ref.dtype)
 
 
-def convolve_kernel(
-    coarse_ref,
-    coarse_back_ref,
-    signal_ref,
-    spectrum_ref,
-    slab_high_ref,
-    slab_low_ref,
-    back_high_ref,
-    back_low_ref,
-    rows_ref,
-    rows_back_ref,
-    out_ref,
-    work_ref,
-    rest_ref,
-):
+def gather_signal(place_ref, piece_refs, signal_ref):
+    lines = len(piece_refs)
+    for k, ref in enumerate(piece_refs):
+        line = lax.rem(place_ref[0] + lines - k, lines)
+        signal_ref[pl.ds(line * ref.shape[0], ref.shape[0])] = ref[...]
+
+
+def convolve_kernel(lines, place_ref, coarse_ref, coarse_back_ref, *refs):
+    piece_refs, refs = refs[:lines], refs[lines:]
+    spectrum_ref, slab_high_ref, slab_low_ref, back_high_ref, back_low_ref = refs[:5]
+    rows_ref, rows_back_ref, out_ref, signal_ref, work_ref, rest_ref = refs[5:]
     _, tok_rows, channels = signal_ref.shape
     step = pl.program_id(0)
 
     @pl.when(step == 0)
     def _():
+        gather_signal(place_ref, piece_refs, signal_ref)
         slab_stage(coarse_ref, signal_ref, slab_high_ref, slab_low_ref, work_ref)
 
     first = step * FREQ_CHUNK
@@ -211,12 +210,15 @@
         slab_back_stage(work_ref, rest_ref, back_high_ref, back_low_ref, [], out_ref)
 
 
-def forward_kernel(coarse_ref, signal_ref, slab_high_ref, slab_low_ref, rows_ref, out_ref, work_ref):
+def forward_kernel(lines, place_ref, coarse_ref, *refs):
+    piece_refs, refs = refs[:lines], refs[lines:]
+    slab_high_ref, slab_low_ref, rows_ref, out_ref, signal_ref, work_ref = refs
     _, tok_rows, channels = signal_ref.shape
     step = pl.program_id(0)
 
     @pl.when(step == 0)
     def _():
+        gather_signal(place_ref, piece_refs, signal_ref)
         slab_stage(coarse_ref, signal_ref, slab_high_ref, slab_low_ref, work_ref)
 
     transformed = rows_stage(work_ref, rows_ref, step * FREQ_CHUNK)
@@ -285,8 +287,12 @@
     )(*arrays)
 
 
-def convolve_fused(signal, spectra, tables):
-    slab_count, tok_rows, channels = signal.shape
+def convolve_fused(place, pieces, spectra, tables):
+    lines = len(pieces)
+    plane, tok_rows, channels = pieces[0].shape
+    slab_count = lines * plane
+    signal = jax.ShapeDtypeStruct((slab_count, tok_rows, channels), BF16)
+    gathered = pltpu.VMEM(signal.shape, BF16)
     freq_count = spectra[0].shape[0]
     rows_flops = 2 * freq_count * channels * (2 * tok_rows) ** 2
     slab_flops = 4 * freq_count * channels * tok_rows * slab_count * TIME_TILE
@@ -294,13 +300,14 @@
     total = None
     for spectrum, table in zip(spectra[:-1], tables[:-1]):
         part = frequency_call(
-            convolve_kernel,
+            functools.partial(convolve_kernel, lines),
             "convolve",
             freq_count,
             [
+                (place, "scalar"),
                 (table["coarse"], "scalar"),
                 (table["coarse_back"], "scalar"),
-                (signal, "whole"),
+                *[(piece, "whole") for piece in pieces],
                 (spectrum, "blocked"),
                 *[(t, "whole") for t in table["slab"]],
                 *[(t, "whole") for t in table["slab_back"]],
@@ -309,7 +316,7 @@
             ],
             jax.ShapeDtypeStruct(signal.shape, F32),
             False,
-            [work, work],
+            [gathered, work, work],
             2 * rows_flops + 5 * slab_flops,
         )
         total = part if total is None else total + part
@@ -317,18 +324,19 @@
         total = jnp.zeros(signal.shape, F32)
     table = tables[-1]
     forward = frequency_call(
-        forward_kernel,
+        functools.partial(forward_kernel, lines),
         "forward",
         freq_count,
         [
+            (place, "scalar"),
             (table["coarse"], "scalar"),
-            (signal, "whole"),
+            *[(piece, "whole") for piece in pieces],
             *[(t, "whole") for t in table["slab"]],
             (table["rows"], "whole"),
         ],
         jax.ShapeDtypeStruct((freq_count, 2, tok_rows, channels), F32),
         True,
-        [work],
+        [gathered, work],
         rows_flops + 2 * slab_flops,
     )
     return frequency_call(
@@ -468,7 +476,8 @@
                 total = term if total is None else total + term
         value = (gate_refs[d][...].astype(F32) * total).astype(BF16)
         for line in range(lines):
-            out_ref[line, plane_at ^ d] = value[:, line * channels : (line + 1) * channels]
+            onward = lax.rem(line + lines - line_at, lines)
+            out_ref[onward, plane_at ^ d] = value[:, line * channels : (line + 1) * channels]
 
 
 def project_fused(place, along, pieces, gates):
@@ -509,7 +518,8 @@
         at = jnp.mod(core - e, len(pieces))
         total += jnp.einsum("phtk,hkc->ptc", piece, weight[at], preferred_element_type=F32)
     value = (gates.astype(F32) * total).astype(BF16)[take_plane]
-    return value.reshape(plane, tok_rows, lines, wide // lines).transpose(2, 0, 1, 3)
+    value = value.reshape(plane, tok_rows, lines, wide // lines).transpose(2, 0, 1, 3)
+    return value[jnp.mod(line_at + jnp.arange(lines), lines)]
 
 
 def after(values, earlier):
@@ -544,7 +554,6 @@
     tie = after if channels % 128 == 0 else lambda values, earlier: values
 
     plane_groups = [[z * plane + p for p in range(plane)] for z in range(lines)]
-    line_groups = [[z * plane + p for z in range(lines)] for p in range(plane)]
     onward = [(i, (i + plane) % ctx_size) for i in range(ctx_size)]
 
     def swap(value, d):
@@ -608,22 +617,23 @@
     ]
     fits = channels % 128 == 0 and ch_size == 2 and feat_cols // 2 % weight_rows == 0
     if fits and weight_rows % 16 == 0 and tok_rows % 16 == 0:
-        signal = project_fused(place, along, pieces, gates)
+        projected = project_fused(place, along, pieces, gates)
     else:
-        signal = project_plain(place, along, pieces, gates)
-    signal = tie([signal], spectra)[0]
-    signal = lax.all_to_all(signal, "ctx", 0, 0, tiled=True, axis_index_groups=line_groups)
-    signal = signal.reshape(ctx_size, tok_rows, channels)
-
+        projected = project_plain(place, along, pieces, gates)
+    signals = [projected[0]] + [
+        lax.ppermute(projected[k], "ctx", [(i, (i + k * plane) % ctx_size) for i in range(ctx_size)])
+        for k in range(1, lines)
+    ]
     for at in range(1, freq_local):
-        later = tie(spread[at : at + 1], [signal])
+        later = tie(spread[at : at + 1], spectra[-1:] + signals[1:])
         spectra.append(lax.all_to_all(later[0], "ctx", 0, 0, tiled=True))
 
     if channels % 128 == 0:
-        convolved = convolve_fused(signal, spectra, tables)
+        convolved = convolve_fused(place, signals, spectra, tables)
     else:
         spectrum = jnp.stack(spectra, 1).reshape(ctx_size * freq_local, 2, tok_rows, channels)
-        convolved = convolve_plain(signal, spectrum)
+        signal = jnp.stack(signals)[jnp.mod(line_at - jnp.arange(lines), lines)]
+        convolved = convolve_plain(signal.reshape(ctx_size, tok_rows, channels), spectrum)
     returned = lax.all_to_all(convolved, "ctx", 0, 0, tiled=True)
     return gate_output(returned, gate_q, plane, lines)
 

time: 346 us -> 340 us (0.983)
  blocking collectives: 117 us -> 70.4 us
  waiting for transfers between devices: 108 us -> 133 us
  starting transfers between devices: 22.6 us -> 36 us
    all_to_all x1 -> x0, blocking collectives: 46.8 us -> none  [per_device(): lax.all_to_all(signal, 'ctx', 0, 0, tiled=True, axis_index_groups=line_gr...]
    ppermute x0 -> x3, waiting for transfers between devices: none -> 25.8 us  [per_device(): lax.ppermute(projected[k], 'ctx', [(i, (i + k * plane) % ctx_size) for i...]
    ppermute x0 -> x3, starting transfers between devices: none -> 7.2 us  [per_device(): lax.ppermute(projected[k], 'ctx', [(i, (i + k * plane) % ctx_size) for i...]
    all_to_all x1, starting transfers between devices: 5.4 us -> 11.6 us  [per_device(): spectra.append(lax.all_to_all(later[0], 'ctx', 0, 0, tiled=True))]
    unnamed x35 -> x39, local copies, waits for them, and re-layouts: 11.1 us -> 11.8 us
  transfers between devices with their start and end apart: 22 -> 25, of which waited for: 16 -> 18; matrix products, arithmetic and copies ran while one was open for 3% -> 4% of each run, Pallas kernels for 17% -> 18%
where the time goes in v4:
time: 340 us; the launch traced here: 339 us
  waiting for transfers between devices  133 us (39%)
  Pallas kernels  77.6 us (23%)
  blocking collectives  70.4 us (21%)
  starting transfers between devices  36 us (11%)
  local copies, waits for them, and re-layouts  21.5 us (6%)
    ppermute x9, waiting for transfers between devices, swap(): return lax.ppermute(value, 'ctx', perm)  61.5 us
    all_to_all x1, blocking collectives, per_device(): returned = lax.all_to_all(convolved, 'ctx', 0, 0, tiled=True)  51.2 us
    pallas_call x3, Pallas kernels, frequency_call(): pl.pallas_call(kernel, grid=(freq_count // FREQ_CHUNK,), in_specs=specs,...  45.4 us
    all_to_all x1, waiting for transfers between devices, per_device(): spectra.append(lax.all_to_all(later[0], 'ctx', 0, 0, tiled=True))  28.1 us
    ppermute x3, waiting for transfers between devices, per_device(): lax.ppermute(projected[k], 'ctx', [(i, (i + k * plane) % ctx_size) for i...  25.8 us
    all_to_all x1, blocking collectives, per_device(): lax.all_to_all(weight, 'ctx', 0, 0, tiled=True, axis_index_groups=plane_g...  19.2 us
    pallas_call x1, Pallas kernels, project_fused(): pl.pallas_call(functools.partial(project_kernel, lines, plane), in_specs=...  14.3 us
    pallas_call x2, Pallas kernels, spread_spectrum(): pl.pallas_call(functools.partial(spread_kernel, lines, channels), grid=(p...  13.9 us
  transfers between devices with their start and end apart: 25, of which 18 were waited for; matrix products, arithmetic and copies ran while one was open for 4% of the time, Pallas kernels for 18%

profile of v4, /device:TPU:0, one launch (start us, length us, event | category | flops | bytes accessed | tf_op | source)
XLA Modules:
  0.0 338.8 jit_solution(2370066824023307693)
XLA Ops:
  2.0 19.2 %all_to_all.20.refs_0_ = bf16[4,256,512]{2,1,0:T(8,128)(2,1)S(1)} all-to-all(bf16[4,256,512]{2,1,0:T(8,128)(2,1)S(1)} %bitcast.30), channel_id=1, replica_groups={{0,2,4,6},{8,10,12,14},{16,18,20,22},{24,26,28,30},{1,3,5,7},{9,11,13,1..., dimensions={0} | all-to-all | bytes 2097152 | tf_op jit(solution)/shard_map/all_to_all | solution.py:567
  24.6 6.9 %spread_spectrum.2 = bf16[4,4,2,384,128]{4,3,2,1,0:T(8,128)(2,1)} custom-call(f32[2,2,384,2048]{3,2,1,0:T(8,128)} %values_ref.3), custom_call_target="tpu_custom_call" | custom-call | bytes 9437184 | tf_op jit(solution)/shard_map/spread_spectrum/pallas_call | solution.py:373
  31.5 9.1 %collective-permute-done.1.refs_1_.refs_2_ = bf16[384,1024]{1,0:T(8,128)(2,1)S(1)} collective-permute-done((bf16[384,1024]{1,0:T(8,128)(2,1)S(1)}, bf16[384,1024]{1,0:T(8,128)(2,1)S(1)}, u32[]{:S(2)}, u32[]{:S(2)}) %collective-permute-start.1) | collective-permute-done | bytes 786464 | tf_op jit(solution)/shard_map/ppermute | solution.py:561
  41.5 5.0 %collective-permute-done.refs_0_ = bf16[4,256,512]{2,1,0:T(8,128)(2,1)S(1)} collective-permute-done((bf16[4,256,512]{2,1,0:T(8,128)(2,1)S(1)}, bf16[4,256,512]{2,1,0:T(8,128)(2,1)S(1)}, u32[]{:S(2)}, u32[]{:S(2)}) %collective-permute-start) | collective-permute-done | bytes 1048608 | tf_op jit(solution)/shard_map/ppermute | solution.py:603
  47.5 2.1 copy.51.refs_0_
  52.3 7.0 %spread_spectrum.3 = bf16[4,4,2,384,128]{4,3,2,1,0:T(8,128)(2,1)} custom-call(f32[2,2,384,2048]{3,2,1,0:T(8,128)} %values_ref.3), custom_call_target="tpu_custom_call" | custom-call | bytes 9437184 | tf_op jit(solution)/shard_map/spread_spectrum/pallas_call | solution.py:373
  60.5 3.3 constant_dynamic-slice_fusion
  66.1 1.6 collective-permute-done.4.refs_1_.refs_10_
  69.0 3.0 collective-permute-done.3.refs_0_
  75.3 14.1 %collective-permute-done.7.refs_7_.refs_3_ = bf16[384,1024]{1,0:T(8,128)(2,1)S(1)} collective-permute-done((bf16[384,1024]{1,0:T(8,128)(2,1)S(1)}, bf16[384,1024]{1,0:T(8,128)(2,1)S(1)}, u32[]{:S(2)}, u32[]{:S(2)}) %collective-permute-start.7) | collective-permute-done | bytes 786464 | tf_op jit(solution)/shard_map/ppermute | solution.py:561
  89.4 1.7 collective-permute-done.8.refs_8_.refs_2_
  91.1 4.6 %collective-permute-done.6.refs_4_.refs_3_.refs_1_ = bf16[4,256,512]{2,1,0:T(8,128)(2,1)S(1)} collective-permute-done((bf16[4,256,512]{2,1,0:T(8,128)(2,1)}, bf16[4,256,512]{2,1,0:T(8,128)(2,1)S(1)}, u32[]{:S(2)}, u32[]{:S(2)}) %collective-permute-start.6) | collective-permute-done | bytes 1048608 | tf_op jit(solution)/shard_map/ppermute | solution.py:603
  96.7 3.7 %all-to-all-start.1 = ((bf16[16,2,384,128]{3,2,1,0:T(8,128)(2,1)}), bf16[16,2,384,128]{3,2,1,0:T(8,128)(2,1)S(1)}, u32[]{:S(2)}, u32[]{:S(2)}) async-start(bf16[16,2,384,128]{3,2,1,0:T(8,128)(2,1)} %after.10), calls=%async_computation.1 | async-start | bytes 6291456 | tf_op jit(solution)/shard_map/all_to_all | solution.py:611
  106.5 1.9 collective-permute-start.17
  109.7 1.7 collective-permute-start.19
  112.0 6.6 %collective-permute-done.17.refs_21_ = bf16[384,512]{1,0:T(8,128)(2,1)S(1)} collective-permute-done((bf16[384,512]{1,0:T(8,128)(2,1)}, bf16[384,512]{1,0:T(8,128)(2,1)S(1)}, u32[]{:S(2)}, u32[]{:S(2)}) %collective-permute-start.17) | collective-permute-done | bytes 393248 | tf_op jit(solution)/shard_map/ppermute | solution.py:561
  118.7 26.1 %collective-permute-done.18.refs_22_ = bf16[384,512]{1,0:T(8,128)(2,1)} collective-permute-done((bf16[384,512]{1,0:T(8,128)(2,1)}, bf16[384,512]{1,0:T(8,128)(2,1)}, u32[]{:S(2)}, u32[]{:S(2)}) %collective-permute-start.18) | collective-permute-done | bytes 393248 | tf_op jit(solution)/shard_map/ppermute | solution.py:561
  144.7 14.3 %project.1 = bf16[4,4,384,128]{3,2,1,0:T(8,128)(2,1)} custom-call(s32[3]{0:T(128)} %pad_add_fusion.place_ref, bf16[4,256,512]{2,1,0:T(8,128)(2,1)} %copy-done.9, bf16[4,256,512]{2,1,0:T(8,128)(2,1)} %after.6.refs_5_.refs_1_, bf16[4,256,512]{2,1,0:T(8,128)(2,1)} %after.8.refs_2_, bf16[4,256,512]{2,1,0:T(8,128)(2,1)} %copy-done.4, ...), custom_call_target="tpu_custom_call" | custom-call | flops 6442450944 | bytes 18350080 | tf_op jit(solution)/shard_map/project/pallas_call | solution.py:490
  159.0 2.2 slice_bitcast_fusion
  161.3 4.8 %collective-permute-start.20 = (bf16[4,384,128]{2,1,0:T(8,128)(2,1)S(1)}, bf16[4,384,128]{2,1,0:T(8,128)(2,1)S(1)}, u32[]{:S(2)}, u32[]{:S(2)}) collective-permute-start(bf16[4,384,128]{2,1,0:T(8,128)(2,1)S(1)} %get-tuple-element.19), channel_id=1, source_target_pairs={{0,8},{2,10},{4,12},{6,14},{8,16},{10,18},{12,20},{14,22},{16,24},... | collective-permute-start | bytes 1179656 | tf_op jit(solution)/shard_map/ppermute | solution.py:624
  166.1 2.4 collective-permute-start.22
  168.5 7.2 %collective-permute-done.20.refs_1_.refs_2_ = bf16[4,384,128]{2,1,0:T(8,128)(2,1)S(1)} collective-permute-done((bf16[4,384,128]{2,1,0:T(8,128)(2,1)S(1)}, bf16[4,384,128]{2,1,0:T(8,128)(2,1)S(1)}, u32[]{:S(2)}, u32[]{:S(2)}) %collective-permute-start.20) | collective-permute-done | bytes 393248 | tf_op jit(solution)/shard_map/ppermute | solution.py:624
  175.7 18.6 %collective-permute-done.21.refs_2_.refs_3_ = bf16[4,384,128]{2,1,0:T(8,128)(2,1)S(1)} collective-permute-done((bf16[4,384,128]{2,1,0:T(8,128)(2,1)S(1)}, bf16[4,384,128]{2,1,0:T(8,128)(2,1)S(1)}, u32[]{:S(2)}, u32[]{:S(2)}) %collective-permute-start.21) | collective-permute-done | bytes 393248 | tf_op jit(solution)/shard_map/ppermute | solution.py:624
  195.0 1.7 copy-done
  196.8 11.6 %all-to-all-start.2 = ((bf16[16,2,384,128]{3,2,1,0:T(8,128)(2,1)}), bf16[16,2,384,128]{3,2,1,0:T(8,128)(2,1)S(1)}, u32[]{:S(2)}, u32[]{:S(2)}) async-start(bf16[16,2,384,128]{3,2,1,0:T(8,128)(2,1)} %after.11), calls=%async_computation.2 | async-start | bytes 6291456 | tf_op jit(solution)/shard_map/all_to_all | solution.py:629
  208.4 10.5 %forward.1.forward_ref = f32[16,2,384,128]{3,2,1,0:T(8,128)} custom-call(s32[3]{0:T(128)} %pad_add_fusion.place_ref, f32[768]{0:T(1024)} %constant.83.clone.coarse_ref, bf16[4,384,128]{2,1,0:T(8,128)(2,1)} %get-tuple-element.20.refs_0_, bf16[4,384,128]{2,1,0:T(8,128)(2,1)} %copy-done.15, bf16[4,384,128]{2,1,0:T(8,128)(2,1)} %copy-done.16, ...), custom_call_target="tpu_custom_call" | custom-call | flops 4026531840 | bytes 3279884 | tf_op jit(solution)/shard_map/forward/pallas_call | solution.py:275
  218.9 20.7 %convolve.1.other_ref = f32[16,384,128]{2,1,0:T(8,128)} custom-call(s32[3]{0:T(128)} %pad_add_fusion.place_ref, f32[768]{0:T(1024)} %constant.75.clone.coarse_ref, f32[768]{0:T(1024)} %constant.76.clone.coarse_back_ref, bf16[4,384,128]{2,1,0:T(8,128)(2,1)} %get-tuple-element.20.refs_0_, bf16[4,384,128]{2,1,0:T(8,128)(2,1)} %copy-done.15, ...), custom_call_target="tpu_custom_call" | custom-call | flops 8858370048 | bytes 8132620 | tf_op jit(solution)/shard_map/convolve/pallas_call | solution.py:275
  239.6 28.1 %all-to-all-done.2.spectrum_ref = bf16[16,2,384,128]{3,2,1,0:T(8,128)(2,1)S(1)} async-done(((bf16[16,2,384,128]{3,2,1,0:T(8,128)(2,1)}), bf16[16,2,384,128]{3,2,1,0:T(8,128)(2,1)S(1)}, u32[]{:S(2)}, u32[]{:S(2)}) %all-to-all-start.2) | async-done | bytes 3145760 | tf_op jit(solution)/shard_map/all_to_all | solution.py:629
  267.7 1.7 copy-done.6
  269.4 14.2 %inverse.1 = bf16[16,384,128]{2,1,0:T(8,128)(2,1)} custom-call(f32[768]{0:T(1024)} %constant.86.clone.coarse_back_ref, f32[16,2,384,128]{3,2,1,0:T(8,128)} %forward.1.forward_ref, bf16[16,2,384,128]{3,2,1,0:T(8,128)(2,1)} %copy-done.6, bf16[256,512]{1,0:T(8,128)(2,1)} %constant.87.clone.back_high_ref, bf16[256,512]{1,0:T(8,128)(2,1)} %constant.88.clone.back_low_ref, ...), custom_call_target="tpu_custom_call" | custom-call | flops 4831838208 | bytes 14289920 | tf_op jit(solution)/shard_map/inverse/pallas_call | solution.py:275
  283.6 51.2 %all_to_all.21 = bf16[16,384,128]{2,1,0:T(8,128)(2,1)} all-to-all(bf16[16,384,128]{2,1,0:T(8,128)(2,1)} %inverse.1), channel_id=1, replica_groups=mesh['ctx'=16,'ch'=2] {'ctx'}, dimensions={0} | all-to-all | bytes 3145728 | tf_op jit(solution)/shard_map/all_to_all | solution.py:637
  334.8 4.0 %gate_output.1 = bf16[384,2048]{1,0:T(8,128)(2,1)} custom-call(bf16[4,4,384,128]{3,2,1,0:T(8,128)(2,1)} %bitcast.29, bf16[384,2048]{1,0:T(8,128)(2,1)} %gate_ref.1), custom_call_target="tpu_custom_call" | custom-call | flops 786432 | bytes 4718592 | tf_op jit(solution)/shard_map/gate_output/pallas_call | solution.py:406
  (80 shorter events, 27.7 us)
Async XLA Ops:
  2.0 20.8 %copy-start.7 = (bf16[384,2048]{1,0:T(8,128)(2,1)S(1)}, bf16[384,2048]{1,0:T(8,128)(2,1)}, u32[]{:S(2)}) copy-start(bf16[384,2048]{1,0:T(8,128)(2,1)} %param.21) | copy-start | bytes 4718596
  21.3 25.2 %collective-permute-start = (bf16[4,256,512]{2,1,0:T(8,128)(2,1)S(1)}, bf16[4,256,512]{2,1,0:T(8,128)(2,1)S(1)}, u32[]{:S(2)}, u32[]{:S(2)}) collective-permute-start(bf16[4,256,512]{2,1,0:T(8,128)(2,1)S(1)} %all_to_all.20.refs_0_), channel_id=1, source_target_pairs={{0,8},{2,10},{4,12},{6,14},{8,16},{10,18},{12,20},{14,22},{16,24},... | collective-permute-start | bytes 3145736 | tf_op jit(solution)/shard_map/ppermute | solution.py:603
  23.0 8.5 %copy-start.12 = (bf16[384,1024]{1,0:T(8,128)(2,1)}, bf16[384,1024]{1,0:T(8,128)(2,1)S(1)}, u32[]{:S(2)}) copy-start(bf16[384,1024]{1,0:T(8,128)(2,1)S(1)} %get-tuple-element.25.refs_5_) | copy-start | bytes 2359300
  23.0 8.4 %copy-start.14 = (bf16[384,1024]{1,0:T(8,128)(2,1)}, bf16[384,1024]{1,0:T(8,128)(2,1)S(1)}, u32[]{:S(2)}) copy-start(bf16[384,1024]{1,0:T(8,128)(2,1)S(1)} %get-tuple-element.26.refs_4_) | copy-start | bytes 2359300
  23.0 17.5 %collective-permute-start.1 = (bf16[384,1024]{1,0:T(8,128)(2,1)S(1)}, bf16[384,1024]{1,0:T(8,128)(2,1)S(1)}, u32[]{:S(2)}, u32[]{:S(2)}) collective-permute-start(bf16[384,1024]{1,0:T(8,128)(2,1)S(1)} %get-tuple-element.26.refs_4_), channel_id=1, source_target_pairs={{0,2},{2,0},{4,6},{6,4},{8,10},{10,8},{12,14},{14,12},{16,18},{18,... | collective-permute-start | bytes 2359304 | tf_op jit(solution)/shard_map/ppermute | solution.py:561
  24.0 17.5 %collective-permute-start.2 = (bf16[384,1024]{1,0:T(8,128)(2,1)S(1)}, bf16[384,1024]{1,0:T(8,128)(2,1)S(1)}, u32[]{:S(2)}, u32[]{:S(2)}) collective-permute-start(bf16[384,1024]{1,0:T(8,128)(2,1)S(1)} %get-tuple-element.25.refs_5_), channel_id=1, source_target_pairs={{0,4},{2,6},{4,0},{6,2},{8,12},{10,14},{12,8},{14,10},{16,20},{18,... | collective-permute-start | bytes 2359304 | tf_op jit(solution)/shard_map/ppermute | solution.py:561
  47.5 24.6 %collective-permute-start.3 = (bf16[4,256,512]{2,1,0:T(8,128)(2,1)}, bf16[4,256,512]{2,1,0:T(8,128)(2,1)}, u32[]{:S(2)}, u32[]{:S(2)}) collective-permute-start(bf16[4,256,512]{2,1,0:T(8,128)(2,1)} %after.6.refs_5_.refs_1_), channel_id=1, source_target_pairs={{0,8},{2,10},{4,12},{6,14},{8,16},{10,18},{12,20},{14,22},{16,24},... | collective-permute-start | bytes 3145736 | tf_op jit(solution)/shard_map/ppermute | solution.py:603
  50.5 17.2 %collective-permute-start.4 = (bf16[384,1024]{1,0:T(8,128)(2,1)}, bf16[384,1024]{1,0:T(8,128)(2,1)}, u32[]{:S(2)}, u32[]{:S(2)}) collective-permute-start(bf16[384,1024]{1,0:T(8,128)(2,1)} %get-tuple-element.11.refs_6_), channel_id=1, source_target_pairs={{0,4},{2,6},{4,0},{6,2},{8,12},{10,14},{12,8},{14,10},{16,20},{18,... | collective-permute-start | bytes 2359304 | tf_op jit(solution)/shard_map/ppermute | solution.py:561
  51.8 17.3 %collective-permute-start.5 = (bf16[384,1024]{1,0:T(8,128)(2,1)}, bf16[384,1024]{1,0:T(8,128)(2,1)}, u32[]{:S(2)}, u32[]{:S(2)}) collective-permute-start(bf16[384,1024]{1,0:T(8,128)(2,1)} %get-tuple-element.12.refs_9_), channel_id=1, source_target_pairs={{0,2},{2,0},{4,6},{6,4},{8,10},{10,8},{12,14},{14,12},{16,18},{18,... | collective-permute-start | bytes 2359304 | tf_op jit(solution)/shard_map/ppermute | solution.py:561
  52.3 7.0 %copy-start.8 = (bf16[384,2048]{1,0:T(8,128)(2,1)S(1)}, bf16[384,2048]{1,0:T(8,128)(2,1)}, u32[]{:S(2)}) copy-start(bf16[384,2048]{1,0:T(8,128)(2,1)} %param.24) | copy-start | bytes 4718596
  72.1 23.6 %collective-permute-start.6 = (bf16[4,256,512]{2,1,0:T(8,128)(2,1)}, bf16[4,256,512]{2,1,0:T(8,128)(2,1)S(1)}, u32[]{:S(2)}, u32[]{:S(2)}) collective-permute-start(bf16[4,256,512]{2,1,0:T(8,128)(2,1)} %after.8.refs_2_), channel_id=1, source_target_pairs={{0,8},{2,10},{4,12},{6,14},{8,16},{10,18},{12,20},{14,22},{16,24},... | collective-permute-start | bytes 3145736 | tf_op jit(solution)/shard_map/ppermute | solution.py:603
  73.2 16.2 %collective-permute-start.7 = (bf16[384,1024]{1,0:T(8,128)(2,1)S(1)}, bf16[384,1024]{1,0:T(8,128)(2,1)S(1)}, u32[]{:S(2)}, u32[]{:S(2)}) collective-permute-start(bf16[384,1024]{1,0:T(8,128)(2,1)S(1)} %copy-done.13), channel_id=1, source_target_pairs={{0,2},{2,0},{4,6},{6,4},{8,10},{10,8},{12,14},{14,12},{16,18},{18,... | collective-permute-start | bytes 2359304 | tf_op jit(solution)/shard_map/ppermute | solution.py:561
  74.8 16.2 %collective-permute-start.8 = (bf16[384,1024]{1,0:T(8,128)(2,1)}, bf16[384,1024]{1,0:T(8,128)(2,1)S(1)}, u32[]{:S(2)}, u32[]{:S(2)}) collective-permute-start(bf16[384,1024]{1,0:T(8,128)(2,1)} %copy-done.14), channel_id=1, source_target_pairs={{0,4},{2,6},{4,0},{6,2},{8,12},{10,14},{12,8},{14,10},{16,20},{18,... | collective-permute-start | bytes 2359304 | tf_op jit(solution)/shard_map/ppermute | solution.py:561
  89.4 6.3 %copy-start.10 = (bf16[384,1024]{1,0:T(8,128)(2,1)}, bf16[384,1024]{1,0:T(8,128)(2,1)S(1)}, u32[]{:S(2)}) copy-start(bf16[384,1024]{1,0:T(8,128)(2,1)S(1)} %collective-permute-done.7.refs_7_.refs_3_) | copy-start | bytes 2359300
  96.7 98.3 %all-to-all-start.1 = ((bf16[16,2,384,128]{3,2,1,0:T(8,128)(2,1)}), bf16[16,2,384,128]{3,2,1,0:T(8,128)(2,1)S(1)}, u32[]{:S(2)}, u32[]{:S(2)}) async-start(bf16[16,2,384,128]{3,2,1,0:T(8,128)(2,1)} %after.10), calls=%async_computation.1 | async-start | bytes 6291456 | tf_op jit(solution)/shard_map/all_to_all | solution.py:611
  100.4 2.7 collective-permute-start.10
  100.5 3.7 %collective-permute-start.9 = (bf16[384,1024]{1,0:T(8,128)(2,1)}, bf16[384,1024]{1,0:T(8,128)(2,1)}, u32[]{:S(2)}, u32[]{:S(2)}) collective-permute-start(bf16[384,1024]{1,0:T(8,128)(2,1)} %copy-done.14), channel_id=1, source_target_pairs={{0,1},{1,0},{2,3},{3,2},{4,5},{5,4},{6,7},{7,6},{8,9},{9,8},{10,11... | collective-permute-start | bytes 2359304 | tf_op jit(solution)/shard_map/ppermute | solution.py:564
  101.0 4.4 %collective-permute-start.12 = (bf16[384,1024]{1,0:T(8,128)(2,1)}, bf16[384,1024]{1,0:T(8,128)(2,1)}, u32[]{:S(2)}, u32[]{:S(2)}) collective-permute-start(bf16[384,1024]{1,0:T(8,128)(2,1)} %copy-done.10), channel_id=1, source_target_pairs={{0,1},{1,0},{2,3},{3,2},{4,5},{5,4},{6,7},{7,6},{8,9},{9,8},{10,11... | collective-permute-start | bytes 2359304 | tf_op jit(solution)/shard_map/ppermute | solution.py:564
  101.1 5.4 %collective-permute-start.13 = (bf16[384,1024]{1,0:T(8,128)(2,1)}, bf16[384,1024]{1,0:T(8,128)(2,1)}, u32[]{:S(2)}, u32[]{:S(2)}) collective-permute-start(bf16[384,1024]{1,0:T(8,128)(2,1)} %copy-done.11), channel_id=1, source_target_pairs={{0,1},{1,0},{2,3},{3,2},{4,5},{5,4},{6,7},{7,6},{8,9},{9,8},{10,11... | collective-permute-start | bytes 2359304 | tf_op jit(solution)/shard_map/ppermute | solution.py:564
  101.5 6.8 %collective-permute-start.11 = (bf16[384,1024]{1,0:T(8,128)(2,1)}, bf16[384,1024]{1,0:T(8,128)(2,1)}, u32[]{:S(2)}, u32[]{:S(2)}) collective-permute-start(bf16[384,1024]{1,0:T(8,128)(2,1)} %get-tuple-element.11.refs_6_), channel_id=1, source_target_pairs={{0,1},{1,0},{2,3},{3,2},{4,5},{5,4},{6,7},{7,6},{8,9},{9,8},{10,11... | collective-permute-start | bytes 2359304 | tf_op jit(solution)/shard_map/ppermute | solution.py:564
  103.1 6.6 %collective-permute-start.14 = (bf16[384,1024]{1,0:T(8,128)(2,1)}, bf16[384,1024]{1,0:T(8,128)(2,1)}, u32[]{:S(2)}, u32[]{:S(2)}) collective-permute-start(bf16[384,1024]{1,0:T(8,128)(2,1)} %get-tuple-element.12.refs_9_), channel_id=1, source_target_pairs={{0,1},{1,0},{2,3},{3,2},{4,5},{5,4},{6,7},{7,6},{8,9},{9,8},{10,11... | collective-permute-start | bytes 2359304 | tf_op jit(solution)/shard_map/ppermute | solution.py:564
  104.2 7.8 %collective-permute-start.15 = (bf16[384,1024]{1,0:T(8,128)(2,1)}, bf16[384,1024]{1,0:T(8,128)(2,1)}, u32[]{:S(2)}, u32[]{:S(2)}) collective-permute-start(bf16[384,1024]{1,0:T(8,128)(2,1)} %collective-permute-done.4.refs_1_.refs_10_), channel_id=1, source_target_pairs={{0,1},{1,0},{2,3},{3,2},{4,5},{5,4},{6,7},{7,6},{8,9},{9,8},{10,11... | collective-permute-start | bytes 2359304 | tf_op jit(solution)/shard_map/ppermute | solution.py:564
  105.4 6.6 %collective-permute-start.16 = (bf16[384,1024]{1,0:T(8,128)(2,1)}, bf16[384,1024]{1,0:T(8,128)(2,1)}, u32[]{:S(2)}, u32[]{:S(2)}) collective-permute-start(bf16[384,1024]{1,0:T(8,128)(2,1)} %collective-permute-done.5.refs_2_.refs_11_), channel_id=1, source_target_pairs={{0,1},{1,0},{2,3},{3,2},{4,5},{5,4},{6,7},{7,6},{8,9},{9,8},{10,11... | collective-permute-start | bytes 2359304 | tf_op jit(solution)/shard_map/ppermute | solution.py:564
  106.5 12.2 %collective-permute-start.17 = (bf16[384,512]{1,0:T(8,128)(2,1)}, bf16[384,512]{1,0:T(8,128)(2,1)S(1)}, u32[]{:S(2)}, u32[]{:S(2)}) collective-permute-start(bf16[384,512]{1,0:T(8,128)(2,1)} %get-tuple-element.14), channel_id=1, source_target_pairs={{0,2},{2,0},{4,6},{6,4},{8,10},{10,8},{12,14},{14,12},{16,18},{18,... | collective-permute-start | bytes 1179656 | tf_op jit(solution)/shard_map/ppermute | solution.py:561
  108.4 36.4 %collective-permute-start.18 = (bf16[384,512]{1,0:T(8,128)(2,1)}, bf16[384,512]{1,0:T(8,128)(2,1)}, u32[]{:S(2)}, u32[]{:S(2)}) collective-permute-start(bf16[384,512]{1,0:T(8,128)(2,1)} %get-tuple-element.15), channel_id=1, source_target_pairs={{0,4},{2,6},{4,0},{6,2},{8,12},{10,14},{12,8},{14,10},{16,20},{18,... | collective-permute-start | bytes 1179656 | tf_op jit(solution)/shard_map/ppermute | solution.py:561
  109.7 35.0 %collective-permute-start.19 = (bf16[384,512]{1,0:T(8,128)(2,1)}, bf16[384,512]{1,0:T(8,128)(2,1)}, u32[]{:S(2)}, u32[]{:S(2)}) collective-permute-start(bf16[384,512]{1,0:T(8,128)(2,1)} %get-tuple-element.16), channel_id=1, source_target_pairs={{0,6},{2,4},{4,2},{6,0},{8,14},{10,12},{12,10},{14,8},{16,22},{18,... | collective-permute-start | bytes 1179656 | tf_op jit(solution)/shard_map/ppermute | solution.py:561
  118.7 26.1 %copy-start.17 = (bf16[384,512]{1,0:T(8,128)(2,1)}, bf16[384,512]{1,0:T(8,128)(2,1)S(1)}, u32[]{:S(2)}) copy-start(bf16[384,512]{1,0:T(8,128)(2,1)S(1)} %collective-permute-done.17.refs_21_) | copy-start | bytes 1179652
  161.3 14.4 %collective-permute-start.20 = (bf16[4,384,128]{2,1,0:T(8,128)(2,1)S(1)}, bf16[4,384,128]{2,1,0:T(8,128)(2,1)S(1)}, u32[]{:S(2)}, u32[]{:S(2)}) collective-permute-start(bf16[4,384,128]{2,1,0:T(8,128)(2,1)S(1)} %get-tuple-element.19), channel_id=1, source_target_pairs={{0,8},{2,10},{4,12},{6,14},{8,16},{10,18},{12,20},{14,22},{16,24},... | collective-permute-start | bytes 1179656 | tf_op jit(solution)/shard_map/ppermute | solution.py:624
  166.1 28.2 %collective-permute-start.21 = (bf16[4,384,128]{2,1,0:T(8,128)(2,1)S(1)}, bf16[4,384,128]{2,1,0:T(8,128)(2,1)S(1)}, u32[]{:S(2)}, u32[]{:S(2)}) collective-permute-start(bf16[4,384,128]{2,1,0:T(8,128)(2,1)S(1)} %get-tuple-element.18), channel_id=1, source_target_pairs={{0,16},{2,18},{4,20},{6,22},{8,24},{10,26},{12,28},{14,30},{16,0},... | collective-permute-start | bytes 1179656 | tf_op jit(solution)/shard_map/ppermute | solution.py:624
  166.1 28.9 %collective-permute-start.22 = (bf16[4,384,128]{2,1,0:T(8,128)(2,1)S(1)}, bf16[4,384,128]{2,1,0:T(8,128)(2,1)}, u32[]{:S(2)}, u32[]{:S(2)}) collective-permute-start(bf16[4,384,128]{2,1,0:T(8,128)(2,1)S(1)} %get-tuple-element.17), channel_id=1, source_target_pairs={{0,24},{2,26},{4,28},{6,30},{8,0},{10,2},{12,4},{14,6},{16,8},{18,... | collective-permute-start | bytes 1179656 | tf_op jit(solution)/shard_map/ppermute | solution.py:624
  175.7 19.3 %copy-start.15 = (bf16[4,384,128]{2,1,0:T(8,128)(2,1)}, bf16[4,384,128]{2,1,0:T(8,128)(2,1)S(1)}, u32[]{:S(2)}) copy-start(bf16[4,384,128]{2,1,0:T(8,128)(2,1)S(1)} %collective-permute-done.20.refs_1_.refs_2_) | copy-start | bytes 1179652
  196.8 71.0 %all-to-all-start.2 = ((bf16[16,2,384,128]{3,2,1,0:T(8,128)(2,1)}), bf16[16,2,384,128]{3,2,1,0:T(8,128)(2,1)S(1)}, u32[]{:S(2)}, u32[]{:S(2)}) async-start(bf16[16,2,384,128]{3,2,1,0:T(8,128)(2,1)} %after.11), calls=%async_computation.2 | async-start | bytes 6291456 | tf_op jit(solution)/shard_map/all_to_all | solution.py:629
  (11 other events, 26.7 us)

commit v5 on v4

--- a/solution.py
+++ b/solution.py
@@ -116,15 +116,17 @@
     return jnp.dot(rows_ref[...], jnp.concatenate(wide, axis=1), preferred_element_type=F32)
 
 
-def product_and_back(forward, spectrum_ref, rows_back_ref, coarse_back_ref, work_ref, rest_ref, first):
+def product_and_back(forward, spectrum_refs, rows_back_ref, coarse_back_ref, work_ref, rest_ref, first):
     _, _, tok_rows, channels = work_ref.shape
     groups = tok_rows // TIME_TILE
     for chunk in range(0, FREQ_CHUNK, PRODUCT_CHUNK):
         products = []
         for at in range(chunk, chunk + PRODUCT_CHUNK):
             real, imag = forward(at)
-            spec_real = spectrum_ref[at, 0].astype(F32)
-            spec_imag = spectrum_ref[at, 1].astype(F32)
+            spec_real, spec_imag = (
+                jnp.concatenate([ref[at, part].astype(F32) for ref in spectrum_refs], axis=0)
+                for part in range(2)
+            )
             products.append(
                 jnp.concatenate(
                     [
@@ -156,11 +158,13 @@
     tile = TIME_TILE
     depth = freq_count * 2 * tile
 
-    @pl.loop(0, tok_rows // tile // 2)
-    def _(pair):
+    width = max(w for w in (1, 2, 4, 8) if tok_rows // tile % w == 0)
+
+    @pl.loop(0, tok_rows // tile // width)
+    def _(turn):
         highs, lows = [], []
-        for half in range(2):
-            start = pl.multiple_of((2 * pair + half) * tile, tile)
+        for at in range(width):
+            start = pl.multiple_of((width * turn + at) * tile, tile)
             highs.append(work_ref[:, :, pl.ds(start, tile), :].reshape(depth, channels))
             lows.append(rest_ref[:, :, pl.ds(start, tile), :].reshape(depth, channels))
         high = jnp.concatenate(highs, axis=1)
@@ -168,9 +172,9 @@
         total = jnp.dot(high_ref[...], high, preferred_element_type=F32)
         total += jnp.dot(low_ref[...], high, preferred_element_type=F32)
         total += jnp.dot(high_ref[...], low, preferred_element_type=F32)
-        for half in range(2):
-            start = pl.multiple_of((2 * pair + half) * tile, tile)
-            lanes = slice(half * channels, (half + 1) * channels)
+        for at in range(width):
+            start = pl.multiple_of((width * turn + at) * tile, tile)
+            lanes = slice(at * channels, (at + 1) * channels)
             value = total[:, lanes].reshape(slab_count, tile, channels)
             for other in others:
                 value += other[:, pl.ds(start, tile), :]
@@ -203,7 +207,7 @@
         lanes = slice(at * channels, (at + 1) * channels)
         return transformed[:tok_rows, lanes], transformed[tok_rows:, lanes]
 
-    product_and_back(forward, spectrum_ref, rows_back_ref, coarse_back_ref, work_ref, rest_ref, first)
+    product_and_back(forward, [spectrum_ref], rows_back_ref, coarse_back_ref, work_ref, rest_ref, first)
 
     @pl.when(step == pl.num_programs(0) - 1)
     def _():
@@ -228,25 +232,16 @@
         out_ref[at, 1] = transformed[tok_rows:, lanes]
 
 
-def inverse_kernel(
-    coarse_back_ref,
-    forward_ref,
-    spectrum_ref,
-    back_high_ref,
-    back_low_ref,
-    rows_back_ref,
-    other_ref,
-    out_ref,
-    work_ref,
-    rest_ref,
-):
+def inverse_kernel(coarse_back_ref, forward_ref, *refs):
+    *spectrum_refs, back_high_ref, back_low_ref, rows_back_ref, other_ref = refs[:-3]
+    out_ref, work_ref, rest_ref = refs[-3:]
     step = pl.program_id(0)
 
     def forward(at):
         return forward_ref[at, 0], forward_ref[at, 1]
 
     product_and_back(
-        forward, spectrum_ref, rows_back_ref, coarse_back_ref, work_ref, rest_ref, step * FREQ_CHUNK
+        forward, spectrum_refs, rows_back_ref, coarse_back_ref, work_ref, rest_ref, step * FREQ_CHUNK
     )
 
     @pl.when(step == pl.num_programs(0) - 1)
@@ -346,7 +341,7 @@
         [
             (table["coarse_back"], "scalar"),
             (forward, "blocked"),
-            (spectra[-1], "blocked"),
+            *[(part, "blocked") for part in spectra[-1]],
             *[(t, "whole") for t in table["slab_back"]],
             (table["rows_back"], "whole"),
             (total, "whole"),
@@ -358,35 +353,36 @@
     )
 
 
-def spread_kernel(lines, channels, values_ref, out_ref):
-    for line in range(lines):
-        out_ref[line, 0, 0] = values_ref[0, 0, :, line * channels : (line + 1) * channels].astype(BF16)
-
-
-def spread_spectrum(filter_spec, at, plane, lines):
-    parts, _, tok_rows, group_channels = filter_spec.shape
+def spread_kernel(plane, lines, channels, values_ref, out_ref):
+    for at in range(plane):
+        for line in range(lines):
+            first = (at * lines + line) * channels
+            out_ref[line, at, 0] = values_ref[0, 0, :, first : first + channels].astype(BF16)
+
+
+def spread_spectrum(filter_spec, at, first, rows, plane, lines):
+    parts, _, _, group_channels = filter_spec.shape
     channels = group_channels // (plane * lines)
     if channels % 128:
-        spec = filter_spec[:, at].reshape(parts, tok_rows, plane, lines, channels)
-        spec = spec.transpose(3, 2, 0, 1, 4).astype(BF16)
-    else:
-        spec = pl.pallas_call(
-            functools.partial(spread_kernel, lines, channels),
-            grid=(parts, plane),
-            in_specs=[
-                pl.BlockSpec((1, 1, tok_rows, lines * channels), lambda i, j: (i, at, 0, j))
-            ],
-            out_specs=pl.BlockSpec((lines, 1, 1, tok_rows, channels), lambda i, j: (0, j, i, 0, 0)),
-            out_shape=jax.ShapeDtypeStruct((lines, plane, parts, tok_rows, channels), BF16),
-            compiler_params=pltpu.CompilerParams(
-                dimension_semantics=("arbitrary", "arbitrary"), vmem_limit_bytes=VMEM_LIMIT
-            ),
-            cost_estimate=pl.CostEstimate(
-                flops=0, bytes_accessed=6 * parts * tok_rows * group_channels, transcendentals=0
-            ),
-            name="spread_spectrum",
-        )(filter_spec)
-    return spec.reshape(plane * lines, parts, tok_rows, channels)
+        spec = filter_spec[:, at, first : first + rows].reshape(parts, rows, plane, lines, channels)
+        return spec.transpose(3, 2, 0, 1, 4).astype(BF16)
+    block = max(r for r in range(16, 97, 16) if rows % r == 0 and first % r == 0)
+    return pl.pallas_call(
+        functools.partial(spread_kernel, plane, lines, channels),
+        grid=(parts, rows // block),
+        in_specs=[
+            pl.BlockSpec((1, 1, block, group_channels), lambda i, j: (i, at, first // block + j, 0))
+        ],
+        out_specs=pl.BlockSpec((lines, plane, 1, block, channels), lambda i, j: (0, 0, i, j, 0)),
+        out_shape=jax.ShapeDtypeStruct((lines, plane, parts, rows, channels), BF16),
+        compiler_params=pltpu.CompilerParams(
+            dimension_semantics=("arbitrary", "arbitrary"), vmem_limit_bytes=VMEM_LIMIT
+        ),
+        cost_estimate=pl.CostEstimate(
+            flops=0, bytes_accessed=6 * parts * rows * group_channels, transcendentals=0
+        ),
+        name="spread_spectrum",
+    )(filter_spec)
 
 
 def gate_kernel(lines, channels, values_ref, gate_ref, out_ref):
@@ -563,9 +559,20 @@
     def other_core(value, e):
         return lax.ppermute(value, "ch", [(i, (i + e) % ch_size) for i in range(ch_size)])
 
+    def line_shift(value, k):
+        return lax.ppermute(value, "ctx", [(i, (i + k * plane) % ctx_size) for i in range(ctx_size)])
+
+    early_rows = tok_rows // 4 // 16 * 16
+    early = spread_spectrum(filter_spec, freq_local - 1, 0, early_rows, plane, lines)
+    early = [
+        lax.dynamic_index_in_dim(early, jnp.mod(line_at + k, lines), 0, keepdims=False)
+        for k in range(lines)
+    ]
+    early = [line_shift(piece, k) if k else piece for k, piece in enumerate(early)]
+
     weight = proj_weight.reshape(weight_rows, plane, wide).transpose(1, 0, 2)
     weight = lax.all_to_all(weight, "ctx", 0, 0, tiled=True, axis_index_groups=plane_groups)
-    along = [weight]
+    along = list(tie([weight], early[1:]))
 
     halves = jnp.split(features, 2, axis=1)
     held = [{0: half} for half in halves]
@@ -595,7 +602,12 @@
     gates = [
         lax.dynamic_index_in_dim(gate_blocks, plane_at ^ d, 1, keepdims=False) for d in range(plane)
     ]
-    spread = [spread_spectrum(filter_spec, at, plane, lines) for at in range(freq_local)]
+    skipped = [0] * (freq_local - 1) + [early_rows]
+    spread = [
+        spread_spectrum(filter_spec, at, skip, tok_rows - skip, plane, lines)
+        for at, skip in enumerate(skipped)
+    ]
+    spread = [spec.reshape((ctx_size,) + spec.shape[2:]) for spec in spread]
     beside = []
     for step in range(max(lines - 1, len(rounds))):
         if step < lines - 1:
@@ -620,17 +632,26 @@
         projected = project_fused(place, along, pieces, gates)
     else:
         projected = project_plain(place, along, pieces, gates)
-    signals = [projected[0]] + [
-        lax.ppermute(projected[k], "ctx", [(i, (i + k * plane) % ctx_size) for i in range(ctx_size)])
-        for k in range(1, lines)
+    signals = [projected[0]] + [line_shift(projected[k], k) for k in range(1, lines)]
+
+    early = [
+        jnp.stack([lax.dynamic_index_in_dim(piece, plane_at ^ d, 0, keepdims=False) for piece in early])
+        for d in range(plane)
     ]
+    early = tie(early, signals[1:])
+    early = jnp.stack([swap(piece, d) if d else piece for d, piece in enumerate(early)])
+    from_plane = (jnp.arange(plane) ^ plane_at)[None, :]
+    early = early[from_plane, jnp.mod(line_at - jnp.arange(lines), lines)[:, None]]
+    early = early.reshape((ctx_size,) + early.shape[2:])
     for at in range(1, freq_local):
         later = tie(spread[at : at + 1], spectra[-1:] + signals[1:])
         spectra.append(lax.all_to_all(later[0], "ctx", 0, 0, tiled=True))
 
+    spectra[-1] = [early, spectra[-1]]
     if channels % 128 == 0:
         convolved = convolve_fused(place, signals, spectra, tables)
     else:
+        spectra[-1] = jnp.concatenate(spectra[-1], axis=2)
         spectrum = jnp.stack(spectra, 1).reshape(ctx_size * freq_local, 2, tok_rows, channels)
         signal = jnp.stack(signals)[jnp.mod(line_at - jnp.arange(lines), lines)]
         convolved = convolve_plain(signal.reshape(ctx_size, tok_rows, channels), spectrum)

time: 340 us -> 337 us (level)
  blocking collectives: 70.4 us -> 45.2 us
  starting transfers between devices: 36 us -> 59.1 us
  waiting for transfers between devices: 133 us -> 126 us
  local copies, waits for them, and re-layouts: 21.5 us -> 28.1 us
    all_to_all x1, waiting for transfers between devices: 28.1 us -> 0.01 us  [per_device(): spectra.append(lax.all_to_all(later[0], 'ctx', 0, 0, tiled=True))]
    all_to_all x1 -> x0, blocking collectives: 19.2 us -> none  [per_device(): lax.all_to_all(weight, 'ctx', 0, 0, tiled=True, axis_index_groups=plane_g...]
    ppermute x9 -> x12, waiting for transfers between devices: 61.5 us -> 75 us  [swap(): return lax.ppermute(value, 'ctx', perm)]
    ppermute x3 -> x6, waiting for transfers between devices: 25.8 us -> 39.3 us  [line_shift(): lax.ppermute(value, 'ctx', [(i, (i + k * plane) % ctx_size) for i in rang...]
    ppermute x9 -> x12, starting transfers between devices: 10.3 us -> 17.8 us  [swap(): return lax.ppermute(value, 'ctx', perm)]
    all_to_all x1, blocking collectives: 51.2 us -> 45.2 us  [per_device(): returned = lax.all_to_all(convolved, 'ctx', 0, 0, tiled=True)]
    ppermute x3, waiting for transfers between devices: 12.6 us -> 6.93 us  [per_device(): along.append(lax.ppermute(along[-1], 'ctx', onward))]
    ppermute x3, starting transfers between devices: 1.58 us -> 6.95 us  [per_device(): along.append(lax.ppermute(along[-1], 'ctx', onward))]
  transfers between devices with their start and end apart: 25 -> 32, of which waited for: 18 -> 20; matrix products, arithmetic and copies ran while one was open for 4% -> 6% of each run, Pallas kernels for 18% -> 17%
where the time goes in v5:
time: 337 us; the launch traced here: 336 us
  waiting for transfers between devices  126 us (37%)
  Pallas kernels  75.3 us (22%)
  starting transfers between devices  59.1 us (18%)
  blocking collectives  45.2 us (13%)
  local copies, waits for them, and re-layouts  28.1 us (8%)
    ppermute x12, waiting for transfers between devices, swap(): return lax.ppermute(value, 'ctx', perm)  75 us
    all_to_all x1, blocking collectives, per_device(): returned = lax.all_to_all(convolved, 'ctx', 0, 0, tiled=True)  45.2 us
    pallas_call x3, Pallas kernels, frequency_call(): pl.pallas_call(kernel, grid=(freq_count // FREQ_CHUNK,), in_specs=specs,...  42.3 us
    ppermute x6, waiting for transfers between devices, line_shift(): lax.ppermute(value, 'ctx', [(i, (i + k * plane) % ctx_size) for i in rang...  39.3 us
    ppermute x12, starting transfers between devices, swap(): return lax.ppermute(value, 'ctx', perm)  17.8 us
    pallas_call x3, Pallas kernels, spread_spectrum(): pl.pallas_call(functools.partial(spread_kernel, plane, lines, channels),...  14.6 us
    pallas_call x1, Pallas kernels, project_fused(): pl.pallas_call(functools.partial(project_kernel, lines, plane), in_specs=...  14.3 us
    unnamed x51, local copies, waits for them, and re-layouts  12.6 us
  transfers between devices with their start and end apart: 32, of which 20 were waited for; matrix products, arithmetic and copies ran while one was open for 6% of the time, Pallas kernels for 17%

profile of v5, /device:TPU:0, one launch (start us, length us, event | category | flops | bytes accessed | tf_op | source)
XLA Modules:
  0.0 336.0 jit_solution(1494564508364150779)
XLA Ops:
  2.8 5.2 %all-to-all-start = ((bf16[4,256,512]{2,1,0:T(8,128)(2,1)}), bf16[4,256,512]{2,1,0:T(8,128)(2,1)S(1)}, u32[]{:S(2)}, u32[]{:S(2)}) async-start(bf16[4,256,512]{2,1,0:T(8,128)(2,1)} %bitcast.4), calls=%async_computation | async-start | bytes 2097152 | tf_op jit(solution)/shard_map/all_to_all | solution.py:574
  8.0 2.2 spread_spectrum.3
  12.9 2.6 collective-permute-start.1
  16.9 4.2 %collective-permute-done.refs_1_ = bf16[4,2,96,128]{3,2,1,0:T(8,128)(2,1)S(1)} collective-permute-done((bf16[4,2,96,128]{3,2,1,0:T(8,128)(2,1)S(1)}, bf16[4,2,96,128]{3,2,1,0:T(8,128)(2,1)S(1)}, u32[]{:S(2)}, u32[]{:S(2)}) %collective-permute-start) | collective-permute-done | bytes 196640 | tf_op jit(solution)/shard_map/ppermute | solution.py:563
  21.0 7.2 %collective-permute-done.1.refs_2_ = bf16[4,2,96,128]{3,2,1,0:T(8,128)(2,1)S(1)} collective-permute-done((bf16[4,2,96,128]{3,2,1,0:T(8,128)(2,1)S(1)}, bf16[4,2,96,128]{3,2,1,0:T(8,128)(2,1)S(1)}, u32[]{:S(2)}, u32[]{:S(2)}) %collective-permute-start.1) | collective-permute-done | bytes 196640 | tf_op jit(solution)/shard_map/ppermute | solution.py:563
  30.1 4.6 %collective-permute-start.3 = (bf16[4,256,512]{2,1,0:T(8,128)(2,1)}, bf16[4,256,512]{2,1,0:T(8,128)(2,1)S(1)}, u32[]{:S(2)}, u32[]{:S(2)}) collective-permute-start(bf16[4,256,512]{2,1,0:T(8,128)(2,1)} %after.8.refs_0_), channel_id=1, source_target_pairs={{0,8},{2,10},{4,12},{6,14},{8,16},{10,18},{12,20},{14,22},{16,24},... | collective-permute-start | bytes 3145736 | tf_op jit(solution)/shard_map/ppermute | solution.py:615
  39.3 6.9 %spread_spectrum.4 = bf16[4,4,2,384,128]{4,3,2,1,0:T(8,128)(2,1)} custom-call(f32[2,2,384,2048]{3,2,1,0:T(8,128)} %values_ref.5), custom_call_target="tpu_custom_call" | custom-call | bytes 9437184 | tf_op jit(solution)/shard_map/spread_spectrum/pallas_call | solution.py:370
  46.2 9.2 %collective-permute-done.4.refs_1_.refs_2_ = bf16[384,1024]{1,0:T(8,128)(2,1)S(1)} collective-permute-done((bf16[384,1024]{1,0:T(8,128)(2,1)S(1)}, bf16[384,1024]{1,0:T(8,128)(2,1)S(1)}, u32[]{:S(2)}, u32[]{:S(2)}) %collective-permute-start.4) | collective-permute-done | bytes 786464 | tf_op jit(solution)/shard_map/ppermute | solution.py:557
  59.2 1.8 collective-permute-start.6
  61.0 2.1 copy.57.refs_0_
  67.0 5.6 %spread_spectrum.5 = bf16[4,4,2,288,128]{4,3,2,1,0:T(8,128)(2,1)} custom-call(f32[2,2,384,2048]{3,2,1,0:T(8,128)} %values_ref.5), custom_call_target="tpu_custom_call" | custom-call | bytes 7077888 | tf_op jit(solution)/shard_map/spread_spectrum/pallas_call | solution.py:370
  73.8 3.3 constant_dynamic-slice_fusion.12
  79.4 3.2 collective-permute-done.7.refs_1_.refs_10_
  89.2 14.3 %collective-permute-done.10.refs_7_.refs_3_ = bf16[384,1024]{1,0:T(8,128)(2,1)S(1)} collective-permute-done((bf16[384,1024]{1,0:T(8,128)(2,1)S(1)}, bf16[384,1024]{1,0:T(8,128)(2,1)S(1)}, u32[]{:S(2)}, u32[]{:S(2)}) %collective-permute-start.10) | collective-permute-done | bytes 786464 | tf_op jit(solution)/shard_map/ppermute | solution.py:557
  105.2 4.5 %collective-permute-done.9.refs_4_.refs_3_.refs_1_ = bf16[4,256,512]{2,1,0:T(8,128)(2,1)S(1)} collective-permute-done((bf16[4,256,512]{2,1,0:T(8,128)(2,1)}, bf16[4,256,512]{2,1,0:T(8,128)(2,1)S(1)}, u32[]{:S(2)}, u32[]{:S(2)}) %collective-permute-start.9) | collective-permute-done | bytes 1048608 | tf_op jit(solution)/shard_map/ppermute | solution.py:615
  110.7 4.3 %all-to-all-start.1 = ((bf16[16,2,384,128]{3,2,1,0:T(8,128)(2,1)}), bf16[16,2,384,128]{3,2,1,0:T(8,128)(2,1)S(1)}, u32[]{:S(2)}, u32[]{:S(2)}) async-start(bf16[16,2,384,128]{3,2,1,0:T(8,128)(2,1)} %after.14), calls=%async_computation.1 | async-start | bytes 6291456 | tf_op jit(solution)/shard_map/all_to_all | solution.py:623
  121.1 1.9 collective-permute-start.20
  126.7 6.6 %collective-permute-done.20.refs_21_ = bf16[384,512]{1,0:T(8,128)(2,1)S(1)} collective-permute-done((bf16[384,512]{1,0:T(8,128)(2,1)}, bf16[384,512]{1,0:T(8,128)(2,1)S(1)}, u32[]{:S(2)}, u32[]{:S(2)}) %collective-permute-start.20) | collective-permute-done | bytes 393248 | tf_op jit(solution)/shard_map/ppermute | solution.py:557
  133.2 26.9 %collective-permute-done.21.refs_22_ = bf16[384,512]{1,0:T(8,128)(2,1)} collective-permute-done((bf16[384,512]{1,0:T(8,128)(2,1)}, bf16[384,512]{1,0:T(8,128)(2,1)}, u32[]{:S(2)}, u32[]{:S(2)}) %collective-permute-start.21) | collective-permute-done | bytes 393248 | tf_op jit(solution)/shard_map/ppermute | solution.py:557
  160.1 14.3 %project.1 = bf16[4,4,384,128]{3,2,1,0:T(8,128)(2,1)} custom-call(s32[3]{0:T(128)} %pad_add_fusion.place_ref, bf16[4,256,512]{2,1,0:T(8,128)(2,1)} %after.8.refs_0_, bf16[4,256,512]{2,1,0:T(8,128)(2,1)} %after.9.refs_5_.refs_1_, bf16[4,256,512]{2,1,0:T(8,128)(2,1)} %after.11.refs_2_, bf16[4,256,512]{2,1,0:T(8,128)(2,1)} %copy-done.4, ...), custom_call_target="tpu_custom_call" | custom-call | flops 6442450944 | bytes 18350080 | tf_op jit(solution)/shard_map/project/pallas_call | solution.py:486
  174.4 2.3 slice_bitcast_fusion
  176.7 3.2 collective-permute-start.23
  182.3 8.3 %collective-permute-done.23.refs_1_.refs_4_.refs_2_ = bf16[4,384,128]{2,1,0:T(8,128)(2,1)S(1)} collective-permute-done((bf16[4,384,128]{2,1,0:T(8,128)(2,1)S(1)}, bf16[4,384,128]{2,1,0:T(8,128)(2,1)S(1)}, u32[]{:S(2)}, u32[]{:S(2)}) %collective-permute-start.23) | collective-permute-done | bytes 393248 | tf_op jit(solution)/shard_map/ppermute | solution.py:563
  190.6 19.5 %collective-permute-done.24.refs_2_.refs_5_.refs_3_ = bf16[4,384,128]{2,1,0:T(8,128)(2,1)S(1)} collective-permute-done((bf16[4,384,128]{2,1,0:T(8,128)(2,1)S(1)}, bf16[4,384,128]{2,1,0:T(8,128)(2,1)S(1)}, u32[]{:S(2)}, u32[]{:S(2)}) %collective-permute-start.24) | collective-permute-done | bytes 393248 | tf_op jit(solution)/shard_map/ppermute | solution.py:563
  212.5 12.1 %all-to-all-start.2 = ((bf16[16,2,288,128]{3,2,1,0:T(8,128)(2,1)}), bf16[16,2,288,128]{3,2,1,0:T(8,128)(2,1)S(1)}, u32[]{:S(2)}, u32[]{:S(2)}) async-start(bf16[16,2,288,128]{3,2,1,0:T(8,128)(2,1)} %after.15), calls=%async_computation.2 | async-start | bytes 4718592 | tf_op jit(solution)/shard_map/all_to_all | solution.py:648
  227.5 1.9 collective-permute-start.26
  231.0 10.4 %forward.1.forward_ref = f32[16,2,384,128]{3,2,1,0:T(8,128)} custom-call(s32[3]{0:T(128)} %pad_add_fusion.place_ref, f32[768]{0:T(1024)} %constant.251.clone.coarse_ref, bf16[4,384,128]{2,1,0:T(8,128)(2,1)} %get-tuple-element.28.refs_0_, bf16[4,384,128]{2,1,0:T(8,128)(2,1)} %copy-done.9, bf16[4,384,128]{2,1,0:T(8,128)(2,1)} %copy-done.10, ...), custom_call_target="tpu_custom_call" | custom-call | flops 4026531840 | bytes 3279884 | tf_op jit(solution)/shard_map/forward/pallas_call | solution.py:270
  241.4 10.5 %collective-permute-done.27 = bf16[4,2,96,128]{3,2,1,0:T(8,128)(2,1)S(1)} collective-permute-done((bf16[4,2,96,128]{3,2,1,0:T(8,128)(2,1)}, bf16[4,2,96,128]{3,2,1,0:T(8,128)(2,1)S(1)}, u32[]{:S(2)}, u32[]{:S(2)}) %collective-permute-start.27) | collective-permute-done | bytes 196640 | tf_op jit(solution)/shard_map/ppermute | solution.py:557
  253.5 19.2 %convolve.1.refs_5_ = f32[16,384,128]{2,1,0:T(8,128)} custom-call(s32[3]{0:T(128)} %pad_add_fusion.place_ref, f32[768]{0:T(1024)} %constant.243.clone.coarse_ref, f32[768]{0:T(1024)} %constant.244.clone.coarse_back_ref, bf16[4,384,128]{2,1,0:T(8,128)(2,1)} %get-tuple-element.28.refs_0_, bf16[4,384,128]{2,1,0:T(8,128)(2,1)} %copy-done.9, ...), custom_call_target="tpu_custom_call" | custom-call | flops 8858370048 | bytes 8132620 | tf_op jit(solution)/shard_map/convolve/pallas_call | solution.py:270
  274.1 12.8 %inverse.1 = bf16[16,384,128]{2,1,0:T(8,128)(2,1)} custom-call(f32[768]{0:T(1024)} %constant.254.clone.coarse_back_ref, f32[16,2,384,128]{3,2,1,0:T(8,128)} %forward.1.forward_ref, bf16[16,2,96,128]{3,2,1,0:T(8,128)(2,1)} %gather_fusion, bf16[16,2,288,128]{3,2,1,0:T(8,128)(2,1)} %copy-done.7, bf16[256,512]{1,0:T(8,128)(2,1)} %constant.255.clone.refs_2_, ...), custom_call_target="tpu_custom_call" | custom-call | flops 4831838208 | bytes 14289920 | tf_op jit(solution)/shard_map/inverse/pallas_call | solution.py:270
  286.8 45.2 %all_to_all.20 = bf16[16,384,128]{2,1,0:T(8,128)(2,1)} all-to-all(bf16[16,384,128]{2,1,0:T(8,128)(2,1)} %inverse.1), channel_id=1, replica_groups=mesh['ctx'=16,'ch'=2] {'ctx'}, dimensions={0} | all-to-all | bytes 3145728 | tf_op jit(solution)/shard_map/all_to_all | solution.py:658
  332.0 4.0 %gate_output.1 = bf16[384,2048]{1,0:T(8,128)(2,1)} custom-call(bf16[4,4,384,128]{3,2,1,0:T(8,128)(2,1)} %bitcast.49, bf16[384,2048]{1,0:T(8,128)(2,1)} %gate_ref.1), custom_call_target="tpu_custom_call" | custom-call | flops 786432 | bytes 4718592 | tf_op jit(solution)/shard_map/gate_output/pallas_call | solution.py:402
  (120 shorter events, 55.7 us)
Async XLA Ops:
  2.8 25.5 %all-to-all-start = ((bf16[4,256,512]{2,1,0:T(8,128)(2,1)}), bf16[4,256,512]{2,1,0:T(8,128)(2,1)S(1)}, u32[]{:S(2)}, u32[]{:S(2)}) async-start(bf16[4,256,512]{2,1,0:T(8,128)(2,1)} %bitcast.4), calls=%async_computation | async-start | bytes 2097152 | tf_op jit(solution)/shard_map/all_to_all | solution.py:574
  11.3 9.7 %collective-permute-start = (bf16[4,2,96,128]{3,2,1,0:T(8,128)(2,1)S(1)}, bf16[4,2,96,128]{3,2,1,0:T(8,128)(2,1)S(1)}, u32[]{:S(2)}, u32[]{:S(2)}) collective-permute-start(bf16[4,2,96,128]{3,2,1,0:T(8,128)(2,1)S(1)} %get-tuple-element.41), channel_id=1, source_target_pairs={{0,8},{2,10},{4,12},{6,14},{8,16},{10,18},{12,20},{14,22},{16,24},... | collective-permute-start | bytes 589832 | tf_op jit(solution)/shard_map/ppermute | solution.py:563
  12.9 15.3 %collective-permute-start.1 = (bf16[4,2,96,128]{3,2,1,0:T(8,128)(2,1)S(1)}, bf16[4,2,96,128]{3,2,1,0:T(8,128)(2,1)S(1)}, u32[]{:S(2)}, u32[]{:S(2)}) collective-permute-start(bf16[4,2,96,128]{3,2,1,0:T(8,128)(2,1)S(1)} %get-tuple-element.40), channel_id=1, source_target_pairs={{0,16},{2,18},{4,20},{6,22},{8,24},{10,26},{12,28},{14,30},{16,0},... | collective-permute-start | bytes 589832 | tf_op jit(solution)/shard_map/ppermute | solution.py:563
  15.5 12.8 %collective-permute-start.2 = (bf16[4,2,96,128]{3,2,1,0:T(8,128)(2,1)S(1)}, bf16[4,2,96,128]{3,2,1,0:T(8,128)(2,1)S(1)}, u32[]{:S(2)}, u32[]{:S(2)}) collective-permute-start(bf16[4,2,96,128]{3,2,1,0:T(8,128)(2,1)S(1)} %get-tuple-element.39), channel_id=1, source_target_pairs={{0,24},{2,26},{4,28},{6,30},{8,0},{10,2},{12,4},{14,6},{16,8},{18,... | collective-permute-start | bytes 589832 | tf_op jit(solution)/shard_map/ppermute | solution.py:563
  30.1 28.1 %collective-permute-start.3 = (bf16[4,256,512]{2,1,0:T(8,128)(2,1)}, bf16[4,256,512]{2,1,0:T(8,128)(2,1)S(1)}, u32[]{:S(2)}, u32[]{:S(2)}) collective-permute-start(bf16[4,256,512]{2,1,0:T(8,128)(2,1)} %after.8.refs_0_), channel_id=1, source_target_pairs={{0,8},{2,10},{4,12},{6,14},{8,16},{10,18},{12,20},{14,22},{16,24},... | collective-permute-start | bytes 3145736 | tf_op jit(solution)/shard_map/ppermute | solution.py:615
  36.2 19.2 %collective-permute-start.4 = (bf16[384,1024]{1,0:T(8,128)(2,1)S(1)}, bf16[384,1024]{1,0:T(8,128)(2,1)S(1)}, u32[]{:S(2)}, u32[]{:S(2)}) collective-permute-start(bf16[384,1024]{1,0:T(8,128)(2,1)S(1)} %get-tuple-element.34.refs_4_), channel_id=1, source_target_pairs={{0,2},{2,0},{4,6},{6,4},{8,10},{10,8},{12,14},{14,12},{16,18},{18,... | collective-permute-start | bytes 2359304 | tf_op jit(solution)/shard_map/ppermute | solution.py:557
  37.9 18.9 %collective-permute-start.5 = (bf16[384,1024]{1,0:T(8,128)(2,1)S(1)}, bf16[384,1024]{1,0:T(8,128)(2,1)S(1)}, u32[]{:S(2)}, u32[]{:S(2)}) collective-permute-start(bf16[384,1024]{1,0:T(8,128)(2,1)S(1)} %get-tuple-element.33.refs_5_), channel_id=1, source_target_pairs={{0,4},{2,6},{4,0},{6,2},{8,12},{10,14},{12,8},{14,10},{16,20},{18,... | collective-permute-start | bytes 2359304 | tf_op jit(solution)/shard_map/ppermute | solution.py:557
  59.2 25.7 %collective-permute-start.6 = (bf16[4,256,512]{2,1,0:T(8,128)(2,1)}, bf16[4,256,512]{2,1,0:T(8,128)(2,1)}, u32[]{:S(2)}, u32[]{:S(2)}) collective-permute-start(bf16[4,256,512]{2,1,0:T(8,128)(2,1)} %after.9.refs_5_.refs_1_), channel_id=1, source_target_pairs={{0,8},{2,10},{4,12},{6,14},{8,16},{10,18},{12,20},{14,22},{16,24},... | collective-permute-start | bytes 3145736 | tf_op jit(solution)/shard_map/ppermute | solution.py:615
  64.0 18.7 %collective-permute-start.7 = (bf16[384,1024]{1,0:T(8,128)(2,1)}, bf16[384,1024]{1,0:T(8,128)(2,1)}, u32[]{:S(2)}, u32[]{:S(2)}) collective-permute-start(bf16[384,1024]{1,0:T(8,128)(2,1)} %get-tuple-element.15.refs_6_), channel_id=1, source_target_pairs={{0,4},{2,6},{4,0},{6,2},{8,12},{10,14},{12,8},{14,10},{16,20},{18,... | collective-permute-start | bytes 2359304 | tf_op jit(solution)/shard_map/ppermute | solution.py:557
  65.6 18.4 %collective-permute-start.8 = (bf16[384,1024]{1,0:T(8,128)(2,1)}, bf16[384,1024]{1,0:T(8,128)(2,1)}, u32[]{:S(2)}, u32[]{:S(2)}) collective-permute-start(bf16[384,1024]{1,0:T(8,128)(2,1)} %get-tuple-element.16.refs_9_), channel_id=1, source_target_pairs={{0,2},{2,0},{4,6},{6,4},{8,10},{10,8},{12,14},{14,12},{16,18},{18,... | collective-permute-start | bytes 2359304 | tf_op jit(solution)/shard_map/ppermute | solution.py:557
  84.9 24.7 %collective-permute-start.9 = (bf16[4,256,512]{2,1,0:T(8,128)(2,1)}, bf16[4,256,512]{2,1,0:T(8,128)(2,1)S(1)}, u32[]{:S(2)}, u32[]{:S(2)}) collective-permute-start(bf16[4,256,512]{2,1,0:T(8,128)(2,1)} %after.11.refs_2_), channel_id=1, source_target_pairs={{0,8},{2,10},{4,12},{6,14},{8,16},{10,18},{12,20},{14,22},{16,24},... | collective-permute-start | bytes 3145736 | tf_op jit(solution)/shard_map/ppermute | solution.py:615
  86.1 17.4 %collective-permute-start.10 = (bf16[384,1024]{1,0:T(8,128)(2,1)S(1)}, bf16[384,1024]{1,0:T(8,128)(2,1)S(1)}, u32[]{:S(2)}, u32[]{:S(2)}) collective-permute-start(bf16[384,1024]{1,0:T(8,128)(2,1)S(1)} %copy-done.15), channel_id=1, source_target_pairs={{0,2},{2,0},{4,6},{6,4},{8,10},{10,8},{12,14},{14,12},{16,18},{18,... | collective-permute-start | bytes 2359304 | tf_op jit(solution)/shard_map/ppermute | solution.py:557
  87.7 17.5 %collective-permute-start.11 = (bf16[384,1024]{1,0:T(8,128)(2,1)}, bf16[384,1024]{1,0:T(8,128)(2,1)S(1)}, u32[]{:S(2)}, u32[]{:S(2)}) collective-permute-start(bf16[384,1024]{1,0:T(8,128)(2,1)} %copy-done.16), channel_id=1, source_target_pairs={{0,4},{2,6},{4,0},{6,2},{8,12},{10,14},{12,8},{14,10},{16,20},{18,... | collective-permute-start | bytes 2359304 | tf_op jit(solution)/shard_map/ppermute | solution.py:557
  110.7 100.2 %all-to-all-start.1 = ((bf16[16,2,384,128]{3,2,1,0:T(8,128)(2,1)}), bf16[16,2,384,128]{3,2,1,0:T(8,128)(2,1)S(1)}, u32[]{:S(2)}, u32[]{:S(2)}) async-start(bf16[16,2,384,128]{3,2,1,0:T(8,128)(2,1)} %after.14), calls=%async_computation.1 | async-start | bytes 6291456 | tf_op jit(solution)/shard_map/all_to_all | solution.py:623
  115.0 2.7 collective-permute-start.12
  115.1 3.7 %collective-permute-start.13 = (bf16[384,1024]{1,0:T(8,128)(2,1)}, bf16[384,1024]{1,0:T(8,128)(2,1)}, u32[]{:S(2)}, u32[]{:S(2)}) collective-permute-start(bf16[384,1024]{1,0:T(8,128)(2,1)} %copy-done.14), channel_id=1, source_target_pairs={{0,1},{1,0},{2,3},{3,2},{4,5},{5,4},{6,7},{7,6},{8,9},{9,8},{10,11... | collective-permute-start | bytes 2359304 | tf_op jit(solution)/shard_map/ppermute | solution.py:560
  115.6 4.4 %collective-permute-start.15 = (bf16[384,1024]{1,0:T(8,128)(2,1)}, bf16[384,1024]{1,0:T(8,128)(2,1)}, u32[]{:S(2)}, u32[]{:S(2)}) collective-permute-start(bf16[384,1024]{1,0:T(8,128)(2,1)} %copy-done.12), channel_id=1, source_target_pairs={{0,1},{1,0},{2,3},{3,2},{4,5},{5,4},{6,7},{7,6},{8,9},{9,8},{10,11... | collective-permute-start | bytes 2359304 | tf_op jit(solution)/shard_map/ppermute | solution.py:560
  115.6 5.4 %collective-permute-start.16 = (bf16[384,1024]{1,0:T(8,128)(2,1)}, bf16[384,1024]{1,0:T(8,128)(2,1)}, u32[]{:S(2)}, u32[]{:S(2)}) collective-permute-start(bf16[384,1024]{1,0:T(8,128)(2,1)} %copy-done.13), channel_id=1, source_target_pairs={{0,1},{1,0},{2,3},{3,2},{4,5},{5,4},{6,7},{7,6},{8,9},{9,8},{10,11... | collective-permute-start | bytes 2359304 | tf_op jit(solution)/shard_map/ppermute | solution.py:560
  116.1 6.8 %collective-permute-start.14 = (bf16[384,1024]{1,0:T(8,128)(2,1)}, bf16[384,1024]{1,0:T(8,128)(2,1)}, u32[]{:S(2)}, u32[]{:S(2)}) collective-permute-start(bf16[384,1024]{1,0:T(8,128)(2,1)} %get-tuple-element.15.refs_6_), channel_id=1, source_target_pairs={{0,1},{1,0},{2,3},{3,2},{4,5},{5,4},{6,7},{7,6},{8,9},{9,8},{10,11... | collective-permute-start | bytes 2359304 | tf_op jit(solution)/shard_map/ppermute | solution.py:560
  117.7 6.7 %collective-permute-start.17 = (bf16[384,1024]{1,0:T(8,128)(2,1)}, bf16[384,1024]{1,0:T(8,128)(2,1)}, u32[]{:S(2)}, u32[]{:S(2)}) collective-permute-start(bf16[384,1024]{1,0:T(8,128)(2,1)} %get-tuple-element.16.refs_9_), channel_id=1, source_target_pairs={{0,1},{1,0},{2,3},{3,2},{4,5},{5,4},{6,7},{7,6},{8,9},{9,8},{10,11... | collective-permute-start | bytes 2359304 | tf_op jit(solution)/shard_map/ppermute | solution.py:560
  118.8 7.8 %collective-permute-start.18 = (bf16[384,1024]{1,0:T(8,128)(2,1)}, bf16[384,1024]{1,0:T(8,128)(2,1)}, u32[]{:S(2)}, u32[]{:S(2)}) collective-permute-start(bf16[384,1024]{1,0:T(8,128)(2,1)} %collective-permute-done.7.refs_1_.refs_10_), channel_id=1, source_target_pairs={{0,1},{1,0},{2,3},{3,2},{4,5},{5,4},{6,7},{7,6},{8,9},{9,8},{10,11... | collective-permute-start | bytes 2359304 | tf_op jit(solution)/shard_map/ppermute | solution.py:560
  119.9 6.7 %collective-permute-start.19 = (bf16[384,1024]{1,0:T(8,128)(2,1)}, bf16[384,1024]{1,0:T(8,128)(2,1)}, u32[]{:S(2)}, u32[]{:S(2)}) collective-permute-start(bf16[384,1024]{1,0:T(8,128)(2,1)} %collective-permute-done.8.refs_2_.refs_11_), channel_id=1, source_target_pairs={{0,1},{1,0},{2,3},{3,2},{4,5},{5,4},{6,7},{7,6},{8,9},{9,8},{10,11... | collective-permute-start | bytes 2359304 | tf_op jit(solution)/shard_map/ppermute | solution.py:560
  121.1 12.2 %collective-permute-start.20 = (bf16[384,512]{1,0:T(8,128)(2,1)}, bf16[384,512]{1,0:T(8,128)(2,1)S(1)}, u32[]{:S(2)}, u32[]{:S(2)}) collective-permute-start(bf16[384,512]{1,0:T(8,128)(2,1)} %get-tuple-element.18), channel_id=1, source_target_pairs={{0,2},{2,0},{4,6},{6,4},{8,10},{10,8},{12,14},{14,12},{16,18},{18,... | collective-permute-start | bytes 1179656 | tf_op jit(solution)/shard_map/ppermute | solution.py:557
  122.9 37.1 %collective-permute-start.21 = (bf16[384,512]{1,0:T(8,128)(2,1)}, bf16[384,512]{1,0:T(8,128)(2,1)}, u32[]{:S(2)}, u32[]{:S(2)}) collective-permute-start(bf16[384,512]{1,0:T(8,128)(2,1)} %get-tuple-element.19), channel_id=1, source_target_pairs={{0,4},{2,6},{4,0},{6,2},{8,12},{10,14},{12,8},{14,10},{16,20},{18,... | collective-permute-start | bytes 1179656 | tf_op jit(solution)/shard_map/ppermute | solution.py:557
  124.4 35.7 %collective-permute-start.22 = (bf16[384,512]{1,0:T(8,128)(2,1)}, bf16[384,512]{1,0:T(8,128)(2,1)}, u32[]{:S(2)}, u32[]{:S(2)}) collective-permute-start(bf16[384,512]{1,0:T(8,128)(2,1)} %get-tuple-element.20), channel_id=1, source_target_pairs={{0,6},{2,4},{4,2},{6,0},{8,14},{10,12},{12,10},{14,8},{16,22},{18,... | collective-permute-start | bytes 1179656 | tf_op jit(solution)/shard_map/ppermute | solution.py:557
  176.7 13.9 %collective-permute-start.23 = (bf16[4,384,128]{2,1,0:T(8,128)(2,1)S(1)}, bf16[4,384,128]{2,1,0:T(8,128)(2,1)S(1)}, u32[]{:S(2)}, u32[]{:S(2)}) collective-permute-start(bf16[4,384,128]{2,1,0:T(8,128)(2,1)S(1)} %get-tuple-element.27), channel_id=1, source_target_pairs={{0,8},{2,10},{4,12},{6,14},{8,16},{10,18},{12,20},{14,22},{16,24},... | collective-permute-start | bytes 1179656 | tf_op jit(solution)/shard_map/ppermute | solution.py:563
  179.9 30.2 %collective-permute-start.24 = (bf16[4,384,128]{2,1,0:T(8,128)(2,1)S(1)}, bf16[4,384,128]{2,1,0:T(8,128)(2,1)S(1)}, u32[]{:S(2)}, u32[]{:S(2)}) collective-permute-start(bf16[4,384,128]{2,1,0:T(8,128)(2,1)S(1)} %get-tuple-element.26), channel_id=1, source_target_pairs={{0,16},{2,18},{4,20},{6,22},{8,24},{10,26},{12,28},{14,30},{16,0},... | collective-permute-start | bytes 1179656 | tf_op jit(solution)/shard_map/ppermute | solution.py:563
  180.6 30.3 %collective-permute-start.25 = (bf16[4,384,128]{2,1,0:T(8,128)(2,1)S(1)}, bf16[4,384,128]{2,1,0:T(8,128)(2,1)}, u32[]{:S(2)}, u32[]{:S(2)}) collective-permute-start(bf16[4,384,128]{2,1,0:T(8,128)(2,1)S(1)} %get-tuple-element.25), channel_id=1, source_target_pairs={{0,24},{2,26},{4,28},{6,30},{8,0},{10,2},{12,4},{14,6},{16,8},{18,... | collective-permute-start | bytes 1179656 | tf_op jit(solution)/shard_map/ppermute | solution.py:563
  212.5 60.1 %all-to-all-start.2 = ((bf16[16,2,288,128]{3,2,1,0:T(8,128)(2,1)}), bf16[16,2,288,128]{3,2,1,0:T(8,128)(2,1)S(1)}, u32[]{:S(2)}, u32[]{:S(2)}) async-start(bf16[16,2,288,128]{3,2,1,0:T(8,128)(2,1)} %after.15), calls=%async_computation.2 | async-start | bytes 4718592 | tf_op jit(solution)/shard_map/all_to_all | solution.py:648
  227.5 13.9 %collective-permute-start.26 = (bf16[4,2,96,128]{3,2,1,0:T(8,128)(2,1)}, bf16[4,2,96,128]{3,2,1,0:T(8,128)(2,1)S(1)}, u32[]{:S(2)}, u32[]{:S(2)}) collective-permute-start(bf16[4,2,96,128]{3,2,1,0:T(8,128)(2,1)} %get-tuple-element.22), channel_id=1, source_target_pairs={{0,2},{2,0},{4,6},{6,4},{8,10},{10,8},{12,14},{14,12},{16,18},{18,... | collective-permute-start | bytes 589832 | tf_op jit(solution)/shard_map/ppermute | solution.py:557
  229.3 22.5 %collective-permute-start.27 = (bf16[4,2,96,128]{3,2,1,0:T(8,128)(2,1)}, bf16[4,2,96,128]{3,2,1,0:T(8,128)(2,1)S(1)}, u32[]{:S(2)}, u32[]{:S(2)}) collective-permute-start(bf16[4,2,96,128]{3,2,1,0:T(8,128)(2,1)} %get-tuple-element.23), channel_id=1, source_target_pairs={{0,4},{2,6},{4,0},{6,2},{8,12},{10,14},{12,8},{14,10},{16,20},{18,... | collective-permute-start | bytes 589832 | tf_op jit(solution)/shard_map/ppermute | solution.py:557
  230.8 21.1 %collective-permute-start.28 = (bf16[4,2,96,128]{3,2,1,0:T(8,128)(2,1)}, bf16[4,2,96,128]{3,2,1,0:T(8,128)(2,1)S(1)}, u32[]{:S(2)}, u32[]{:S(2)}) collective-permute-start(bf16[4,2,96,128]{3,2,1,0:T(8,128)(2,1)} %get-tuple-element.24), channel_id=1, source_target_pairs={{0,6},{2,4},{4,2},{6,0},{8,14},{10,12},{12,10},{14,8},{16,22},{18,... | collective-permute-start | bytes 589832 | tf_op jit(solution)/shard_map/ppermute | solution.py:557
  (24 other events, 169.0 us)

commit v6 on v5

--- a/solution.py
+++ b/solution.py
@@ -282,7 +282,7 @@
     )(*arrays)
 
 
-def convolve_fused(place, pieces, spectra, tables):
+def convolve_fused(place, pieces, spectra, tables, early_rows):
     lines = len(pieces)
     plane, tok_rows, channels = pieces[0].shape
     slab_count = lines * plane
@@ -341,7 +341,8 @@
         [
             (table["coarse_back"], "scalar"),
             (forward, "blocked"),
-            *[(part, "blocked") for part in spectra[-1]],
+            (early_rows(total), "blocked"),
+            (spectra[-1], "blocked"),
             *[(t, "whole") for t in table["slab_back"]],
             (table["rows_back"], "whole"),
             (total, "whole"),
@@ -639,19 +640,22 @@
         for d in range(plane)
     ]
     early = tie(early, signals[1:])
-    early = jnp.stack([swap(piece, d) if d else piece for d, piece in enumerate(early)])
-    from_plane = (jnp.arange(plane) ^ plane_at)[None, :]
-    early = early[from_plane, jnp.mod(line_at - jnp.arange(lines), lines)[:, None]]
-    early = early.reshape((ctx_size,) + early.shape[2:])
+    early = [swap(piece, d) if d else piece for d, piece in enumerate(early)]
+
+    def early_spectrum(done):
+        stacked = jnp.stack(tie(early, [done]))
+        from_plane = (jnp.arange(plane) ^ plane_at)[None, :]
+        from_line = jnp.mod(line_at - jnp.arange(lines), lines)[:, None]
+        return stacked[from_plane, from_line].reshape((ctx_size,) + stacked.shape[2:])
+
     for at in range(1, freq_local):
         later = tie(spread[at : at + 1], spectra[-1:] + signals[1:])
         spectra.append(lax.all_to_all(later[0], "ctx", 0, 0, tiled=True))
 
-    spectra[-1] = [early, spectra[-1]]
     if channels % 128 == 0:
-        convolved = convolve_fused(place, signals, spectra, tables)
+        convolved = convolve_fused(place, signals, spectra, tables, early_spectrum)
     else:
-        spectra[-1] = jnp.concatenate(spectra[-1], axis=2)
+        spectra[-1] = jnp.concatenate([early_spectrum(None), spectra[-1]], axis=2)
         spectrum = jnp.stack(spectra, 1).reshape(ctx_size * freq_local, 2, tok_rows, channels)
         signal = jnp.stack(signals)[jnp.mod(line_at - jnp.arange(lines), lines)]
         convolved = convolve_plain(signal.reshape(ctx_size, tok_rows, channels), spectrum)

time: 337 us -> 337 us (level)
  waiting for transfers between devices: 126 us -> 121 us
    ppermute x12, waiting for transfers between devices: 75 us -> 64.5 us  [swap(): return lax.ppermute(value, 'ctx', perm)]
    all_to_all x1, waiting for transfers between devices: 0.01 us -> 5.87 us  [per_device(): spectra.append(lax.all_to_all(later[0], 'ctx', 0, 0, tiled=True))]
    unnamed x51 -> x55, local copies, waits for them, and re-layouts: 12.6 us -> 13.3 us
where the time goes in v6:
time: 337 us; the launch traced here: 336 us
  waiting for transfers between devices  121 us (36%)
  Pallas kernels  75.3 us (22%)
  starting transfers between devices  59 us (18%)
  blocking collectives  47.8 us (14%)
  local copies, waits for them, and re-layouts  28.8 us (9%)
  other arithmetic  3.59 us (1%)
    ppermute x12, waiting for transfers between devices, swap(): return lax.ppermute(value, 'ctx', perm)  64.5 us
    all_to_all x1, blocking collectives, per_device(): returned = lax.all_to_all(convolved, 'ctx', 0, 0, tiled=True)  47.8 us
    pallas_call x3, Pallas kernels, frequency_call(): pl.pallas_call(kernel, grid=(freq_count // FREQ_CHUNK,), in_specs=specs,...  42.3 us
    ppermute x6, waiting for transfers between devices, line_shift(): lax.ppermute(value, 'ctx', [(i, (i + k * plane) % ctx_size) for i in rang...  39.3 us
    ppermute x12, starting transfers between devices, swap(): return lax.ppermute(value, 'ctx', perm)  17.8 us
    pallas_call x3, Pallas kernels, spread_spectrum(): pl.pallas_call(functools.partial(spread_kernel, plane, lines, channels),...  14.7 us
    pallas_call x1, Pallas kernels, project_fused(): pl.pallas_call(functools.partial(project_kernel, lines, plane), in_specs=...  14.3 us
    unnamed x55, local copies, waits for them, and re-layouts  13.3 us
  transfers between devices with their start and end apart: 32, of which 20 were waited for; matrix products, arithmetic and copies ran while one was open for 6% of the time, Pallas kernels for 17%

profile of v6, /device:TPU:0, one launch (start us, length us, event | category | flops | bytes accessed | tf_op | source)
XLA Modules:
  0.0 336.0 jit_solution(7869179605531133226)
XLA Ops:
  2.8 5.2 %all-to-all-start = ((bf16[4,256,512]{2,1,0:T(8,128)(2,1)}), bf16[4,256,512]{2,1,0:T(8,128)(2,1)S(1)}, u32[]{:S(2)}, u32[]{:S(2)}) async-start(bf16[4,256,512]{2,1,0:T(8,128)(2,1)} %bitcast.4), calls=%async_computation | async-start | bytes 2097152 | tf_op jit(solution)/shard_map/all_to_all | solution.py:575
  8.0 2.2 spread_spectrum.3
  12.9 2.6 collective-permute-start.1
  16.9 4.2 %collective-permute-done.refs_1_ = bf16[4,2,96,128]{3,2,1,0:T(8,128)(2,1)S(1)} collective-permute-done((bf16[4,2,96,128]{3,2,1,0:T(8,128)(2,1)S(1)}, bf16[4,2,96,128]{3,2,1,0:T(8,128)(2,1)S(1)}, u32[]{:S(2)}, u32[]{:S(2)}) %collective-permute-start) | collective-permute-done | bytes 196640 | tf_op jit(solution)/shard_map/ppermute | solution.py:564
  21.1 7.2 %collective-permute-done.1.refs_2_ = bf16[4,2,96,128]{3,2,1,0:T(8,128)(2,1)S(1)} collective-permute-done((bf16[4,2,96,128]{3,2,1,0:T(8,128)(2,1)S(1)}, bf16[4,2,96,128]{3,2,1,0:T(8,128)(2,1)S(1)}, u32[]{:S(2)}, u32[]{:S(2)}) %collective-permute-start.1) | collective-permute-done | bytes 196640 | tf_op jit(solution)/shard_map/ppermute | solution.py:564
  30.1 4.6 %collective-permute-start.3 = (bf16[4,256,512]{2,1,0:T(8,128)(2,1)}, bf16[4,256,512]{2,1,0:T(8,128)(2,1)S(1)}, u32[]{:S(2)}, u32[]{:S(2)}) collective-permute-start(bf16[4,256,512]{2,1,0:T(8,128)(2,1)} %after.9.refs_0_), channel_id=1, source_target_pairs={{0,8},{2,10},{4,12},{6,14},{8,16},{10,18},{12,20},{14,22},{16,24},... | collective-permute-start | bytes 3145736 | tf_op jit(solution)/shard_map/ppermute | solution.py:616
  39.3 6.9 %spread_spectrum.4 = bf16[4,4,2,384,128]{4,3,2,1,0:T(8,128)(2,1)} custom-call(f32[2,2,384,2048]{3,2,1,0:T(8,128)} %values_ref.5), custom_call_target="tpu_custom_call" | custom-call | bytes 9437184 | tf_op jit(solution)/shard_map/spread_spectrum/pallas_call | solution.py:371
  46.3 9.2 %collective-permute-done.4.refs_1_.refs_2_ = bf16[384,1024]{1,0:T(8,128)(2,1)S(1)} collective-permute-done((bf16[384,1024]{1,0:T(8,128)(2,1)S(1)}, bf16[384,1024]{1,0:T(8,128)(2,1)S(1)}, u32[]{:S(2)}, u32[]{:S(2)}) %collective-permute-start.4) | collective-permute-done | bytes 786464 | tf_op jit(solution)/shard_map/ppermute | solution.py:558
  59.2 1.8 collective-permute-start.6
  61.0 2.1 copy.61.refs_0_
  67.0 5.6 %spread_spectrum.5 = bf16[4,4,2,288,128]{4,3,2,1,0:T(8,128)(2,1)} custom-call(f32[2,2,384,2048]{3,2,1,0:T(8,128)} %values_ref.5), custom_call_target="tpu_custom_call" | custom-call | bytes 7077888 | tf_op jit(solution)/shard_map/spread_spectrum/pallas_call | solution.py:371
  73.8 3.3 constant_dynamic-slice_fusion.12
  79.4 3.2 collective-permute-done.7.refs_1_.refs_10_
  89.2 14.3 %collective-permute-done.10.refs_7_.refs_3_ = bf16[384,1024]{1,0:T(8,128)(2,1)S(1)} collective-permute-done((bf16[384,1024]{1,0:T(8,128)(2,1)S(1)}, bf16[384,1024]{1,0:T(8,128)(2,1)S(1)}, u32[]{:S(2)}, u32[]{:S(2)}) %collective-permute-start.10) | collective-permute-done | bytes 786464 | tf_op jit(solution)/shard_map/ppermute | solution.py:558
  105.2 4.5 %collective-permute-done.9.refs_4_.refs_3_.refs_1_ = bf16[4,256,512]{2,1,0:T(8,128)(2,1)S(1)} collective-permute-done((bf16[4,256,512]{2,1,0:T(8,128)(2,1)}, bf16[4,256,512]{2,1,0:T(8,128)(2,1)S(1)}, u32[]{:S(2)}, u32[]{:S(2)}) %collective-permute-start.9) | collective-permute-done | bytes 1048608 | tf_op jit(solution)/shard_map/ppermute | solution.py:616
  110.7 4.3 %all-to-all-start.1 = ((bf16[16,2,384,128]{3,2,1,0:T(8,128)(2,1)}), bf16[16,2,384,128]{3,2,1,0:T(8,128)(2,1)S(1)}, u32[]{:S(2)}, u32[]{:S(2)}) async-start(bf16[16,2,384,128]{3,2,1,0:T(8,128)(2,1)} %after.15), calls=%async_computation.1 | async-start | bytes 6291456 | tf_op jit(solution)/shard_map/all_to_all | solution.py:624
  121.1 1.9 collective-permute-start.20
  126.7 6.5 %collective-permute-done.20.refs_21_ = bf16[384,512]{1,0:T(8,128)(2,1)S(1)} collective-permute-done((bf16[384,512]{1,0:T(8,128)(2,1)}, bf16[384,512]{1,0:T(8,128)(2,1)S(1)}, u32[]{:S(2)}, u32[]{:S(2)}) %collective-permute-start.20) | collective-permute-done | bytes 393248 | tf_op jit(solution)/shard_map/ppermute | solution.py:558
  133.2 26.9 %collective-permute-done.21.refs_22_ = bf16[384,512]{1,0:T(8,128)(2,1)} collective-permute-done((bf16[384,512]{1,0:T(8,128)(2,1)}, bf16[384,512]{1,0:T(8,128)(2,1)}, u32[]{:S(2)}, u32[]{:S(2)}) %collective-permute-start.21) | collective-permute-done | bytes 393248 | tf_op jit(solution)/shard_map/ppermute | solution.py:558
  160.1 14.3 %project.1 = bf16[4,4,384,128]{3,2,1,0:T(8,128)(2,1)} custom-call(s32[3]{0:T(128)} %pad_add_fusion.place_ref, bf16[4,256,512]{2,1,0:T(8,128)(2,1)} %after.9.refs_0_, bf16[4,256,512]{2,1,0:T(8,128)(2,1)} %after.10.refs_5_.refs_1_, bf16[4,256,512]{2,1,0:T(8,128)(2,1)} %after.12.refs_2_, bf16[4,256,512]{2,1,0:T(8,128)(2,1)} %copy-done.4, ...), custom_call_target="tpu_custom_call" | custom-call | flops 6442450944 | bytes 18350080 | tf_op jit(solution)/shard_map/project/pallas_call | solution.py:487
  174.4 2.3 slice_bitcast_fusion
  176.7 3.2 collective-permute-start.23
  182.3 8.3 %collective-permute-done.23.refs_1_.refs_4_.refs_2_ = bf16[4,384,128]{2,1,0:T(8,128)(2,1)S(1)} collective-permute-done((bf16[4,384,128]{2,1,0:T(8,128)(2,1)S(1)}, bf16[4,384,128]{2,1,0:T(8,128)(2,1)S(1)}, u32[]{:S(2)}, u32[]{:S(2)}) %collective-permute-start.23) | collective-permute-done | bytes 393248 | tf_op jit(solution)/shard_map/ppermute | solution.py:564
  190.6 19.6 %collective-permute-done.24.refs_2_.refs_5_.refs_3_ = bf16[4,384,128]{2,1,0:T(8,128)(2,1)S(1)} collective-permute-done((bf16[4,384,128]{2,1,0:T(8,128)(2,1)S(1)}, bf16[4,384,128]{2,1,0:T(8,128)(2,1)S(1)}, u32[]{:S(2)}, u32[]{:S(2)}) %collective-permute-start.24) | collective-permute-done | bytes 393248 | tf_op jit(solution)/shard_map/ppermute | solution.py:564
  212.6 12.1 %all-to-all-start.2 = ((bf16[16,2,288,128]{3,2,1,0:T(8,128)(2,1)}), bf16[16,2,288,128]{3,2,1,0:T(8,128)(2,1)S(1)}, u32[]{:S(2)}, u32[]{:S(2)}) async-start(bf16[16,2,288,128]{3,2,1,0:T(8,128)(2,1)} %after.17), calls=%async_computation.2 | async-start | bytes 4718592 | tf_op jit(solution)/shard_map/all_to_all | solution.py:653
  227.5 1.9 collective-permute-start.26
  231.0 10.4 %forward.1.forward_ref = f32[16,2,384,128]{3,2,1,0:T(8,128)} custom-call(s32[3]{0:T(128)} %pad_add_fusion.place_ref, f32[768]{0:T(1024)} %constant.251.clone.coarse_ref, bf16[4,384,128]{2,1,0:T(8,128)(2,1)} %get-tuple-element.36.refs_0_, bf16[4,384,128]{2,1,0:T(8,128)(2,1)} %copy-done.8, bf16[4,384,128]{2,1,0:T(8,128)(2,1)} %copy-done.9, ...), custom_call_target="tpu_custom_call" | custom-call | flops 4026531840 | bytes 3279884 | tf_op jit(solution)/shard_map/forward/pallas_call | solution.py:270
  241.4 19.2 %convolve.1.refs_4_.refs_5_ = f32[16,384,128]{2,1,0:T(8,128)} custom-call(s32[3]{0:T(128)} %pad_add_fusion.place_ref, f32[768]{0:T(1024)} %constant.243.clone.coarse_ref, f32[768]{0:T(1024)} %constant.244.clone.coarse_back_ref, bf16[4,384,128]{2,1,0:T(8,128)(2,1)} %get-tuple-element.36.refs_0_, bf16[4,384,128]{2,1,0:T(8,128)(2,1)} %copy-done.8, ...), custom_call_target="tpu_custom_call" | custom-call | flops 8858370048 | bytes 8132620 | tf_op jit(solution)/shard_map/convolve/pallas_call | solution.py:270
  264.2 5.9 %all-to-all-done.2.refs_1_ = bf16[16,2,288,128]{3,2,1,0:T(8,128)(2,1)S(1)} async-done(((bf16[16,2,288,128]{3,2,1,0:T(8,128)(2,1)}), bf16[16,2,288,128]{3,2,1,0:T(8,128)(2,1)S(1)}, u32[]{:S(2)}, u32[]{:S(2)}) %all-to-all-start.2) | async-done | bytes 2359328 | tf_op jit(solution)/shard_map/all_to_all | solution.py:653
  271.5 12.8 %inverse.1 = bf16[16,384,128]{2,1,0:T(8,128)(2,1)} custom-call(f32[768]{0:T(1024)} %constant.254.clone.coarse_back_ref, f32[16,2,384,128]{3,2,1,0:T(8,128)} %forward.1.forward_ref, bf16[16,2,96,128]{3,2,1,0:T(8,128)(2,1)} %gather_fusion, bf16[16,2,288,128]{3,2,1,0:T(8,128)(2,1)} %copy-done.7, bf16[256,512]{1,0:T(8,128)(2,1)} %constant.255.clone.refs_2_, ...), custom_call_target="tpu_custom_call" | custom-call | flops 4831838208 | bytes 14289920 | tf_op jit(solution)/shard_map/inverse/pallas_call | solution.py:270
  284.2 47.8 %all_to_all.20 = bf16[16,384,128]{2,1,0:T(8,128)(2,1)} all-to-all(bf16[16,384,128]{2,1,0:T(8,128)(2,1)} %inverse.1), channel_id=1, replica_groups=mesh['ctx'=16,'ch'=2] {'ctx'}, dimensions={0} | all-to-all | bytes 3145728 | tf_op jit(solution)/shard_map/all_to_all | solution.py:662
  332.0 4.0 %gate_output.1 = bf16[384,2048]{1,0:T(8,128)(2,1)} custom-call(bf16[4,4,384,128]{3,2,1,0:T(8,128)(2,1)} %bitcast.49, bf16[384,2048]{1,0:T(8,128)(2,1)} %gate_ref.1), custom_call_target="tpu_custom_call" | custom-call | flops 786432 | bytes 4718592 | tf_op jit(solution)/shard_map/gate_output/pallas_call | solution.py:403
  (125 shorter events, 57.6 us)
Async XLA Ops:
  2.8 25.5 %all-to-all-start = ((bf16[4,256,512]{2,1,0:T(8,128)(2,1)}), bf16[4,256,512]{2,1,0:T(8,128)(2,1)S(1)}, u32[]{:S(2)}, u32[]{:S(2)}) async-start(bf16[4,256,512]{2,1,0:T(8,128)(2,1)} %bitcast.4), calls=%async_computation | async-start | bytes 2097152 | tf_op jit(solution)/shard_map/all_to_all | solution.py:575
  11.3 9.7 %collective-permute-start = (bf16[4,2,96,128]{3,2,1,0:T(8,128)(2,1)S(1)}, bf16[4,2,96,128]{3,2,1,0:T(8,128)(2,1)S(1)}, u32[]{:S(2)}, u32[]{:S(2)}) collective-permute-start(bf16[4,2,96,128]{3,2,1,0:T(8,128)(2,1)S(1)} %get-tuple-element.49), channel_id=1, source_target_pairs={{0,8},{2,10},{4,12},{6,14},{8,16},{10,18},{12,20},{14,22},{16,24},... | collective-permute-start | bytes 589832 | tf_op jit(solution)/shard_map/ppermute | solution.py:564
  12.9 15.3 %collective-permute-start.1 = (bf16[4,2,96,128]{3,2,1,0:T(8,128)(2,1)S(1)}, bf16[4,2,96,128]{3,2,1,0:T(8,128)(2,1)S(1)}, u32[]{:S(2)}, u32[]{:S(2)}) collective-permute-start(bf16[4,2,96,128]{3,2,1,0:T(8,128)(2,1)S(1)} %get-tuple-element.48), channel_id=1, source_target_pairs={{0,16},{2,18},{4,20},{6,22},{8,24},{10,26},{12,28},{14,30},{16,0},... | collective-permute-start | bytes 589832 | tf_op jit(solution)/shard_map/ppermute | solution.py:564
  15.5 12.8 %collective-permute-start.2 = (bf16[4,2,96,128]{3,2,1,0:T(8,128)(2,1)S(1)}, bf16[4,2,96,128]{3,2,1,0:T(8,128)(2,1)S(1)}, u32[]{:S(2)}, u32[]{:S(2)}) collective-permute-start(bf16[4,2,96,128]{3,2,1,0:T(8,128)(2,1)S(1)} %get-tuple-element.47), channel_id=1, source_target_pairs={{0,24},{2,26},{4,28},{6,30},{8,0},{10,2},{12,4},{14,6},{16,8},{18,... | collective-permute-start | bytes 589832 | tf_op jit(solution)/shard_map/ppermute | solution.py:564
  30.1 28.1 %collective-permute-start.3 = (bf16[4,256,512]{2,1,0:T(8,128)(2,1)}, bf16[4,256,512]{2,1,0:T(8,128)(2,1)S(1)}, u32[]{:S(2)}, u32[]{:S(2)}) collective-permute-start(bf16[4,256,512]{2,1,0:T(8,128)(2,1)} %after.9.refs_0_), channel_id=1, source_target_pairs={{0,8},{2,10},{4,12},{6,14},{8,16},{10,18},{12,20},{14,22},{16,24},... | collective-permute-start | bytes 3145736 | tf_op jit(solution)/shard_map/ppermute | solution.py:616
  36.2 19.2 %collective-permute-start.4 = (bf16[384,1024]{1,0:T(8,128)(2,1)S(1)}, bf16[384,1024]{1,0:T(8,128)(2,1)S(1)}, u32[]{:S(2)}, u32[]{:S(2)}) collective-permute-start(bf16[384,1024]{1,0:T(8,128)(2,1)S(1)} %get-tuple-element.42.refs_4_), channel_id=1, source_target_pairs={{0,2},{2,0},{4,6},{6,4},{8,10},{10,8},{12,14},{14,12},{16,18},{18,... | collective-permute-start | bytes 2359304 | tf_op jit(solution)/shard_map/ppermute | solution.py:558
  37.9 18.9 %collective-permute-start.5 = (bf16[384,1024]{1,0:T(8,128)(2,1)S(1)}, bf16[384,1024]{1,0:T(8,128)(2,1)S(1)}, u32[]{:S(2)}, u32[]{:S(2)}) collective-permute-start(bf16[384,1024]{1,0:T(8,128)(2,1)S(1)} %get-tuple-element.41.refs_5_), channel_id=1, source_target_pairs={{0,4},{2,6},{4,0},{6,2},{8,12},{10,14},{12,8},{14,10},{16,20},{18,... | collective-permute-start | bytes 2359304 | tf_op jit(solution)/shard_map/ppermute | solution.py:558
  59.2 25.8 %collective-permute-start.6 = (bf16[4,256,512]{2,1,0:T(8,128)(2,1)}, bf16[4,256,512]{2,1,0:T(8,128)(2,1)}, u32[]{:S(2)}, u32[]{:S(2)}) collective-permute-start(bf16[4,256,512]{2,1,0:T(8,128)(2,1)} %after.10.refs_5_.refs_1_), channel_id=1, source_target_pairs={{0,8},{2,10},{4,12},{6,14},{8,16},{10,18},{12,20},{14,22},{16,24},... | collective-permute-start | bytes 3145736 | tf_op jit(solution)/shard_map/ppermute | solution.py:616
  63.9 18.7 %collective-permute-start.7 = (bf16[384,1024]{1,0:T(8,128)(2,1)}, bf16[384,1024]{1,0:T(8,128)(2,1)}, u32[]{:S(2)}, u32[]{:S(2)}) collective-permute-start(bf16[384,1024]{1,0:T(8,128)(2,1)} %get-tuple-element.19.refs_6_), channel_id=1, source_target_pairs={{0,4},{2,6},{4,0},{6,2},{8,12},{10,14},{12,8},{14,10},{16,20},{18,... | collective-permute-start | bytes 2359304 | tf_op jit(solution)/shard_map/ppermute | solution.py:558
  65.6 18.4 %collective-permute-start.8 = (bf16[384,1024]{1,0:T(8,128)(2,1)}, bf16[384,1024]{1,0:T(8,128)(2,1)}, u32[]{:S(2)}, u32[]{:S(2)}) collective-permute-start(bf16[384,1024]{1,0:T(8,128)(2,1)} %get-tuple-element.20.refs_9_), channel_id=1, source_target_pairs={{0,2},{2,0},{4,6},{6,4},{8,10},{10,8},{12,14},{14,12},{16,18},{18,... | collective-permute-start | bytes 2359304 | tf_op jit(solution)/shard_map/ppermute | solution.py:558
  85.0 24.7 %collective-permute-start.9 = (bf16[4,256,512]{2,1,0:T(8,128)(2,1)}, bf16[4,256,512]{2,1,0:T(8,128)(2,1)S(1)}, u32[]{:S(2)}, u32[]{:S(2)}) collective-permute-start(bf16[4,256,512]{2,1,0:T(8,128)(2,1)} %after.12.refs_2_), channel_id=1, source_target_pairs={{0,8},{2,10},{4,12},{6,14},{8,16},{10,18},{12,20},{14,22},{16,24},... | collective-permute-start | bytes 3145736 | tf_op jit(solution)/shard_map/ppermute | solution.py:616
  86.1 17.4 %collective-permute-start.10 = (bf16[384,1024]{1,0:T(8,128)(2,1)S(1)}, bf16[384,1024]{1,0:T(8,128)(2,1)S(1)}, u32[]{:S(2)}, u32[]{:S(2)}) collective-permute-start(bf16[384,1024]{1,0:T(8,128)(2,1)S(1)} %copy-done.14), channel_id=1, source_target_pairs={{0,2},{2,0},{4,6},{6,4},{8,10},{10,8},{12,14},{14,12},{16,18},{18,... | collective-permute-start | bytes 2359304 | tf_op jit(solution)/shard_map/ppermute | solution.py:558
  87.7 17.5 %collective-permute-start.11 = (bf16[384,1024]{1,0:T(8,128)(2,1)}, bf16[384,1024]{1,0:T(8,128)(2,1)S(1)}, u32[]{:S(2)}, u32[]{:S(2)}) collective-permute-start(bf16[384,1024]{1,0:T(8,128)(2,1)} %copy-done.15), channel_id=1, source_target_pairs={{0,4},{2,6},{4,0},{6,2},{8,12},{10,14},{12,8},{14,10},{16,20},{18,... | collective-permute-start | bytes 2359304 | tf_op jit(solution)/shard_map/ppermute | solution.py:558
  110.7 100.3 %all-to-all-start.1 = ((bf16[16,2,384,128]{3,2,1,0:T(8,128)(2,1)}), bf16[16,2,384,128]{3,2,1,0:T(8,128)(2,1)S(1)}, u32[]{:S(2)}, u32[]{:S(2)}) async-start(bf16[16,2,384,128]{3,2,1,0:T(8,128)(2,1)} %after.15), calls=%async_computation.1 | async-start | bytes 6291456 | tf_op jit(solution)/shard_map/all_to_all | solution.py:624
  115.0 2.7 collective-permute-start.12
  115.1 3.7 %collective-permute-start.13 = (bf16[384,1024]{1,0:T(8,128)(2,1)}, bf16[384,1024]{1,0:T(8,128)(2,1)}, u32[]{:S(2)}, u32[]{:S(2)}) collective-permute-start(bf16[384,1024]{1,0:T(8,128)(2,1)} %copy-done.13), channel_id=1, source_target_pairs={{0,1},{1,0},{2,3},{3,2},{4,5},{5,4},{6,7},{7,6},{8,9},{9,8},{10,11... | collective-permute-start | bytes 2359304 | tf_op jit(solution)/shard_map/ppermute | solution.py:561
  115.6 4.4 %collective-permute-start.15 = (bf16[384,1024]{1,0:T(8,128)(2,1)}, bf16[384,1024]{1,0:T(8,128)(2,1)}, u32[]{:S(2)}, u32[]{:S(2)}) collective-permute-start(bf16[384,1024]{1,0:T(8,128)(2,1)} %copy-done.11), channel_id=1, source_target_pairs={{0,1},{1,0},{2,3},{3,2},{4,5},{5,4},{6,7},{7,6},{8,9},{9,8},{10,11... | collective-permute-start | bytes 2359304 | tf_op jit(solution)/shard_map/ppermute | solution.py:561
  115.7 5.4 %collective-permute-start.16 = (bf16[384,1024]{1,0:T(8,128)(2,1)}, bf16[384,1024]{1,0:T(8,128)(2,1)}, u32[]{:S(2)}, u32[]{:S(2)}) collective-permute-start(bf16[384,1024]{1,0:T(8,128)(2,1)} %copy-done.12), channel_id=1, source_target_pairs={{0,1},{1,0},{2,3},{3,2},{4,5},{5,4},{6,7},{7,6},{8,9},{9,8},{10,11... | collective-permute-start | bytes 2359304 | tf_op jit(solution)/shard_map/ppermute | solution.py:561
  116.1 6.8 %collective-permute-start.14 = (bf16[384,1024]{1,0:T(8,128)(2,1)}, bf16[384,1024]{1,0:T(8,128)(2,1)}, u32[]{:S(2)}, u32[]{:S(2)}) collective-permute-start(bf16[384,1024]{1,0:T(8,128)(2,1)} %get-tuple-element.19.refs_6_), channel_id=1, source_target_pairs={{0,1},{1,0},{2,3},{3,2},{4,5},{5,4},{6,7},{7,6},{8,9},{9,8},{10,11... | collective-permute-start | bytes 2359304 | tf_op jit(solution)/shard_map/ppermute | solution.py:561
  117.7 6.7 %collective-permute-start.17 = (bf16[384,1024]{1,0:T(8,128)(2,1)}, bf16[384,1024]{1,0:T(8,128)(2,1)}, u32[]{:S(2)}, u32[]{:S(2)}) collective-permute-start(bf16[384,1024]{1,0:T(8,128)(2,1)} %get-tuple-element.20.refs_9_), channel_id=1, source_target_pairs={{0,1},{1,0},{2,3},{3,2},{4,5},{5,4},{6,7},{7,6},{8,9},{9,8},{10,11... | collective-permute-start | bytes 2359304 | tf_op jit(solution)/shard_map/ppermute | solution.py:561
  118.8 7.9 %collective-permute-start.18 = (bf16[384,1024]{1,0:T(8,128)(2,1)}, bf16[384,1024]{1,0:T(8,128)(2,1)}, u32[]{:S(2)}, u32[]{:S(2)}) collective-permute-start(bf16[384,1024]{1,0:T(8,128)(2,1)} %collective-permute-done.7.refs_1_.refs_10_), channel_id=1, source_target_pairs={{0,1},{1,0},{2,3},{3,2},{4,5},{5,4},{6,7},{7,6},{8,9},{9,8},{10,11... | collective-permute-start | bytes 2359304 | tf_op jit(solution)/shard_map/ppermute | solution.py:561
  120.0 6.7 %collective-permute-start.19 = (bf16[384,1024]{1,0:T(8,128)(2,1)}, bf16[384,1024]{1,0:T(8,128)(2,1)}, u32[]{:S(2)}, u32[]{:S(2)}) collective-permute-start(bf16[384,1024]{1,0:T(8,128)(2,1)} %collective-permute-done.8.refs_2_.refs_11_), channel_id=1, source_target_pairs={{0,1},{1,0},{2,3},{3,2},{4,5},{5,4},{6,7},{7,6},{8,9},{9,8},{10,11... | collective-permute-start | bytes 2359304 | tf_op jit(solution)/shard_map/ppermute | solution.py:561
  121.1 12.2 %collective-permute-start.20 = (bf16[384,512]{1,0:T(8,128)(2,1)}, bf16[384,512]{1,0:T(8,128)(2,1)S(1)}, u32[]{:S(2)}, u32[]{:S(2)}) collective-permute-start(bf16[384,512]{1,0:T(8,128)(2,1)} %get-tuple-element.22), channel_id=1, source_target_pairs={{0,2},{2,0},{4,6},{6,4},{8,10},{10,8},{12,14},{14,12},{16,18},{18,... | collective-permute-start | bytes 1179656 | tf_op jit(solution)/shard_map/ppermute | solution.py:558
  123.0 37.2 %collective-permute-start.21 = (bf16[384,512]{1,0:T(8,128)(2,1)}, bf16[384,512]{1,0:T(8,128)(2,1)}, u32[]{:S(2)}, u32[]{:S(2)}) collective-permute-start(bf16[384,512]{1,0:T(8,128)(2,1)} %get-tuple-element.23), channel_id=1, source_target_pairs={{0,4},{2,6},{4,0},{6,2},{8,12},{10,14},{12,8},{14,10},{16,20},{18,... | collective-permute-start | bytes 1179656 | tf_op jit(solution)/shard_map/ppermute | solution.py:558
  124.4 35.7 %collective-permute-start.22 = (bf16[384,512]{1,0:T(8,128)(2,1)}, bf16[384,512]{1,0:T(8,128)(2,1)}, u32[]{:S(2)}, u32[]{:S(2)}) collective-permute-start(bf16[384,512]{1,0:T(8,128)(2,1)} %get-tuple-element.24), channel_id=1, source_target_pairs={{0,6},{2,4},{4,2},{6,0},{8,14},{10,12},{12,10},{14,8},{16,22},{18,... | collective-permute-start | bytes 1179656 | tf_op jit(solution)/shard_map/ppermute | solution.py:558
  176.7 13.9 %collective-permute-start.23 = (bf16[4,384,128]{2,1,0:T(8,128)(2,1)S(1)}, bf16[4,384,128]{2,1,0:T(8,128)(2,1)S(1)}, u32[]{:S(2)}, u32[]{:S(2)}) collective-permute-start(bf16[4,384,128]{2,1,0:T(8,128)(2,1)S(1)} %get-tuple-element.35), channel_id=1, source_target_pairs={{0,8},{2,10},{4,12},{6,14},{8,16},{10,18},{12,20},{14,22},{16,24},... | collective-permute-start | bytes 1179656 | tf_op jit(solution)/shard_map/ppermute | solution.py:564
  179.9 30.3 %collective-permute-start.24 = (bf16[4,384,128]{2,1,0:T(8,128)(2,1)S(1)}, bf16[4,384,128]{2,1,0:T(8,128)(2,1)S(1)}, u32[]{:S(2)}, u32[]{:S(2)}) collective-permute-start(bf16[4,384,128]{2,1,0:T(8,128)(2,1)S(1)} %get-tuple-element.34), channel_id=1, source_target_pairs={{0,16},{2,18},{4,20},{6,22},{8,24},{10,26},{12,28},{14,30},{16,0},... | collective-permute-start | bytes 1179656 | tf_op jit(solution)/shard_map/ppermute | solution.py:564
  180.6 30.3 %collective-permute-start.25 = (bf16[4,384,128]{2,1,0:T(8,128)(2,1)S(1)}, bf16[4,384,128]{2,1,0:T(8,128)(2,1)}, u32[]{:S(2)}, u32[]{:S(2)}) collective-permute-start(bf16[4,384,128]{2,1,0:T(8,128)(2,1)S(1)} %get-tuple-element.33), channel_id=1, source_target_pairs={{0,24},{2,26},{4,28},{6,30},{8,0},{10,2},{12,4},{14,6},{16,8},{18,... | collective-permute-start | bytes 1179656 | tf_op jit(solution)/shard_map/ppermute | solution.py:564
  212.6 57.5 %all-to-all-start.2 = ((bf16[16,2,288,128]{3,2,1,0:T(8,128)(2,1)}), bf16[16,2,288,128]{3,2,1,0:T(8,128)(2,1)S(1)}, u32[]{:S(2)}, u32[]{:S(2)}) async-start(bf16[16,2,288,128]{3,2,1,0:T(8,128)(2,1)} %after.17), calls=%async_computation.2 | async-start | bytes 4718592 | tf_op jit(solution)/shard_map/all_to_all | solution.py:653
  227.5 33.1 %collective-permute-start.26 = (bf16[4,2,96,128]{3,2,1,0:T(8,128)(2,1)}, bf16[4,2,96,128]{3,2,1,0:T(8,128)(2,1)S(1)}, u32[]{:S(2)}, u32[]{:S(2)}) collective-permute-start(bf16[4,2,96,128]{3,2,1,0:T(8,128)(2,1)} %get-tuple-element.26), channel_id=1, source_target_pairs={{0,2},{2,0},{4,6},{6,4},{8,10},{10,8},{12,14},{14,12},{16,18},{18,... | collective-permute-start | bytes 589832 | tf_op jit(solution)/shard_map/ppermute | solution.py:558
  229.4 31.2 %collective-permute-start.27 = (bf16[4,2,96,128]{3,2,1,0:T(8,128)(2,1)}, bf16[4,2,96,128]{3,2,1,0:T(8,128)(2,1)S(1)}, u32[]{:S(2)}, u32[]{:S(2)}) collective-permute-start(bf16[4,2,96,128]{3,2,1,0:T(8,128)(2,1)} %get-tuple-element.27), channel_id=1, source_target_pairs={{0,4},{2,6},{4,0},{6,2},{8,12},{10,14},{12,8},{14,10},{16,20},{18,... | collective-permute-start | bytes 589832 | tf_op jit(solution)/shard_map/ppermute | solution.py:558
  230.8 29.8 %collective-permute-start.28 = (bf16[4,2,96,128]{3,2,1,0:T(8,128)(2,1)}, bf16[4,2,96,128]{3,2,1,0:T(8,128)(2,1)S(1)}, u32[]{:S(2)}, u32[]{:S(2)}) collective-permute-start(bf16[4,2,96,128]{3,2,1,0:T(8,128)(2,1)} %get-tuple-element.28), channel_id=1, source_target_pairs={{0,6},{2,4},{4,2},{6,0},{8,14},{10,12},{12,10},{14,8},{16,22},{18,... | collective-permute-start | bytes 589832 | tf_op jit(solution)/shard_map/ppermute | solution.py:558
  (26 other events, 150.2 us)
